TPU v7x, 32 devices: a whole 2x2x4 slice. The times are simulated.
32 devices in a mesh: grp: 2 (over y), gx: 8 (over z, x), gy: 2 (over core).
Axes of the slice: x: 2, y: 2, z: 4, core: 2. Of those that a mesh axis runs over, the one named last changes fastest.
Arguments:
- source_matrix: float32 [64, 128, 1024], P('grp', 'gx', 'gy'), parts along dimension 0, may hold values from -6 to 6
- source_fracture: float32 [64, 4096], P(('grp', 'gy'), 'gx'), parts along dimension 0, may hold values from -6 to 6
- aperture: float32 [64, 4096], P(('grp', 'gy'), 'gx'), parts along dimension 0, may hold values from 0.5 to 2
- storage: float32 [128, 1024], P('gx', 'gy'), may hold values from 0.1 to 1
- perm_class: int32 [128, 1024], P('gx', 'gy'), may hold values from 0 to 7
- class_perm: float32 [8], replicated, may hold values from 0.1 to 10
- send_slots: int32 [8, 128], P('gx'), may hold values from 0 to 511
- isect_local: int32 [32, 128], P('gx'), may hold values from 0 to 511
- isect_other: int32 [32, 128], P('gx'), may hold values from 0 to 639, as said below
- isect_count: int32 [32], P('gx'), may hold values from 0 to 128, as said below
- ov_cell: int32 [8, 2, 2, 128], P('gx', 'gy'), may hold values from 0 to 8191
- ov_frac: int32 [8, 2, 2, 128], P('gx', 'gy'), may hold values from 0 to 511
- ov_weight: float32 [8, 2, 2, 128], P('gx', 'gy'), may hold values from 0.2 to 2
- ov_count: int32 [8, 2, 2], P('gx', 'gy'), may hold values from 0 to 128, as said below
Outputs:
- pressure_matrix: float32 [64, 128, 1024], P('grp', 'gx', 'gy'), parts along dimension 0
- pressure_fracture: float32 [64, 4096], P(('grp', 'gy'), 'gx'), parts along dimension 0
There are 2 independent parts, one for each index of `grp`. A program takes and returns all parts, laid end to end along the dimension named above; an argument that names none is the same for every part. Nothing has to cross between parts.
Inputs may be any that keep to these rules, and one draw needn't show every extreme that they name: `isect_count`: live rows come first in a partition's intersection blocks and fill the blocks in order; some partition fills all its blocks and some partition has no live rows. `isect_other`: most intersection rows are local; the others name ghost slots of all four neighbour groups. `ov_count`: live rows come first in a device's margin blocks and fill the blocks in order; some device fills all its blocks and some device has no live rows.
All inputs are finite; a program needn't handle non-finite values.
Results may differ from a plain program's by a relative error of at most 0.0003.
Values sent between devices are 32-bit elements; how exact they have to be, the bound alone decides.
No kernel may reach another device: no remote copies, remote signals or barrier semaphores. Data moves between devices by JAX's collectives and lax.ppermute only.
A program may use at most 64 MiB of HBM per device.

v0:
```python
import functools

import jax
import jax.numpy as jnp
from jax import lax
from jax.experimental import pallas as pl
from jax.experimental.pallas import tpu as pltpu
from jax.sharding import PartitionSpec as P

FRACTURE_STORAGE = 0.1
F32 = jnp.float32
BF16 = jnp.bfloat16
LANES = 128
GROUP = 4


def split3(x):
    high = x.astype(BF16)
    rest = x - high.astype(F32)
    mid = rest.astype(BF16)
    low = (rest - mid.astype(F32)).astype(BF16)
    return jnp.concatenate([high, mid, low], axis=0)


def pick(x, table, transposed=False):
    rows = x.shape[0]
    dims = (((1,), (1 if transposed else 0,)), ((), ()))
    out = lax.dot_general(split3(x), table, dims, preferred_element_type=F32)
    return out[:rows] + out[rows : 2 * rows] + out[2 * rows :]


def harmonic(first_perm, second_perm):
    return 2.0 * first_perm * second_perm / (first_perm + second_perm)


def one_hot(index_row, size):
    shape = (size, index_row.shape[1])
    ids = lax.broadcasted_iota(jnp.int32, shape, 0)
    return jnp.where(ids == index_row, 1.0, 0.0).astype(BF16)


def to_blocks(x):
    return jnp.concatenate(
        [x[:, q : q + LANES] for q in range(0, x.shape[1], LANES)], axis=0
    )


def from_blocks(x, rows):
    return jnp.concatenate(
        [x[q : q + rows] for q in range(0, x.shape[0], rows)], axis=1
    )


def by_group(first, second, third, fourth):
    group = first.shape[1] // 4
    lane = lax.broadcasted_iota(jnp.int32, first.shape, 1)
    return jnp.where(
        lane < group,
        first,
        jnp.where(lane < 2 * group, second, jnp.where(lane < 3 * group, third, fourth)),
    )


def total_rows(x):
    return jnp.sum(jnp.transpose(x), axis=0, keepdims=True)


def fold_lanes(x):
    rows, width = x.shape
    out = x[:, :LANES]
    for q in range(LANES, width, LANES):
        out = out + x[:, q : q + LANES]
    return out


def tables_kernel(local_ref, other_ref, frac_ref, first_ref, second_ref, ofrac_ref):
    first_ref[...] = one_hot(local_ref[...], first_ref.shape[0])
    second_ref[...] = one_hot(other_ref[...], second_ref.shape[0])
    ofrac_ref[...] = one_hot(frac_ref[...], ofrac_ref.shape[0])


def opening_kernel(
    place_ref,
    perm_table_ref,
    class_ref,
    col_ref,
    storage_ref,
    source_ref,
    aperture_ref,
    slots_ref,
    cell_ref,
    weight_ref,
    coef_ref,
    oy_ref,
    ox_ref,
    oslot_ref,
    cond_ref,
    up_ref,
    down_ref,
    far_ref,
):
    x_cells, y_cells = class_ref.shape
    members = source_ref.shape[0]
    half = aperture_ref.shape[0]
    high_side = place_ref[2] == 0

    def perm_of(classes):
        perm = jnp.zeros(classes.shape, F32)
        for index in range(perm_table_ref.shape[0]):
            perm = jnp.where(classes == index, perm_table_ref[index], perm)
        return perm

    perm = perm_of(class_ref[...])
    col = perm_of(col_ref[...])
    lane = lax.broadcasted_iota(jnp.int32, perm.shape, 1)
    row = lax.broadcasted_iota(jnp.int32, perm.shape, 0)
    north = jnp.concatenate([perm[:, 1:], col], axis=1)
    south = jnp.concatenate([col, perm[:, :-1]], axis=1)
    tn = jnp.where((lane == y_cells - 1) & jnp.logical_not(high_side), 0.0, harmonic(perm, north))
    ts = jnp.where((lane == 0) & high_side, 0.0, harmonic(perm, south))
    east = jnp.concatenate([perm[1:], perm[:1]], axis=0)
    west = jnp.concatenate([perm[-1:], perm[:-1]], axis=0)
    te = jnp.where(row == x_cells - 1, 0.0, harmonic(perm, east))
    tw = jnp.where(row == 0, 0.0, harmonic(perm, west))

    cell = cell_ref[...]
    oy = one_hot(cell % y_cells, y_cells)
    oy_ref[...] = oy
    shape_x = (x_cells, cell.shape[1])
    at_x = lax.broadcasted_iota(jnp.int32, shape_x, 0) == cell // y_cells
    ox_ref[...] = jnp.where(at_x, 1.0, 0.0)
    wsum = pick(jnp.where(at_x, weight_ref[...], 0.0), oy, True)

    part = storage_ref[...] + te + tw + tn + ts + wsum
    coef_ref[0] = te
    coef_ref[1] = tw
    coef_ref[2] = tn
    coef_ref[3] = ts
    coef_ref[4] = part
    coef_ref[5] = perm

    aperture = aperture_ref[...]
    cond = aperture * aperture * aperture
    cond_ref[...] = cond
    oslot = one_hot(slots_ref[...], cond.shape[1])
    oslot_ref[...] = oslot
    supplied = pick(cond, oslot)
    far_ref[...] = supplied
    blocks = y_cells // LANES
    for ref, at in ((up_ref, x_cells - 1), (down_ref, 0)):
        edge = source_ref[:, at, :]
        ref[0 : blocks * members, :] = to_blocks(edge)
        ref[blocks * members : blocks * members + blocks, :] = to_blocks(perm[at : at + 1])
        ref[blocks * members + blocks : blocks * members + 2 * blocks, :] = to_blocks(part[at : at + 1])
        ref[blocks * members + 2 * blocks : blocks * members + 2 * blocks + half, :] = supplied


def network_out(vf, sr, first, second, oslot):
    cells = first.shape[0]
    supplied = pick(vf, oslot)
    at_first = pick(vf, first)
    sums = pick(sr * at_first, second[cells:], True)
    return supplied, at_first, sums


def margin_values(read, members, oy, ox, scratch_ref):
    x_cells = ox.shape[0]

    @pl.loop(0, members // GROUP)
    def _(index):
        start = index * GROUP
        block = read(start)
        y_cells = block.shape[2]
        found = pick(block.reshape(GROUP * x_cells, y_cells), oy)
        found = found.reshape(GROUP, x_cells, -1) * ox[None]
        for m in range(GROUP):
            scratch_ref[pl.ds(start + m, 1), :] = jnp.sum(found[m], axis=0, keepdims=True)


def edge_column(tile_low, tile_high, high_side, m):
    tile = jnp.where(high_side, tile_high, tile_low)
    return pltpu.roll(tile, jnp.where(high_side, lax.rem(m + 1, LANES), m), 1)


def send_core(y_ref, vf, margin, weight, ofrac, column, j, half, work_ref, wown_ref):
    frac_blocks = vf.shape[1] // LANES
    work_ref[...] = pick(margin * weight, ofrac, True)
    wown_ref[...] = work_ref[pl.ds(pl.multiple_of(j * half, half), half), :]
    other = work_ref[pl.ds(pl.multiple_of((1 - j) * half, half), half), :]
    size = frac_blocks * half
    y_ref[0:size, :] = to_blocks(vf)
    y_ref[size : 2 * size, :] = to_blocks(other)
    y_ref[2 * size : 2 * size + column.shape[0], :] = column


def first_kernel(
    place_ref,
    count_ref,
    coef_ref,
    cond_ref,
    source_ref,
    source_f_ref,
    weight_ref,
    near_a_ref,
    near_b_ref,
    far_c_ref,
    far_d_ref,
    first_ref,
    second_ref,
    ofrac_ref,
    oslot_ref,
    oy_ref,
    ox_ref,
    unit_ref,
    v_ref,
    vf_ref,
    halo_ref,
    sr_ref,
    scale_f_ref,
    at_first_ref,
    wown_ref,
    sent_ref,
    core_ref,
    dots_ref,
    margin_ref,
    work_ref,
    acc_ref,
    column_ref,
):
    members, x_cells, y_cells = source_ref.shape
    half, frac_cells = source_f_ref.shape
    blocks = y_cells // LANES
    even = place_ref[0] == 0
    low_pair = place_ref[1] == 0
    j = place_ref[2]
    high_side = j == 0
    base = blocks * members

    def plus1(at, size):
        return jnp.where(even, near_a_ref[at : at + size, :], near_b_ref[at : at + size, :])

    def minus1(at, size):
        return jnp.where(even, near_b_ref[at : at + size, :], near_a_ref[at : at + size, :])

    te, tw = coef_ref[0], coef_ref[1]
    part, perm = coef_ref[4], coef_ref[5]
    row = lax.broadcasted_iota(jnp.int32, perm.shape, 0)
    perm_plus = from_blocks(plus1(base, blocks), 1)
    perm_minus = from_blocks(minus1(base, blocks), 1)
    part_plus = from_blocks(plus1(base + blocks, blocks), 1)
    part_minus = from_blocks(minus1(base + blocks, blocks), 1)
    te_edge = jnp.where(place_ref[4] == 1, 0.0, harmonic(perm[x_cells - 1 :], perm_plus))
    tw_edge = jnp.where(place_ref[3] == 1, 0.0, harmonic(perm[:1], perm_minus))
    te = jnp.where(row == x_cells - 1, te_edge, te)
    tw = jnp.where(row == 0, tw_edge, tw)
    diag = (
        part
        + jnp.where(row == x_cells - 1, te_edge, 0.0)
        + jnp.where(row == 0, tw_edge, 0.0)
    )
    inverse = 1.0 / diag
    unit_ref[0] = te * inverse
    unit_ref[1] = tw * inverse
    unit_ref[2] = coef_ref[2] * inverse
    unit_ref[3] = coef_ref[3] * inverse
    unit_ref[4] = inverse
    unit_ref[5] = diag
    halo_ref[0] = from_blocks(plus1(0, base), members) / (part_plus + te_edge)
    halo_ref[1] = from_blocks(minus1(0, base), members) / (part_minus + tw_edge)

    slot_at = base + 2 * blocks
    far_plus = jnp.where(low_pair, far_c_ref[...], far_d_ref[...])
    far_minus = jnp.where(low_pair, far_d_ref[...], far_c_ref[...])
    ghosts = by_group(minus1(slot_at, half), plus1(slot_at, half), far_minus, far_plus)
    first, second, oslot = first_ref[...], second_ref[...], oslot_ref[...]
    cond = cond_ref[...]
    cond_first = pick(cond, first)
    cond_second = pick(cond, second[:frac_cells]) + pick(ghosts, second[frac_cells:])
    lane = lax.broadcasted_iota(jnp.int32, cond_first.shape, 1)
    live = jnp.zeros(cond_first.shape, jnp.bool_)
    for block in range(cond_first.shape[1] // LANES):
        start = block * LANES
        live = live | ((lane >= start) & (lane < start + count_ref[block]))
    sr = jnp.where(live, harmonic(cond_first, cond_second), 0.0)
    sr_ref[...] = sr
    diag_f = FRACTURE_STORAGE + pick(sr, first, True)
    inverse_f = 1.0 / diag_f
    scale_f_ref[0] = inverse_f
    scale_f_ref[1] = diag_f
    source_f = source_f_ref[...]
    vf = source_f * inverse_f
    vf_ref[...] = vf
    supplied, at_first, sums = network_out(vf, sr, first, second, oslot)
    at_first_ref[...] = at_first
    sent_ref[0:half, :] = supplied
    sent_ref[half : 2 * half, :] = sums
    sent_ref[2 * half : 3 * half, :] = pick(sr, second[frac_cells:], True)

    acc_ref[...] = jnp.zeros_like(acc_ref)
    acc_ref[pl.ds(pl.multiple_of(j * half, half), half), :] = fold_lanes(source_f * vf)
    lane_c = lax.broadcasted_iota(jnp.int32, (x_cells, LANES), 1)
    column_ref[...] = jnp.zeros_like(column_ref)

    @pl.loop(0, members)
    def _(m):
        value = source_ref[m]
        scaled = value * unit_ref[4]
        v_ref[m] = scaled
        acc_ref[pl.ds(m, 1), :] += jnp.sum(fold_lanes(value * scaled), axis=0, keepdims=True)
        moved = edge_column(scaled[:, :LANES], scaled[:, y_cells - LANES :], high_side, m)
        column_ref[...] = jnp.where(lane_c == m, moved, column_ref[...])

    margin_values(lambda s: v_ref[pl.ds(s, GROUP)], members, oy_ref[...], ox_ref[...], margin_ref)
    weight = weight_ref[...]
    send_core(core_ref, vf, margin_ref[...], weight, ofrac_ref[...], column_ref[...], j, half, work_ref, wown_ref)
    wsum = pick(jnp.broadcast_to(weight, (8, weight.shape[1])), ofrac_ref[...], True)
    tail = core_ref.shape[0] - 8 * (frac_cells // LANES)
    core_ref[tail:, :] = to_blocks(wsum)
    dots_ref[...] = jnp.broadcast_to(total_rows(acc_ref[...]), dots_ref.shape)


def step_kernel(
    kind,
    place_ref,
    v_ref,
    vf_ref,
    halo_in_ref,
    near_a_ref,
    near_b_ref,
    far_c_ref,
    far_d_ref,
    core_in_ref,
    at_first_in_ref,
    wown_in_ref,
    sr_ref,
    scale_f_ref,
    own_f_in_ref,
    unit_ref,
    weight_ref,
    first_ref,
    second_ref,
    ofrac_ref,
    oslot_ref,
    oy_ref,
    ox_ref,
    *refs,
):
    if kind == "last":
        dots_ref, flow_ref, work_ref, acc_ref, acc2_ref = refs
    else:
        (
            out_ref,
            out_f_ref,
            own_f_ref,
            at_first_ref,
            wown_ref,
            up_ref,
            down_ref,
            sent_ref,
            core_ref,
            dots_ref,
            flow_ref,
            work_ref,
            acc_ref,
            acc2_ref,
            margin_ref,
            column_ref,
        ) = refs
    members, x_cells, y_cells = v_ref.shape
    half, frac_cells = vf_ref.shape
    blocks = y_cells // LANES
    frac_blocks = frac_cells // LANES
    even = place_ref[0] == 0
    low_pair = place_ref[1] == 0
    j = place_ref[2]
    high_side = j == 0
    base = 0 if kind == "first" else blocks * members

    def plus1(at, size):
        return jnp.where(even, near_a_ref[at : at + size, :], near_b_ref[at : at + size, :])

    def minus1(at, size):
        return jnp.where(even, near_b_ref[at : at + size, :], near_a_ref[at : at + size, :])

    def plus2(at, size):
        return jnp.where(low_pair, far_c_ref[at : at + size, :], far_d_ref[at : at + size, :])

    def minus2(at, size):
        return jnp.where(low_pair, far_d_ref[at : at + size, :], far_c_ref[at : at + size, :])

    first, second, oslot = first_ref[...], second_ref[...], oslot_ref[...]
    vf = vf_ref[...]
    ghosts = by_group(minus1(base, half), plus1(base, half), minus2(0, half), plus2(0, half))
    sums = by_group(
        plus1(base + half, half), minus1(base + half, half), plus2(half, half), minus2(half, half)
    )
    size = frac_blocks * half
    theirs = from_blocks(core_in_ref[0:size, :], half)
    their_sums = from_blocks(core_in_ref[size : 2 * size, :], half)
    column_in = core_in_ref[2 * size : 2 * size + x_cells, :]
    if kind == "first":
        at = 2 * half
        back = by_group(
            plus1(base + at, half), minus1(base + at, half), plus2(at, half), minus2(at, half)
        )
        wsum = pick(jnp.broadcast_to(weight_ref[...], (8, weight_ref.shape[1])), ofrac_ref[...], True)
        tail = core_in_ref.shape[0] - 8 * frac_blocks
        wsum = wsum + from_blocks(core_in_ref[tail:, :], 8)
        own_f = FRACTURE_STORAGE + wsum[:1] + pick(back, oslot, True)
        own_f_ref[...] = own_f
    else:
        own_f = own_f_in_ref[...]
        if kind == "middle":
            own_f_ref[...] = own_f
    sr = sr_ref[...]
    at_second = pick(vf, second[:frac_cells]) + pick(ghosts, second[frac_cells:])
    flux = sr * (at_first_in_ref[...] - at_second)
    image_f = own_f * vf + pick(flux, first, True) - pick(flux, second[:frac_cells], True)
    image_f = image_f - pick(sums, oslot, True) - wown_in_ref[...] - their_sums
    next_f = image_f * scale_f_ref[0]

    own_rows = pl.ds(pl.multiple_of(j * half, half), half)
    work_ref[own_rows, :] = vf
    work_ref[pl.ds(pl.multiple_of((1 - j) * half, half), half), :] = theirs
    weight = weight_ref[...]
    flow_ref[...] = pick(work_ref[...], ofrac_ref[...]) * weight

    acc_ref[...] = jnp.zeros_like(acc_ref)
    acc2_ref[...] = jnp.zeros_like(acc2_ref)
    acc_ref[own_rows, :] = fold_lanes(vf * image_f)
    if kind != "last":
        acc2_ref[own_rows, :] = fold_lanes(next_f * image_f)
        column_ref[...] = jnp.zeros_like(column_ref)
        out_f_ref[...] = next_f
    lane_c = lax.broadcasted_iota(jnp.int32, (x_cells, LANES), 1)
    lane = lax.broadcasted_iota(jnp.int32, (x_cells, y_cells), 1)
    row = lax.broadcasted_iota(jnp.int32, (x_cells, y_cells), 0)
    oy, ox = oy_ref[...], ox_ref[...]

    def halo(m, side):
        if kind == "first":
            return halo_in_ref[side, pl.ds(m, 1), :]
        pieces = []
        for q in range(blocks):
            a = near_a_ref[pl.ds(q * members + m, 1), :]
            b = near_b_ref[pl.ds(q * members + m, 1), :]
            pieces.append(jnp.where(even, a, b) if side == 0 else jnp.where(even, b, a))
        return jnp.concatenate(pieces, axis=1)

    @pl.loop(0, members // GROUP)
    def _(index):
        start = index * GROUP
        parts = []
        for k in range(GROUP):
            parts.append(ox * flow_ref[pl.ds(start + k, 1), :])
        coupled = pick(jnp.concatenate(parts, axis=0), oy, True)
        for k in range(GROUP):
            m = start + k
            value = v_ref[m]
            east = jnp.where(row == x_cells - 1, halo(m, 0), pltpu.roll(value, x_cells - 1, 0))
            west = jnp.where(row == 0, halo(m, 1), pltpu.roll(value, 1, 0))
            moved = pltpu.roll(column_in, jnp.where(high_side, LANES - 1 - m, lax.rem(LANES - m, LANES)), 1)
            moved = jnp.concatenate([moved] * blocks, axis=1)
            north = jnp.where(lane == y_cells - 1, moved, pltpu.roll(value, y_cells - 1, 1))
            south = jnp.where(lane == 0, moved, pltpu.roll(value, 1, 1))
            image = value - unit_ref[0] * east - unit_ref[1] * west
            image = image - unit_ref[2] * north - unit_ref[3] * south
            image = image - coupled[k * x_cells : (k + 1) * x_cells] * unit_ref[4]
            heavy = image * unit_ref[5]
            acc_ref[pl.ds(m, 1), :] += jnp.sum(fold_lanes(value * heavy), axis=0, keepdims=True)
            if kind != "last":
                acc2_ref[pl.ds(m, 1), :] += jnp.sum(fold_lanes(image * heavy), axis=0, keepdims=True)
                out_ref[m] = image
                shifted = edge_column(image[:, :LANES], image[:, y_cells - LANES :], high_side, m)
                column_ref[...] = jnp.where(lane_c == m, shifted, column_ref[...])
                for q in range(blocks):
                    cut = image[:, q * LANES : (q + 1) * LANES]
                    up_ref[pl.ds(q * members + m, 1), :] = cut[x_cells - 1 :]
                    down_ref[pl.ds(q * members + m, 1), :] = cut[:1]

    dots = [total_rows(acc_ref[...])]
    if kind != "last":
        dots.append(total_rows(acc2_ref[...]))
        supplied, at_first, sums = network_out(next_f, sr, first, second, oslot)
        at_first_ref[...] = at_first
        at = blocks * members
        for ref, where in ((up_ref, at), (down_ref, at), (sent_ref, 0)):
            ref[where : where + half, :] = supplied
            ref[where + half : where + 2 * half, :] = sums
        margin_values(lambda s: out_ref[pl.ds(s, GROUP)], members, oy, ox, margin_ref)
        send_core(
            core_ref, next_f, margin_ref[...], weight, ofrac_ref[...], column_ref[...], j, half, work_ref, wown_ref
        )
    dots.append(jnp.zeros((8 - len(dots), members), F32))
    dots_ref[...] = jnp.concatenate(dots, axis=0)


def close_kernel(place_ref, totals_ref, v0_ref, v1_ref, v2_ref, f0_ref, f1_ref, f2_ref, x_ref, xf_ref, c_ref):
    members, x_cells, y_cells = v0_ref.shape
    half, frac_cells = f0_ref.shape

    total = jnp.sum(totals_ref[...], axis=0)
    m0, m1, m2, m3, m4, m5 = (total[k : k + 1] for k in range(6))
    alpha0 = m0 / m1
    rz1 = m0 - 2.0 * alpha0 * m1 + alpha0 * alpha0 * m2
    beta1 = rz1 / m0
    a, b = 1.0 + beta1, -alpha0
    pap1 = a * a * m1 + 2.0 * a * b * m2 + b * b * m3
    alpha1 = rz1 / pap1
    e = -alpha0 - alpha1 * a
    g = -alpha1 * b
    rz2 = m0 + 2.0 * e * m1 + (e * e + 2.0 * g) * m2 + 2.0 * e * g * m3 + g * g * m4
    beta2 = rz2 / rz1
    c = 1.0 + beta2 * a
    d = e + beta2 * b
    pap2 = c * c * m1 + 2.0 * c * d * m2 + (d * d + 2.0 * c * g) * m3 + 2.0 * d * g * m4 + g * g * m5
    alpha2 = rz2 / pap2
    c0 = alpha0 + alpha1 * a + alpha2 * c
    c1 = alpha1 * b + alpha2 * d
    c2 = alpha2 * g
    for k, row in enumerate((c0, c1, c2)):
        c_ref[k] = jnp.transpose(jnp.broadcast_to(row, (LANES, LANES)))
    j = place_ref[2]
    own = pl.ds(pl.multiple_of(j * half, half), half)

    def wide(k, rows, width):
        return jnp.concatenate([c_ref[k, rows, :]] * (width // LANES), axis=1)

    xf_ref[...] = (
        wide(0, own, frac_cells) * f0_ref[...]
        + wide(1, own, frac_cells) * f1_ref[...]
        + wide(2, own, frac_cells) * f2_ref[...]
    )

    @pl.loop(0, members)
    def _(m):
        rows = pl.ds(m, 1)
        x_ref[m] = (
            wide(0, rows, y_cells) * v0_ref[m]
            + wide(1, rows, y_cells) * v1_ref[m]
            + wide(2, rows, y_cells) * v2_ref[m]
        )


def pairs_of(count, stride, phase):
    out = []
    for index in range(count):
        if (index // stride) % 2 == phase:
            mate = (index + stride) % count
            out += [(index, mate), (mate, index)]
    return out


VMEM = pl.BlockSpec(memory_space=pltpu.VMEM)
SMEM = pl.BlockSpec(memory_space=pltpu.SMEM)


def call(kernel, name, args, outs, scratch=(), scalars=0, cost=None):
    return pl.pallas_call(
        kernel,
        name=name,
        out_shape=[jax.ShapeDtypeStruct(shape, dtype) for shape, dtype in outs],
        in_specs=[SMEM] * scalars + [VMEM] * (len(args) - scalars),
        out_specs=[VMEM] * len(outs),
        scratch_shapes=list(scratch),
        compiler_params=pltpu.CompilerParams(vmem_limit_bytes=40 * 1024 * 1024),
        cost_estimate=cost,
    )(*args)


def per_device(
    source_matrix,
    source_fracture,
    aperture,
    storage,
    perm_class,
    class_perm,
    send_slots,
    isect_local,
    isect_other,
    isect_count,
    ov_cell,
    ov_frac,
    ov_weight,
    ov_count,
):
    members, x_cells, y_cells = source_matrix.shape
    half, frac_cells = source_fracture.shape
    slots = send_slots.shape[1]
    rows = isect_local.size
    margin = ov_cell.size
    count = lax.axis_size("gx")
    i, j = lax.axis_index("gx"), lax.axis_index("gy")
    place = jnp.stack(
        [i % 2, (i // 2) % 2, j, (i == 0).astype(jnp.int32), (i == count - 1).astype(jnp.int32)]
    ).astype(jnp.int32)

    def near(up, down):
        even = i % 2 == 0
        to_a = jnp.where(even, up, down)
        to_b = jnp.where(even, down, up)
        return (
            lax.ppermute(to_a, "gx", pairs_of(count, 1, 0)),
            lax.ppermute(to_b, "gx", pairs_of(count, 1, 1)),
        )

    def far(value):
        return (
            lax.ppermute(value, "gx", pairs_of(count, 2, 0)),
            lax.ppermute(value, "gx", pairs_of(count, 2, 1)),
        )

    def core(value):
        return lax.ppermute(value, "gy", [(0, 1), (1, 0)])

    blocks = y_cells // LANES
    frac_blocks = frac_cells // LANES
    positions = jnp.arange(LANES, dtype=jnp.int32)
    ov_live = positions[None, :] < ov_count.reshape(-1, 1)
    weight = jnp.where(ov_live, ov_weight.reshape(ov_live.shape), 0.0).reshape(1, margin)
    col = core(jnp.where(j == 0, perm_class[:, y_cells - 1 :], perm_class[:, :1]))
    near_rows = blocks * members + 2 * blocks + half
    coef, oy, ox, oslot, cond, up, down, supplied = call(
        opening_kernel,
        "opening",
        (
            place,
            class_perm,
            perm_class,
            col,
            storage,
            source_matrix,
            aperture,
            send_slots,
            ov_cell.reshape(1, margin),
            weight,
        ),
        [
            ((6, x_cells, y_cells), F32),
            ((y_cells, margin), BF16),
            ((x_cells, margin), F32),
            ((frac_cells, slots), BF16),
            ((half, frac_cells), F32),
            ((near_rows, LANES), F32),
            ((near_rows, LANES), F32),
            ((half, slots), F32),
        ],
        scalars=2,
    )
    near_a, near_b = near(up, down)
    far_c, far_d = far(supplied)
    first, second, ofrac = call(
        tables_kernel,
        "tables",
        (isect_local.reshape(1, rows), isect_other.reshape(1, rows), ov_frac.reshape(1, margin)),
        [((frac_cells, rows), BF16), ((frac_cells + slots, rows), BF16), ((frac_cells, margin), BF16)],
    )
    core_rows = 2 * frac_blocks * half + x_cells
    (unit, v0, f0, halo, sr, scale_f, at_first, wown, sent, core_msg, dots0) = call(
        first_kernel,
        "first_vector",
        (
            place,
            isect_count,
            coef,
            cond,
            source_matrix,
            source_fracture,
            weight,
            near_a,
            near_b,
            far_c,
            far_d,
            first,
            second,
            ofrac,
            oslot,
            oy,
            ox,
        ),
        [
            ((6, x_cells, y_cells), F32),
            ((members, x_cells, y_cells), F32),
            ((half, frac_cells), F32),
            ((2, members, y_cells), F32),
            ((half, rows), F32),
            ((2, half, frac_cells), F32),
            ((half, rows), F32),
            ((half, frac_cells), F32),
            ((3 * half, LANES), F32),
            ((core_rows + 8 * frac_blocks, LANES), F32),
            ((8, members), F32),
        ],
        scratch=[
            pltpu.VMEM((members, margin), F32),
            pltpu.VMEM((members, frac_cells), F32),
            pltpu.VMEM((members, LANES), F32),
            pltpu.VMEM((x_cells, LANES), F32),
        ],
        scalars=2,
    )
    step_scratch = [
        pltpu.VMEM((members, margin), F32),
        pltpu.VMEM((members, frac_cells), F32),
        pltpu.VMEM((members, LANES), F32),
        pltpu.VMEM((members, LANES), F32),
    ]
    more_scratch = [pltpu.VMEM((members, margin), F32), pltpu.VMEM((x_cells, LANES), F32)]
    near_rows = blocks * members + 2 * half
    step_outs = [
        ((members, x_cells, y_cells), F32),
        ((half, frac_cells), F32),
        ((half, frac_cells), F32),
        ((half, rows), F32),
        ((half, frac_cells), F32),
        ((near_rows, LANES), F32),
        ((near_rows, LANES), F32),
        ((2 * half, LANES), F32),
        ((core_rows, LANES), F32),
        ((8, members), F32),
    ]
    fixed = (unit, weight, first, second, ofrac, oslot, oy, ox)

    near_a, near_b = near(sent, sent)
    far_c, far_d = far(sent)
    core_in = core(core_msg)
    v1, f1, own_f, at_first, wown, up, down, sent, core_msg, dots1 = call(
        functools.partial(step_kernel, "first"),
        "power_1",
        (place, v0, f0, halo, near_a, near_b, far_c, far_d, core_in, at_first, wown, sr, scale_f, scale_f) + fixed,
        step_outs,
        scratch=step_scratch + more_scratch,
        scalars=1,
    )
    near_a, near_b = near(up, down)
    far_c, far_d = far(sent)
    core_in = core(core_msg)
    v2, f2, own_f, at_first, wown, up, down, sent, core_msg, dots2 = call(
        functools.partial(step_kernel, "middle"),
        "power_2",
        (place, v1, f1, halo, near_a, near_b, far_c, far_d, core_in, at_first, wown, sr, scale_f, own_f) + fixed,
        step_outs,
        scratch=step_scratch + more_scratch,
        scalars=1,
    )
    near_a, near_b = near(up, down)
    far_c, far_d = far(sent)
    core_in = core(core_msg)
    (dots3,) = call(
        functools.partial(step_kernel, "last"),
        "power_3",
        (place, v2, f2, halo, near_a, near_b, far_c, far_d, core_in, at_first, wown, sr, scale_f, own_f) + fixed,
        [((8, members), F32)],
        scratch=step_scratch,
        scalars=1,
    )
    moments = jnp.concatenate([dots0[:1], dots1[:2], dots2[:2], dots3[:1], dots3[2:4]], axis=0)
    moments = jnp.pad(moments, ((0, 0), (0, LANES - members)))
    peers = count * lax.axis_size("gy")
    totals = lax.all_to_all(jnp.broadcast_to(moments[None], (peers, 8, LANES)), ("gx", "gy"), 0, 0)
    return call(
        close_kernel,
        "iterate",
        (place, totals, v0, v1, v2, f0, f1, f2),
        [((members, x_cells, y_cells), F32), ((half, frac_cells), F32)],
        scratch=[pltpu.VMEM((3, LANES, LANES), F32)],
        scalars=1,
    )


def solution(mesh):
    placed = (
        P("grp", "gx", "gy"),
        P(("grp", "gy"), "gx"),
        P(("grp", "gy"), "gx"),
        P("gx", "gy"),
        P("gx", "gy"),
        P(),
        P("gx", None),
        P("gx", None),
        P("gx", None),
        P("gx"),
        P("gx", "gy", None, None),
        P("gx", "gy", None, None),
        P("gx", "gy", None, None),
        P("gx", "gy", None),
    )
    return jax.shard_map(
        per_device,
        mesh=mesh,
        in_specs=placed,
        out_specs=(P("grp", "gx", "gy"), P(("grp", "gy"), "gx")),
        check_vma=False,
    )
```

profile of v0, /device:TPU:0, one launch (start us, length us, event | category | flops | bytes accessed | tf_op | source)
XLA Modules:
  0.0 80.5 jit_solution(17588723891558453029)
XLA Ops:
  0.6 0.0 copy-start.5
  0.6 0.8 slice_select_fusion
  1.4 0.5 collective-permute-start
  1.9 0.0 copy-start.2
  1.9 0.0 copy-start.4
  2.0 0.6 copy-done.14
  2.6 0.1 compare_bitcast_fusion
  2.6 0.1 stack.31.place_ref
  2.7 0.0 collective-permute-done.col_ref
  2.7 0.0 copy-done.8
  2.8 0.6 copy-done.10
  3.4 1.2 %copy-done = f32[32,16,512]{2,1,0:T(8,128)S(1)} copy-done((f32[32,16,512]{2,1,0:T(8,128)S(1)}, f32[32,16,512]{2,1,0:T(8,128)}, u32[]{:S(2)}) %copy-start) | copy-done | bytes 1048600
  4.6 0.8 %opening.1 = (f32[6,16,512]{2,1,0:T(8,128)S(1)}, bf16[512,256]{1,0:T(8,128)(2,1)S(1)}, f32[16,256]{1,0:T(8,128)S(1)}, bf16[512,128]{1,0:T(8,128)(2,1)S(1)}, f32[...) custom-call(s32[5]{0:T(128)S(1)} %stack.31.place_ref, ...), custom_call_target="tpu_custom_call" | custom-call | tf_op jit(solution)/shard_map/opening/pallas_call | solution.py:559
  5.5 0.0 copy-start.3
  5.5 5.6 %collective-permute-start.2 = (f32[152,128]{1,0:T(8,128)S(1)}, f32[152,128]{1,0:T(8,128)S(1)}, u32[]{:S(2)}, u32[]{:S(2)}) collective-permute-start(f32[152,128]{1,0:T(8,128)S(1)} %get-tuple-element.90), channel_id=1, source_target_pairs={{2,4},{4,2},{6,8},{8,6},{10,12},{12,10},{14,0},{0,14},{3,5},{5,3},... | collective-permute-start | bytes 233480 | tf_op jit(solution)/shard_map/ppermute | solution.py:604
  11.1 0.0 collective-permute-start.1
  11.1 0.6 collective-permute-start.4
  11.7 1.0 %collective-permute-start.3 = (f32[16,128]{1,0:T(8,128)S(1)}, f32[16,128]{1,0:T(8,128)S(1)}, u32[]{:S(2)}, u32[]{:S(2)}) collective-permute-start(f32[16,128]{1,0:T(8,128)S(1)} %get-tuple-element.48), channel_id=1, source_target_pairs={{0,4},{4,0},{2,6},{6,2},{8,12},{12,8},{10,14},{14,10},{1,5},{5,1},... | collective-permute-start | bytes 24584 | tf_op jit(solution)/shard_map/ppermute | solution.py:609
  12.8 0.7 copy-done.7
  13.4 0.0 copy-done.6
  13.5 0.0 copy-done.9
  13.5 0.3 tables.1
  13.7 2.8 %collective-permute-done.4.far_d_ref = f32[16,128]{1,0:T(8,128)S(1)} collective-permute-done((f32[16,128]{1,0:T(8,128)S(1)}, f32[16,128]{1,0:T(8,128)S(1)}, u32[]{:S(2)}, u32[]{:S(2)}) %collective-permute-start.4) | collective-permute-done | bytes 8224 | tf_op jit(solution)/shard_map/ppermute | solution.py:610
  16.5 0.0 collective-permute-done.3.far_c_ref
  16.5 0.0 collective-permute-done.2.near_b_ref
  16.6 0.0 collective-permute-done.1.near_a_ref
  16.6 0.0 copy-start.12
  16.6 0.6 copy-done.12
  17.2 6.2 %first_vector.1 = (f32[6,16,512]{2,1,0:T(8,128)S(1)}, f32[32,16,512]{2,1,0:T(8,128)S(1)}, f32[16,512]{1,0:T(8,128)S(1)}, f32[2,32,512]{2,1,0:T(8,128)S(1)}, f32[...) custom-call(s32[5]{0:T(128)S(1)} %stack.31.place_ref, ...), custom_call_target="tpu_custom_call" | custom-call | tf_op jit(solution)/shard_map/first_vector/pallas_call | solution.py:559
  23.4 0.0 collective-permute-start.9
  23.5 2.1 %collective-permute-start.8 = (f32[48,128]{1,0:T(8,128)S(1)}, f32[48,128]{1,0:T(8,128)S(1)}, u32[]{:S(2)}, u32[]{:S(2)}) collective-permute-start(f32[48,128]{1,0:T(8,128)S(1)} %get-tuple-element.59), channel_id=1, source_target_pairs={{4,8},{8,4},{6,10},{10,6},{12,0},{0,12},{14,2},{2,14},{5,9},{9,5},... | collective-permute-start | bytes 73736 | tf_op jit(solution)/shard_map/ppermute | solution.py:610
  25.5 0.0 collective-permute-start.7
  25.5 3.3 %collective-permute-start.6 = (f32[48,128]{1,0:T(8,128)S(1)}, f32[48,128]{1,0:T(8,128)S(1)}, u32[]{:S(2)}, u32[]{:S(2)}) collective-permute-start(f32[48,128]{1,0:T(8,128)S(1)} %get-tuple-element.59), channel_id=1, source_target_pairs={{2,4},{4,2},{6,8},{8,6},{10,12},{12,10},{14,0},{0,14},{3,5},{5,3},... | collective-permute-start | bytes 73736 | tf_op jit(solution)/shard_map/ppermute | solution.py:604
  28.8 0.2 collective-permute-start.5
  29.0 0.1 collective-permute-done.8.far_d_ref
  29.1 0.3 collective-permute-done.7.far_c_ref
  29.4 2.7 %collective-permute-done.6.near_b_ref = f32[48,128]{1,0:T(8,128)S(1)} collective-permute-done((f32[48,128]{1,0:T(8,128)S(1)}, f32[48,128]{1,0:T(8,128)S(1)}, u32[]{:S(2)}, u32[]{:S(2)}) %collective-permute-start.6) | collective-permute-done | bytes 24608 | tf_op jit(solution)/shard_map/ppermute | solution.py:604
  32.1 0.6 collective-permute-done.5.near_a_ref
  32.6 0.0 collective-permute-done.9.core_in_ref
  32.6 6.5 %power_1.1 = (f32[32,16,512]{2,1,0:T(8,128)S(1)}, f32[16,512]{1,0:T(8,128)S(1)}, f32[16,512]{1,0:T(8,128)S(1)}, f32[16,512]{1,0:T(8,128)S(1)}, f32[16,512]{1,0:T...) custom-call(s32[5]{0:T(128)S(1)} %stack.31.place_ref, ...), custom_call_target="tpu_custom_call" | custom-call | tf_op jit(solution)/shard_map/power_1/pallas_call | solution.py:559
  39.2 2.8 %collective-permute-start.11 = (f32[160,128]{1,0:T(8,128)S(1)}, f32[160,128]{1,0:T(8,128)S(1)}, u32[]{:S(2)}, u32[]{:S(2)}) collective-permute-start(f32[160,128]{1,0:T(8,128)S(1)} %get-tuple-element.88), channel_id=1, source_target_pairs={{2,4},{4,2},{6,8},{8,6},{10,12},{12,10},{14,0},{0,14},{3,5},{5,3},... | collective-permute-start | bytes 245768 | tf_op jit(solution)/shard_map/ppermute | solution.py:604
  42.0 0.0 collective-permute-start.10
  42.0 0.0 collective-permute-start.14
  42.0 2.6 %collective-permute-start.13 = (f32[32,128]{1,0:T(8,128)S(1)}, f32[32,128]{1,0:T(8,128)S(1)}, u32[]{:S(2)}, u32[]{:S(2)}) collective-permute-start(f32[32,128]{1,0:T(8,128)S(1)} %get-tuple-element.71), channel_id=1, source_target_pairs={{4,8},{8,4},{6,10},{10,6},{12,0},{0,12},{14,2},{2,14},{5,9},{9,5},... | collective-permute-start | bytes 49160 | tf_op jit(solution)/shard_map/ppermute | solution.py:610
  44.6 0.0 collective-permute-start.12
  44.6 3.0 %collective-permute-done.13.far_d_ref = f32[32,128]{1,0:T(8,128)S(1)} collective-permute-done((f32[32,128]{1,0:T(8,128)S(1)}, f32[32,128]{1,0:T(8,128)S(1)}, u32[]{:S(2)}, u32[]{:S(2)}) %collective-permute-start.13) | collective-permute-done | bytes 16416 | tf_op jit(solution)/shard_map/ppermute | solution.py:610
  47.5 0.8 collective-permute-done.12.far_c_ref
  48.3 0.0 collective-permute-done.14.core_in_ref
  48.3 0.0 collective-permute-done.11.near_b_ref
  48.3 0.0 collective-permute-done.10.near_a_ref
  48.3 6.5 %power_2.1 = (f32[32,16,512]{2,1,0:T(8,128)S(1)}, f32[16,512]{1,0:T(8,128)S(1)}, f32[16,512]{1,0:T(8,128)S(1)}, f32[16,512]{1,0:T(8,128)S(1)}, f32[16,512]{1,0:T...) custom-call(s32[5]{0:T(128)S(1)} %stack.31.place_ref, ...), custom_call_target="tpu_custom_call" | custom-call | tf_op jit(solution)/shard_map/power_2/pallas_call | solution.py:559
  54.8 2.8 %collective-permute-start.16 = (f32[160,128]{1,0:T(8,128)S(1)}, f32[160,128]{1,0:T(8,128)S(1)}, u32[]{:S(2)}, u32[]{:S(2)}) collective-permute-start(f32[160,128]{1,0:T(8,128)S(1)} %get-tuple-element.86), channel_id=1, source_target_pairs={{2,4},{4,2},{6,8},{8,6},{10,12},{12,10},{14,0},{0,14},{3,5},{5,3},... | collective-permute-start | bytes 245768 | tf_op jit(solution)/shard_map/ppermute | solution.py:604
  57.6 0.0 collective-permute-start.15
  57.6 0.0 collective-permute-start.19
  57.6 2.6 %collective-permute-start.18 = (f32[32,128]{1,0:T(8,128)S(1)}, f32[32,128]{1,0:T(8,128)S(1)}, u32[]{:S(2)}, u32[]{:S(2)}) collective-permute-start(f32[32,128]{1,0:T(8,128)S(1)} %get-tuple-element.81), channel_id=1, source_target_pairs={{4,8},{8,4},{6,10},{10,6},{12,0},{0,12},{14,2},{2,14},{5,9},{9,5},... | collective-permute-start | bytes 49160 | tf_op jit(solution)/shard_map/ppermute | solution.py:610
  60.2 0.0 collective-permute-start.17
  60.2 3.0 %collective-permute-done.18.far_d_ref = f32[32,128]{1,0:T(8,128)S(1)} collective-permute-done((f32[32,128]{1,0:T(8,128)S(1)}, f32[32,128]{1,0:T(8,128)S(1)}, u32[]{:S(2)}, u32[]{:S(2)}) %collective-permute-start.18) | collective-permute-done | bytes 16416 | tf_op jit(solution)/shard_map/ppermute | solution.py:610
  63.2 0.8 collective-permute-done.17.far_c_ref
  63.9 0.0 collective-permute-done.19.core_in_ref
  63.9 0.0 collective-permute-done.16.near_b_ref
  63.9 0.0 collective-permute-done.15.near_a_ref
  64.0 3.6 %power_3.1 = f32[8,32]{1,0:T(8,128)S(1)} custom-call(s32[5]{0:T(128)S(1)} %stack.31.place_ref, f32[32,16,512]{2,1,0:T(8,128)S(1)} %get-tuple-element.77.v_ref.v2_ref, f32[16,512]{1,0:T(8,128)S(1)} %get-tuple-element.78.vf_ref.f2_ref, f32[2,32,512]{2,1,0:T(8,128)S(1)} %get-tuple-element.58.halo_in_ref, f32[160,128]{1,0:T(8,128)S(1)} %collective-permute-done.15.near_a_ref, ...), custom_call_target="tpu_custom_call" | custom-call | tf_op jit(solution)/shard_map/power_3/pallas_call | solution.py:559
  67.6 10.8 %all_to_all.5.totals_ref = f32[16,8,128]{2,1,0:T(8,128)S(1)} all-to-all(f32[16,8,128]{2,1,0:T(8,128)S(1)} %broadcast_in_dim.12), channel_id=1, replica_groups=mesh['grp'=2,'gx'=8,'gy'=2] {'gx','gy'}, dimensions={0} | all-to-all | bytes 131072 | tf_op jit(solution)/shard_map/all_to_all | solution.py:760
  78.4 2.1 %iterate.1 = (f32[32,16,512]{2,1,0:T(8,128)}, f32[16,512]{1,0:T(8,128)}) custom-call(s32[5]{0:T(128)S(1)} %stack.31.place_ref, f32[16,8,128]{2,1,0:T(8,128)S(1)} %all_to_all.5.totals_ref, f32[32,16,512]{2,1,0:T(8,128)S(1)} %get-tuple-element.56.v_ref.v0_ref, f32[32,16,512]{2,1,0:T(8,128)S(1)} %get-tuple-element.67.v_ref.v1_ref, ...), custom_call_target="tpu_custom_call" | custom-call | tf_op jit(solution)/shard_map/iterate/pallas_call | solution.py:559
  (29 shorter events, 0.1 us)
Async XLA Ops:
  0.6 2.1 %copy-start.5 = (f32[16,512]{1,0:T(8,128)S(1)}, f32[16,512]{1,0:T(8,128)}, u32[]{:S(2)}) copy-start(f32[16,512]{1,0:T(8,128)} %aperture_ref.1) | copy-start | bytes 98308
  1.4 1.3 %collective-permute-start = (s32[16,1]{1,0:T(8,128)S(1)}, s32[16,1]{1,0:T(8,128)S(1)}, u32[]{:S(2)}, u32[]{:S(2)}) collective-permute-start(s32[16,1]{1,0:T(8,128)S(1)} %slice_select_fusion), channel_id=1, source_target_pairs={{0,1},{1,0},{2,3},{3,2},{4,5},{5,4},{6,7},{7,6},{8,9},{9,8},{10,11... | collective-permute-start | bytes 200 | tf_op jit(solution)/shard_map/ppermute | solution.py:614
  1.9 0.7 copy-start.13
  1.9 0.7 copy-start.14
  1.9 0.8 %copy-start.8 = (s32[1,1,2,128]{3,2,1,0:T(2,128)S(1)}, s32[1,1,2,128]{3,2,1,0:T(2,128)}, u32[]{:S(2)}) copy-start(s32[1,1,2,128]{3,2,1,0:T(2,128)} %param.24) | copy-start | bytes 3076
  1.9 0.9 %copy-start.11 = (s32[1,128]{1,0:T(1,128)S(1)}, s32[1,128]{1,0:T(1,128)}, u32[]{:S(2)}) copy-start(s32[1,128]{1,0:T(1,128)} %slots_ref.1) | copy-start | bytes 1540
  1.9 0.9 %copy-start.2 = (s32[16,512]{1,0:T(8,128)S(1)}, s32[16,512]{1,0:T(8,128)}, u32[]{:S(2)}) copy-start(s32[16,512]{1,0:T(8,128)} %class_ref.1) | copy-start | bytes 98308
  1.9 0.9 %copy-start.4 = (f32[16,512]{1,0:T(8,128)S(1)}, f32[16,512]{1,0:T(8,128)}, u32[]{:S(2)}) copy-start(f32[16,512]{1,0:T(8,128)} %storage_ref.1) | copy-start | bytes 98308
  2.7 0.7 copy-start.10
  3.4 1.2 %copy-start = (f32[32,16,512]{2,1,0:T(8,128)S(1)}, f32[32,16,512]{2,1,0:T(8,128)}, u32[]{:S(2)}) copy-start(f32[32,16,512]{2,1,0:T(8,128)} %source_ref.3) | copy-start | bytes 3145732
  4.6 12.0 %copy-start.1 = (f32[32,16,512]{2,1,0:T(8,128)S(1)}, f32[32,16,512]{2,1,0:T(8,128)}, u32[]{:S(2)}) copy-start(f32[32,16,512]{2,1,0:T(8,128)} %source_ref.3) | copy-start | bytes 3145732
  5.5 11.1 %copy-start.3 = (f32[16,512]{1,0:T(8,128)S(1)}, f32[16,512]{1,0:T(8,128)}, u32[]{:S(2)}) copy-start(f32[16,512]{1,0:T(8,128)} %source_f_ref.1) | copy-start | bytes 98308
  5.5 11.1 %collective-permute-start.2 = (f32[152,128]{1,0:T(8,128)S(1)}, f32[152,128]{1,0:T(8,128)S(1)}, u32[]{:S(2)}, u32[]{:S(2)}) collective-permute-start(f32[152,128]{1,0:T(8,128)S(1)} %get-tuple-element.90), channel_id=1, source_target_pairs={{2,4},{4,2},{6,8},{8,6},{10,12},{12,10},{14,0},{0,14},{3,5},{5,3},... | collective-permute-start | bytes 233480 | tf_op jit(solution)/shard_map/ppermute | solution.py:604
  11.1 5.5 %collective-permute-start.1 = (f32[152,128]{1,0:T(8,128)S(1)}, f32[152,128]{1,0:T(8,128)S(1)}, u32[]{:S(2)}, u32[]{:S(2)}) collective-permute-start(f32[152,128]{1,0:T(8,128)S(1)} %get-tuple-element.91), channel_id=1, source_target_pairs={{0,2},{2,0},{4,6},{6,4},{8,10},{10,8},{12,14},{14,12},{1,3},{3,1},... | collective-permute-start | bytes 233480 | tf_op jit(solution)/shard_map/ppermute | solution.py:603
  11.1 5.4 %collective-permute-start.4 = (f32[16,128]{1,0:T(8,128)S(1)}, f32[16,128]{1,0:T(8,128)S(1)}, u32[]{:S(2)}, u32[]{:S(2)}) collective-permute-start(f32[16,128]{1,0:T(8,128)S(1)} %get-tuple-element.48), channel_id=1, source_target_pairs={{4,8},{8,4},{6,10},{10,6},{12,0},{0,12},{14,2},{2,14},{5,9},{9,5},... | collective-permute-start | bytes 24584 | tf_op jit(solution)/shard_map/ppermute | solution.py:610
  11.7 4.8 %collective-permute-start.3 = (f32[16,128]{1,0:T(8,128)S(1)}, f32[16,128]{1,0:T(8,128)S(1)}, u32[]{:S(2)}, u32[]{:S(2)}) collective-permute-start(f32[16,128]{1,0:T(8,128)S(1)} %get-tuple-element.48), channel_id=1, source_target_pairs={{0,4},{4,0},{2,6},{6,2},{8,12},{12,8},{10,14},{14,10},{1,5},{5,1},... | collective-permute-start | bytes 24584 | tf_op jit(solution)/shard_map/ppermute | solution.py:609
  12.8 0.7 copy-start.7
  12.8 0.7 copy-start.6
  12.8 0.7 copy-start.9
  16.6 0.7 copy-start.12
  23.4 9.2 %collective-permute-start.9 = (f32[176,128]{1,0:T(8,128)S(1)}, f32[176,128]{1,0:T(8,128)S(1)}, u32[]{:S(2)}, u32[]{:S(2)}) collective-permute-start(f32[176,128]{1,0:T(8,128)S(1)} %get-tuple-element.60), channel_id=1, source_target_pairs={{0,1},{1,0},{2,3},{3,2},{4,5},{5,4},{6,7},{7,6},{8,9},{9,8},{10,11... | collective-permute-start | bytes 270344 | tf_op jit(solution)/shard_map/ppermute | solution.py:614
  23.5 5.7 %collective-permute-start.8 = (f32[48,128]{1,0:T(8,128)S(1)}, f32[48,128]{1,0:T(8,128)S(1)}, u32[]{:S(2)}, u32[]{:S(2)}) collective-permute-start(f32[48,128]{1,0:T(8,128)S(1)} %get-tuple-element.59), channel_id=1, source_target_pairs={{4,8},{8,4},{6,10},{10,6},{12,0},{0,12},{14,2},{2,14},{5,9},{9,5},... | collective-permute-start | bytes 73736 | tf_op jit(solution)/shard_map/ppermute | solution.py:610
  25.5 3.9 %collective-permute-start.7 = (f32[48,128]{1,0:T(8,128)S(1)}, f32[48,128]{1,0:T(8,128)S(1)}, u32[]{:S(2)}, u32[]{:S(2)}) collective-permute-start(f32[48,128]{1,0:T(8,128)S(1)} %get-tuple-element.59), channel_id=1, source_target_pairs={{0,4},{4,0},{2,6},{6,2},{8,12},{12,8},{10,14},{14,10},{1,5},{5,1},... | collective-permute-start | bytes 73736 | tf_op jit(solution)/shard_map/ppermute | solution.py:609
  25.5 6.5 %collective-permute-start.6 = (f32[48,128]{1,0:T(8,128)S(1)}, f32[48,128]{1,0:T(8,128)S(1)}, u32[]{:S(2)}, u32[]{:S(2)}) collective-permute-start(f32[48,128]{1,0:T(8,128)S(1)} %get-tuple-element.59), channel_id=1, source_target_pairs={{2,4},{4,2},{6,8},{8,6},{10,12},{12,10},{14,0},{0,14},{3,5},{5,3},... | collective-permute-start | bytes 73736 | tf_op jit(solution)/shard_map/ppermute | solution.py:604
  28.8 3.8 %collective-permute-start.5 = (f32[48,128]{1,0:T(8,128)S(1)}, f32[48,128]{1,0:T(8,128)S(1)}, u32[]{:S(2)}, u32[]{:S(2)}) collective-permute-start(f32[48,128]{1,0:T(8,128)S(1)} %get-tuple-element.59), channel_id=1, source_target_pairs={{0,2},{2,0},{4,6},{6,4},{8,10},{10,8},{12,14},{14,12},{1,3},{3,1},... | collective-permute-start | bytes 73736 | tf_op jit(solution)/shard_map/ppermute | solution.py:603
  39.2 9.1 %collective-permute-start.11 = (f32[160,128]{1,0:T(8,128)S(1)}, f32[160,128]{1,0:T(8,128)S(1)}, u32[]{:S(2)}, u32[]{:S(2)}) collective-permute-start(f32[160,128]{1,0:T(8,128)S(1)} %get-tuple-element.88), channel_id=1, source_target_pairs={{2,4},{4,2},{6,8},{8,6},{10,12},{12,10},{14,0},{0,14},{3,5},{5,3},... | collective-permute-start | bytes 245768 | tf_op jit(solution)/shard_map/ppermute | solution.py:604
  42.0 6.3 %collective-permute-start.10 = (f32[160,128]{1,0:T(8,128)S(1)}, f32[160,128]{1,0:T(8,128)S(1)}, u32[]{:S(2)}, u32[]{:S(2)}) collective-permute-start(f32[160,128]{1,0:T(8,128)S(1)} %get-tuple-element.89), channel_id=1, source_target_pairs={{0,2},{2,0},{4,6},{6,4},{8,10},{10,8},{12,14},{14,12},{1,3},{3,1},... | collective-permute-start | bytes 245768 | tf_op jit(solution)/shard_map/ppermute | solution.py:603
  42.0 6.3 %collective-permute-start.14 = (f32[144,128]{1,0:T(8,128)S(1)}, f32[144,128]{1,0:T(8,128)S(1)}, u32[]{:S(2)}, u32[]{:S(2)}) collective-permute-start(f32[144,128]{1,0:T(8,128)S(1)} %get-tuple-element.72), channel_id=1, source_target_pairs={{0,1},{1,0},{2,3},{3,2},{4,5},{5,4},{6,7},{7,6},{8,9},{9,8},{10,11... | collective-permute-start | bytes 221192 | tf_op jit(solution)/shard_map/ppermute | solution.py:614
  42.0 5.5 %collective-permute-start.13 = (f32[32,128]{1,0:T(8,128)S(1)}, f32[32,128]{1,0:T(8,128)S(1)}, u32[]{:S(2)}, u32[]{:S(2)}) collective-permute-start(f32[32,128]{1,0:T(8,128)S(1)} %get-tuple-element.71), channel_id=1, source_target_pairs={{4,8},{8,4},{6,10},{10,6},{12,0},{0,12},{14,2},{2,14},{5,9},{9,5},... | collective-permute-start | bytes 49160 | tf_op jit(solution)/shard_map/ppermute | solution.py:610
  44.6 3.7 %collective-permute-start.12 = (f32[32,128]{1,0:T(8,128)S(1)}, f32[32,128]{1,0:T(8,128)S(1)}, u32[]{:S(2)}, u32[]{:S(2)}) collective-permute-start(f32[32,128]{1,0:T(8,128)S(1)} %get-tuple-element.71), channel_id=1, source_target_pairs={{0,4},{4,0},{2,6},{6,2},{8,12},{12,8},{10,14},{14,10},{1,5},{5,1},... | collective-permute-start | bytes 49160 | tf_op jit(solution)/shard_map/ppermute | solution.py:609
  54.8 9.1 %collective-permute-start.16 = (f32[160,128]{1,0:T(8,128)S(1)}, f32[160,128]{1,0:T(8,128)S(1)}, u32[]{:S(2)}, u32[]{:S(2)}) collective-permute-start(f32[160,128]{1,0:T(8,128)S(1)} %get-tuple-element.86), channel_id=1, source_target_pairs={{2,4},{4,2},{6,8},{8,6},{10,12},{12,10},{14,0},{0,14},{3,5},{5,3},... | collective-permute-start | bytes 245768 | tf_op jit(solution)/shard_map/ppermute | solution.py:604
  57.6 6.3 %collective-permute-start.15 = (f32[160,128]{1,0:T(8,128)S(1)}, f32[160,128]{1,0:T(8,128)S(1)}, u32[]{:S(2)}, u32[]{:S(2)}) collective-permute-start(f32[160,128]{1,0:T(8,128)S(1)} %get-tuple-element.87), channel_id=1, source_target_pairs={{0,2},{2,0},{4,6},{6,4},{8,10},{10,8},{12,14},{14,12},{1,3},{3,1},... | collective-permute-start | bytes 245768 | tf_op jit(solution)/shard_map/ppermute | solution.py:603
  57.6 6.3 %collective-permute-start.19 = (f32[144,128]{1,0:T(8,128)S(1)}, f32[144,128]{1,0:T(8,128)S(1)}, u32[]{:S(2)}, u32[]{:S(2)}) collective-permute-start(f32[144,128]{1,0:T(8,128)S(1)} %get-tuple-element.82), channel_id=1, source_target_pairs={{0,1},{1,0},{2,3},{3,2},{4,5},{5,4},{6,7},{7,6},{8,9},{9,8},{10,11... | collective-permute-start | bytes 221192 | tf_op jit(solution)/shard_map/ppermute | solution.py:614
  57.6 5.5 %collective-permute-start.18 = (f32[32,128]{1,0:T(8,128)S(1)}, f32[32,128]{1,0:T(8,128)S(1)}, u32[]{:S(2)}, u32[]{:S(2)}) collective-permute-start(f32[32,128]{1,0:T(8,128)S(1)} %get-tuple-element.81), channel_id=1, source_target_pairs={{4,8},{8,4},{6,10},{10,6},{12,0},{0,12},{14,2},{2,14},{5,9},{9,5},... | collective-permute-start | bytes 49160 | tf_op jit(solution)/shard_map/ppermute | solution.py:610
  60.2 3.7 %collective-permute-start.17 = (f32[32,128]{1,0:T(8,128)S(1)}, f32[32,128]{1,0:T(8,128)S(1)}, u32[]{:S(2)}, u32[]{:S(2)}) collective-permute-start(f32[32,128]{1,0:T(8,128)S(1)} %get-tuple-element.81), channel_id=1, source_target_pairs={{0,4},{4,0},{2,6},{6,2},{8,12},{12,8},{10,14},{14,10},{1,5},{5,1},... | collective-permute-start | bytes 49160 | tf_op jit(solution)/shard_map/ppermute | solution.py:609
where the time goes:
time: 80.8 us; the launch traced here: 80.5 us
  Pallas kernels  26 us (32%)
  starting transfers between devices  24 us (30%)
  waiting for transfers between devices  13.9 us (17%)
  blocking collectives  10.8 us (13%)
  local copies, waits for them, and re-layouts  3.96 us (5%)
  other arithmetic  0.92 us (1%)
  between operations  0.88 us (1%)
    pallas_call x7, Pallas kernels, call(): pl.pallas_call(kernel, name=name, out_shape=[jax.ShapeDtypeStruct(shape,...  26 us
    ppermute x4, starting transfers between devices, near(): lax.ppermute(to_b, 'gx', pairs_of(count, 1, 1))  14.4 us
    all_to_all x1, blocking collectives, per_device(): lax.all_to_all(jnp.broadcast_to(moments[None], (peers, 8, LANES)), ('gx',...  10.8 us
    ppermute x4, waiting for transfers between devices, far(): lax.ppermute(value, 'gx', pairs_of(count, 2, 1))  8.84 us
    ppermute x4, starting transfers between devices, far(): lax.ppermute(value, 'gx', pairs_of(count, 2, 1))  7.89 us
    unnamed x30, local copies, waits for them, and re-layouts  3.82 us
    ppermute x4, waiting for transfers between devices, near(): lax.ppermute(to_b, 'gx', pairs_of(count, 1, 1))  2.67 us
    ppermute x4, waiting for transfers between devices, far(): lax.ppermute(value, 'gx', pairs_of(count, 2, 0))  1.81 us
  transfers between devices with their start and end apart: 20, of which 9 were waited for; matrix products, arithmetic and copies ran while one was open for 0% of the time, Pallas kernels for 0%

commit v1 on v0

v1 whole, which is shorter than its diff:
```python
import functools

import jax
import jax.numpy as jnp
from jax import lax
from jax.experimental import pallas as pl
from jax.experimental.pallas import tpu as pltpu
from jax.sharding import PartitionSpec as P

FRACTURE_STORAGE = 0.1
F32 = jnp.float32
BF16 = jnp.bfloat16
LANES = 128
GROUP = 16


def split3(x):
    high = x.astype(BF16)
    rest = x - high.astype(F32)
    mid = rest.astype(BF16)
    low = (rest - mid.astype(F32)).astype(BF16)
    return jnp.concatenate([high, mid, low], axis=0)


def pick(x, table, transposed=False):
    rows = x.shape[0]
    dims = (((1,), (1 if transposed else 0,)), ((), ()))
    out = lax.dot_general(split3(x), table, dims, preferred_element_type=F32)
    return out[:rows] + out[rows : 2 * rows] + out[2 * rows :]


def harmonic(first_perm, second_perm):
    return 2.0 * first_perm * second_perm / (first_perm + second_perm)


def one_hot(index_row, size):
    shape = (size, index_row.shape[1])
    ids = lax.broadcasted_iota(jnp.int32, shape, 0)
    return jnp.where(ids == index_row, 1.0, 0.0).astype(BF16)


def to_blocks(x):
    return jnp.concatenate(
        [x[:, q : q + LANES] for q in range(0, x.shape[1], LANES)], axis=0
    )


def from_blocks(x, rows):
    return jnp.concatenate(
        [x[q : q + rows] for q in range(0, x.shape[0], rows)], axis=1
    )


def by_group(first, second, third, fourth):
    group = first.shape[1] // 4
    lane = lax.broadcasted_iota(jnp.int32, first.shape, 1)
    return jnp.where(
        lane < group,
        first,
        jnp.where(lane < 2 * group, second, jnp.where(lane < 3 * group, third, fourth)),
    )


def total_rows(x):
    return jnp.sum(jnp.transpose(x), axis=0, keepdims=True)


def fold_lanes(x):
    rows, width = x.shape
    out = x[:, :LANES]
    for q in range(LANES, width, LANES):
        out = out + x[:, q : q + LANES]
    return out


def opening_kernel(
    place_ref,
    perm_table_ref,
    class_ref,
    col_ref,
    storage_ref,
    source_ref,
    aperture_ref,
    slots_ref,
    cell_ref,
    weight_ref,
    coef_ref,
    oy_ref,
    ox_ref,
    oslot_ref,
    cond_ref,
    up_ref,
    down_ref,
    far_ref,
):
    x_cells, y_cells = class_ref.shape
    members = source_ref.shape[0]
    half = aperture_ref.shape[0]
    high_side = place_ref[2] == 0

    def perm_of(classes):
        perm = jnp.zeros(classes.shape, F32)
        for index in range(perm_table_ref.shape[0]):
            perm = jnp.where(classes == index, perm_table_ref[index], perm)
        return perm

    perm = perm_of(class_ref[...])
    col = perm_of(col_ref[...])
    lane = lax.broadcasted_iota(jnp.int32, perm.shape, 1)
    row = lax.broadcasted_iota(jnp.int32, perm.shape, 0)
    north = jnp.concatenate([perm[:, 1:], col], axis=1)
    south = jnp.concatenate([col, perm[:, :-1]], axis=1)
    tn = jnp.where((lane == y_cells - 1) & jnp.logical_not(high_side), 0.0, harmonic(perm, north))
    ts = jnp.where((lane == 0) & high_side, 0.0, harmonic(perm, south))
    east = jnp.concatenate([perm[1:], perm[:1]], axis=0)
    west = jnp.concatenate([perm[-1:], perm[:-1]], axis=0)
    te = jnp.where(row == x_cells - 1, 0.0, harmonic(perm, east))
    tw = jnp.where(row == 0, 0.0, harmonic(perm, west))

    cell = cell_ref[...]
    oy = one_hot(cell % y_cells, y_cells)
    oy_ref[...] = oy
    shape_x = (x_cells, cell.shape[1])
    at_x = lax.broadcasted_iota(jnp.int32, shape_x, 0) == cell // y_cells
    ox_ref[...] = jnp.where(at_x, 1.0, 0.0)
    wsum = pick(jnp.where(at_x, weight_ref[...], 0.0), oy, True)

    part = storage_ref[...] + te + tw + tn + ts + wsum
    coef_ref[0] = te
    coef_ref[1] = tw
    coef_ref[2] = tn
    coef_ref[3] = ts
    coef_ref[4] = part
    coef_ref[5] = perm

    aperture = aperture_ref[...]
    cond = aperture * aperture * aperture
    cond_ref[...] = cond
    oslot = one_hot(slots_ref[...], cond.shape[1])
    oslot_ref[...] = oslot
    supplied = pick(cond, oslot)
    far_ref[...] = supplied
    blocks = y_cells // LANES
    for ref, at in ((up_ref, x_cells - 1), (down_ref, 0)):
        edge = source_ref[:, at, :]
        ref[0 : blocks * members, :] = to_blocks(edge)
        ref[blocks * members : blocks * members + blocks, :] = to_blocks(perm[at : at + 1])
        ref[blocks * members + blocks : blocks * members + 2 * blocks, :] = to_blocks(part[at : at + 1])
        ref[blocks * members + 2 * blocks : blocks * members + 2 * blocks + half, :] = supplied


def neighbours(place_ref, near_a_ref, near_b_ref, far_c_ref, far_d_ref):
    def reader(flag, at_zero, at_one):
        return lambda at, size: jnp.where(
            place_ref[flag] == 0, at_zero[at : at + size, :], at_one[at : at + size, :]
        )

    return (
        reader(0, near_a_ref, near_b_ref),
        reader(0, near_b_ref, near_a_ref),
        reader(1, far_c_ref, far_d_ref),
        reader(1, far_d_ref, far_c_ref),
    )


def spread(x, members):
    return jnp.concatenate(
        [jnp.broadcast_to(x[:, q : q + LANES], (members, LANES)) for q in range(0, x.shape[1], LANES)], axis=0
    )


def margin_values(found, ox):
    found = found.reshape(-1, *ox.shape) * ox[None]
    return jnp.sum(found, axis=1)


def border_column(tile_low, tile_high, high_side, m):
    tile = jnp.where(high_side, tile_high, tile_low)
    return pltpu.roll(tile, jnp.where(high_side, lax.rem(m + 1, LANES), m), 1)


def border_row(row_values, high_side):
    members, y_cells = row_values.shape
    tile = jnp.where(high_side, row_values[:, y_cells - LANES :], row_values[:, :LANES])
    turned = jnp.transpose(tile)
    line = jnp.where(high_side, turned[LANES - 1 :], turned[:1])
    return jnp.concatenate([line, jnp.zeros((1, LANES - members), F32)], axis=1)


def finish_edges(high_rows, low_rows, partial_ref, column, high_side, oy, ox):
    members = high_rows.shape[0]
    x_cells = ox.shape[0]
    found = pick(jnp.concatenate([high_rows, low_rows], axis=0), oy)
    margin = partial_ref[...] + found[:members] * ox[x_cells - 1 :] + found[members:] * ox[:1]
    row = lax.broadcasted_iota(jnp.int32, column.shape, 0)
    column = jnp.where(row == x_cells - 1, border_row(high_rows, high_side), column)
    return margin, jnp.where(row == 0, border_row(low_rows, high_side), column)


def send_network(vf, sr, table, ghost_table, diff_ref, refs):
    half = vf.shape[0]
    rows = sr.shape[1]
    found = pick(vf, table)
    diff_ref[...] = found[:, :rows]
    sums = pick(sr * found[:, :rows], ghost_table, True)
    for ref, at in refs:
        ref[at : at + half, :] = found[:, rows:]
        ref[at + half : at + 2 * half, :] = sums


def send_core(core_ref, vf, margin, weight, ofrac, column, j, work_ref, wown_ref):
    half, frac_cells = vf.shape
    work_ref[...] = pick(margin * weight, ofrac, True)
    wown_ref[...] = work_ref[pl.ds(pl.multiple_of(j * half, half), half), :]
    other = work_ref[pl.ds(pl.multiple_of((1 - j) * half, half), half), :]
    size = frac_cells // LANES * half
    core_ref[0:size, :] = to_blocks(vf)
    core_ref[size : 2 * size, :] = to_blocks(other)
    core_ref[2 * size : 2 * size + column.shape[0], :] = column


def inside_kernel(
    place_ref,
    coef_ref,
    source_ref,
    local_ref,
    other_ref,
    frac_ref,
    oslot_ref,
    oy_ref,
    ox_ref,
    first_ref,
    second_ref,
    table_ref,
    ghost_table_ref,
    ofrac_ref,
    v_ref,
    margin_ref,
    column_ref,
):
    members, x_cells, y_cells = source_ref.shape
    frac_cells = table_ref.shape[0]
    rows = local_ref.shape[1]
    other = other_ref[...]
    first, second = one_hot(local_ref[...], frac_cells), one_hot(other, frac_cells)
    first_ref[...] = first
    second_ref[...] = second
    table_ref[:, :rows] = first - second
    table_ref[:, rows:] = oslot_ref[...]
    ghost_table_ref[...] = one_hot(other - frac_cells, ghost_table_ref.shape[0])
    ofrac_ref[...] = one_hot(frac_ref[...], frac_cells)

    high_side = place_ref[2] == 0
    inverse = 1.0 / coef_ref[4]
    row_x = lax.broadcasted_iota(jnp.int32, ox_ref.shape, 0)
    inner_x = jnp.where((row_x == 0) | (row_x == x_cells - 1), 0.0, ox_ref[...])
    lane_c = lax.broadcasted_iota(jnp.int32, (x_cells, LANES), 1)
    column_ref[...] = jnp.zeros_like(column_ref)

    @pl.loop(0, members // GROUP)
    def _(index):
        start = index * GROUP
        block = source_ref[pl.ds(start, GROUP)] * inverse[None]
        v_ref[pl.ds(start, GROUP)] = block
        found = pick(block.reshape(GROUP * x_cells, y_cells), oy_ref[...])
        margin_ref[pl.ds(start, GROUP), :] = margin_values(found, inner_x)
        column = column_ref[...]
        for k in range(GROUP):
            m = start + k
            moved = border_column(block[k, :, :LANES], block[k, :, y_cells - LANES :], high_side, m)
            column = jnp.where(lane_c == m, moved, column)
        column_ref[...] = column


def first_kernel(
    place_ref,
    count_ref,
    coef_ref,
    cond_ref,
    source_ref,
    source_f_ref,
    weight_ref,
    near_a_ref,
    near_b_ref,
    far_c_ref,
    far_d_ref,
    first_ref,
    second_ref,
    table_ref,
    ghost_table_ref,
    ofrac_ref,
    oy_ref,
    ox_ref,
    inner_margin_ref,
    inner_column_ref,
    v_in_ref,
    unit_ref,
    vf_ref,
    halo_ref,
    sr_ref,
    scale_f_ref,
    diff_ref,
    wown_ref,
    sent_ref,
    core_ref,
    v_ref,
    work_ref,
):
    members, x_cells, y_cells = source_ref.shape
    half, frac_cells = source_f_ref.shape
    blocks = y_cells // LANES
    j = place_ref[2]
    high_side = j == 0
    base = blocks * members
    plus1, minus1, plus2, minus2 = neighbours(place_ref, near_a_ref, near_b_ref, far_c_ref, far_d_ref)

    slot_at = base + 2 * blocks
    ghosts = by_group(minus1(slot_at, half), plus1(slot_at, half), minus2(0, half), plus2(0, half))
    table, ghost_table = table_ref[...], ghost_table_ref[...]
    cond = cond_ref[...]
    cond_first = pick(cond, first_ref[...])
    cond_second = pick(cond, second_ref[...]) + pick(ghosts, ghost_table)
    lane = lax.broadcasted_iota(jnp.int32, cond_first.shape, 1)
    live = jnp.zeros(cond_first.shape, jnp.bool_)
    for block in range(cond_first.shape[1] // LANES):
        start = block * LANES
        live = live | ((lane >= start) & (lane < start + count_ref[block]))
    sr = jnp.where(live, harmonic(cond_first, cond_second), 0.0)
    sr_ref[...] = sr
    diag_f = FRACTURE_STORAGE + pick(sr, first_ref[...], True)
    inverse_f = 1.0 / diag_f
    scale_f_ref[0] = inverse_f
    scale_f_ref[1] = diag_f
    vf = source_f_ref[...] * inverse_f
    vf_ref[...] = vf
    send_network(vf, sr, table, ghost_table, diff_ref, [(sent_ref, 0)])
    sent_ref[2 * half : 3 * half, :] = pick(sr, ghost_table, True)

    perm, part = coef_ref[5], coef_ref[4]
    row = lax.broadcasted_iota(jnp.int32, perm.shape, 0)
    perm_plus = from_blocks(plus1(base, blocks), 1)
    perm_minus = from_blocks(minus1(base, blocks), 1)
    part_plus = from_blocks(plus1(base + blocks, blocks), 1)
    part_minus = from_blocks(minus1(base + blocks, blocks), 1)
    te_edge = jnp.where(place_ref[4] == 1, 0.0, harmonic(perm[x_cells - 1 :], perm_plus))
    tw_edge = jnp.where(place_ref[3] == 1, 0.0, harmonic(perm[:1], perm_minus))
    te = jnp.where(row == x_cells - 1, te_edge, coef_ref[0])
    tw = jnp.where(row == 0, tw_edge, coef_ref[1])
    diag = part + jnp.where(row == x_cells - 1, te_edge, 0.0) + jnp.where(row == 0, tw_edge, 0.0)
    inverse = 1.0 / diag
    unit_ref[0] = te * inverse
    unit_ref[1] = tw * inverse
    unit_ref[2] = coef_ref[2] * inverse
    unit_ref[3] = coef_ref[3] * inverse
    unit_ref[4] = inverse
    unit_ref[5] = diag
    halo_ref[0] = plus1(0, base) * spread(1.0 / (part_plus + te_edge), members)
    halo_ref[1] = minus1(0, base) * spread(1.0 / (part_minus + tw_edge), members)
    high_rows = source_ref[:, x_cells - 1, :] * inverse[x_cells - 1 :]
    low_rows = source_ref[:, 0, :] * inverse[:1]
    v_ref[:, x_cells - 1, :] = high_rows
    v_ref[:, 0, :] = low_rows
    margin, column = finish_edges(
        high_rows, low_rows, inner_margin_ref, inner_column_ref[...], high_side, oy_ref[...], ox_ref[...]
    )
    weight = weight_ref[...]
    send_core(core_ref, vf, margin, weight, ofrac_ref[...], column, j, work_ref, wown_ref)
    wsum = pick(jnp.broadcast_to(weight, (8, weight.shape[1])), ofrac_ref[...], True)
    tail = core_ref.shape[0] - 8 * (frac_cells // LANES)
    core_ref[tail:, :] = to_blocks(wsum)


def interior_kernel(
    power,
    place_ref,
    v_ref,
    before_ref,
    vf_ref,
    before_f_ref,
    core_ref,
    scale_f_ref,
    unit_ref,
    weight_ref,
    ofrac_ref,
    oy_ref,
    ox_ref,
    *refs,
):
    if power < 3:
        image_ref, margin_ref, column_ref, dots_ref, flow_ref, work_ref, *acc_refs = refs
    else:
        dots_ref, flow_ref, work_ref, *acc_refs = refs
    members, x_cells, y_cells = v_ref.shape
    half, frac_cells = vf_ref.shape
    blocks = y_cells // LANES
    j = place_ref[2]
    high_side = j == 0
    size = frac_cells // LANES * half
    theirs = from_blocks(core_ref[0:size, :], half)
    column_in = core_ref[2 * size : 2 * size + x_cells, :]
    vf = vf_ref[...]
    own_rows = pl.ds(pl.multiple_of(j * half, half), half)
    work_ref[own_rows, :] = vf
    work_ref[pl.ds(pl.multiple_of((1 - j) * half, half), half), :] = theirs
    flow_ref[...] = pick(work_ref[...], ofrac_ref[...]) * weight_ref[...]

    heavy_f = vf * scale_f_ref[1]
    for ref in acc_refs:
        ref[...] = jnp.zeros_like(ref)
    acc_refs[0][own_rows, :] = fold_lanes(vf * heavy_f)
    if power > 1:
        acc_refs[1][own_rows, :] = fold_lanes(before_f_ref[...] * heavy_f)

    lane_c = lax.broadcasted_iota(jnp.int32, (x_cells, LANES), 1)
    lane = lax.broadcasted_iota(jnp.int32, (x_cells, y_cells), 1)
    row = lax.broadcasted_iota(jnp.int32, (x_cells, y_cells), 0)
    row_x = lax.broadcasted_iota(jnp.int32, ox_ref.shape, 0)
    oy, ox = oy_ref[...], ox_ref[...]
    inner_x = jnp.where((row_x == 0) | (row_x == x_cells - 1), 0.0, ox)
    te = jnp.where(row == x_cells - 1, 0.0, unit_ref[0])
    tw = jnp.where(row == 0, 0.0, unit_ref[1])
    if power < 3:
        column_ref[...] = jnp.zeros_like(column_ref)

    @pl.loop(0, members // GROUP)
    def _(index):
        start = index * GROUP
        parts = []
        for k in range(GROUP):
            parts.append(ox * flow_ref[pl.ds(start + k, 1), :])
        coupled = pick(jnp.concatenate(parts, axis=0), oy, True)
        if power < 3:
            column = column_ref[...]
        for k in range(GROUP):
            m = start + k
            value = v_ref[m]
            east = pltpu.roll(value, x_cells - 1, 0)
            west = pltpu.roll(value, 1, 0)
            moved = pltpu.roll(column_in, jnp.where(high_side, LANES - 1 - m, lax.rem(LANES - m, LANES)), 1)
            moved = jnp.concatenate([moved] * blocks, axis=1)
            north = jnp.where(lane == y_cells - 1, moved, pltpu.roll(value, y_cells - 1, 1))
            south = jnp.where(lane == 0, moved, pltpu.roll(value, 1, 1))
            image = value - te * east - tw * west - unit_ref[2] * north - unit_ref[3] * south
            image = image - coupled[k * x_cells : (k + 1) * x_cells] * unit_ref[4]
            heavy = value * unit_ref[5]
            at = pl.ds(m, 1)
            acc_refs[0][at, :] += jnp.sum(fold_lanes(value * heavy), axis=0, keepdims=True)
            if power > 1:
                acc_refs[1][at, :] += jnp.sum(fold_lanes(before_ref[m] * heavy), axis=0, keepdims=True)
            if power < 3:
                image_ref[m] = image
                shifted = border_column(image[:, :LANES], image[:, y_cells - LANES :], high_side, m)
                column = jnp.where(lane_c == m, shifted, column)
            else:
                acc_refs[2][at, :] += jnp.sum(fold_lanes(image * heavy), axis=0, keepdims=True)
        if power < 3:
            column_ref[...] = column
            block = image_ref[pl.ds(start, GROUP)]
            found = pick(block.reshape(GROUP * x_cells, y_cells), oy)
            margin_ref[pl.ds(start, GROUP), :] = margin_values(found, inner_x)

    dots = [total_rows(ref[...]) for ref in acc_refs]
    dots.append(jnp.zeros((8 - len(dots), members), F32))
    dots_ref[...] = jnp.concatenate(dots, axis=0)


def finish_kernel(
    power,
    place_ref,
    vf_ref,
    near_a_ref,
    near_b_ref,
    far_c_ref,
    far_d_ref,
    core_in_ref,
    diff_in_ref,
    wown_in_ref,
    sr_ref,
    scale_f_ref,
    unit_ref,
    table_ref,
    ghost_table_ref,
    *refs,
):
    if power == 1:
        (
            halo_ref,
            weight_ref,
            ofrac_ref,
            oy_ref,
            ox_ref,
            inner_margin_ref,
            inner_column_ref,
            image_in_ref,
            own_f_ref,
            *refs,
        ) = refs
    elif power == 2:
        (
            own_f_in_ref,
            weight_ref,
            ofrac_ref,
            oy_ref,
            ox_ref,
            inner_margin_ref,
            inner_column_ref,
            image_in_ref,
            *refs,
        ) = refs
    if power < 3:
        out_f_ref, diff_ref, wown_ref, up_ref, down_ref, sent_ref, core_ref, image_ref, work_ref = refs
    else:
        own_f_in_ref, v_ref, dots1_ref, dots2_ref, dots3_ref, moments_ref, acc_ref = refs
    half, frac_cells = vf_ref.shape
    x_cells, y_cells = unit_ref.shape[1:]
    members = (near_a_ref.shape[0] - 2 * half) // (y_cells // LANES) if power > 1 else image_ref.shape[0]
    blocks = y_cells // LANES
    frac_blocks = frac_cells // LANES
    j = place_ref[2]
    high_side = j == 0
    base = 0 if power == 1 else blocks * members
    plus1, minus1, plus2, minus2 = neighbours(place_ref, near_a_ref, near_b_ref, far_c_ref, far_d_ref)
    rows = sr_ref.shape[1]

    table, ghost_table = table_ref[...], ghost_table_ref[...]
    vf = vf_ref[...]
    ghosts = by_group(minus1(base, half), plus1(base, half), minus2(0, half), plus2(0, half))
    sums = by_group(
        plus1(base + half, half), minus1(base + half, half), plus2(half, half), minus2(half, half)
    )
    size = frac_blocks * half
    their_sums = from_blocks(core_in_ref[size : 2 * size, :], half)
    if power == 1:
        at = 2 * half
        back = by_group(
            plus1(base + at, half), minus1(base + at, half), plus2(at, half), minus2(at, half)
        )
        weight = weight_ref[...]
        wsum = pick(jnp.broadcast_to(weight, (8, weight.shape[1])), ofrac_ref[...], True)
        tail = core_in_ref.shape[0] - 8 * frac_blocks
        wsum = wsum + from_blocks(core_in_ref[tail:, :], 8)
        own_f = FRACTURE_STORAGE + wsum[:1] + pick(back, table[:, rows:], True)
        own_f_ref[...] = own_f
    else:
        own_f = own_f_in_ref[...]
    sr = sr_ref[...]
    flux = sr * (diff_in_ref[...] - pick(ghosts, ghost_table))
    image_f = own_f * vf + pick(jnp.concatenate([flux, -sums], axis=1), table, True)
    image_f = image_f - wown_in_ref[...] - their_sums

    if power == 3:
        acc_ref[...] = jnp.zeros_like(acc_ref)
        acc_ref[pl.ds(pl.multiple_of(j * half, half), half), :] = fold_lanes(vf * image_f)
        for side, at, reader in ((0, x_cells - 1, plus1), (1, 0, minus1)):
            factor = unit_ref[side, at : at + 1, :] * unit_ref[5, at : at + 1, :]
            edge = v_ref[:, at, :] * factor
            for q in range(blocks):
                beyond = reader(q * members, members)
                acc_ref[...] -= edge[:, q * LANES : (q + 1) * LANES] * beyond
        last = total_rows(acc_ref[...]) + dots3_ref[2:3, :]
        gap = jnp.zeros((1, LANES - 3 * members), F32)
        lines = [
            jnp.concatenate([dots1_ref[0:1, :], dots2_ref[1:2, :], dots2_ref[0:1, :], gap], axis=1),
            jnp.concatenate([dots3_ref[1:2, :], dots3_ref[0:1, :], last, gap], axis=1),
        ]
        lines = jnp.concatenate(lines, axis=0)
        moments_ref[...] = jnp.broadcast_to(lines[None], moments_ref.shape)
        return

    next_f = image_f * scale_f_ref[0]
    out_f_ref[...] = next_f
    at = blocks * members
    send_network(next_f, sr, table, ghost_table, diff_ref, [(up_ref, at), (down_ref, at), (sent_ref, 0)])

    edges = []
    for side, at, reader, ref in ((0, x_cells - 1, plus1, up_ref), (1, 0, minus1, down_ref)):
        factor = unit_ref[side, at : at + 1, :]
        old = image_in_ref[:, at, :]
        pieces = []
        for q in range(blocks):
            beyond = halo_ref[side, q * members : (q + 1) * members, :] if power == 1 else reader(q * members, members)
            cut = slice(q * LANES, (q + 1) * LANES)
            piece = old[:, cut] - factor[:, cut] * beyond
            ref[q * members : (q + 1) * members, :] = piece
            pieces.append(piece)
        edge = jnp.concatenate(pieces, axis=1)
        image_ref[:, at, :] = edge
        edges.append(edge)
    margin, column = finish_edges(
        edges[0], edges[1], inner_margin_ref, inner_column_ref[...], high_side, oy_ref[...], ox_ref[...]
    )
    send_core(core_ref, next_f, margin, weight_ref[...], ofrac_ref[...], column, j, work_ref, wown_ref)


def close_kernel(place_ref, totals_ref, v0_ref, v1_ref, v2_ref, f0_ref, f1_ref, f2_ref, x_ref, xf_ref, c_ref):
    members, x_cells, y_cells = v0_ref.shape
    half, frac_cells = f0_ref.shape

    total = jnp.sum(totals_ref[...], axis=0)
    m0, m1, m2, m3, m4, m5 = (
        total[k // 3 : k // 3 + 1, k % 3 * members : k % 3 * members + members] for k in range(6)
    )
    alpha0 = m0 / m1
    rz1 = m0 - 2.0 * alpha0 * m1 + alpha0 * alpha0 * m2
    beta1 = rz1 / m0
    a, b = 1.0 + beta1, -alpha0
    pap1 = a * a * m1 + 2.0 * a * b * m2 + b * b * m3
    alpha1 = rz1 / pap1
    e = -alpha0 - alpha1 * a
    g = -alpha1 * b
    rz2 = m0 + 2.0 * e * m1 + (e * e + 2.0 * g) * m2 + 2.0 * e * g * m3 + g * g * m4
    beta2 = rz2 / rz1
    c = 1.0 + beta2 * a
    d = e + beta2 * b
    pap2 = c * c * m1 + 2.0 * c * d * m2 + (d * d + 2.0 * c * g) * m3 + 2.0 * d * g * m4 + g * g * m5
    alpha2 = rz2 / pap2
    c0 = alpha0 + alpha1 * a + alpha2 * c
    c1 = alpha1 * b + alpha2 * d
    c2 = alpha2 * g
    for k, row in enumerate((c0, c1, c2)):
        row = jnp.concatenate([row, jnp.zeros((1, LANES - members), F32)], axis=1)
        c_ref[k] = jnp.transpose(jnp.broadcast_to(row, (LANES, LANES)))
    j = place_ref[2]
    own = pl.ds(pl.multiple_of(j * half, half), half)

    def wide(k, rows, width):
        return jnp.concatenate([c_ref[k, rows, :]] * (width // LANES), axis=1)

    xf_ref[...] = (
        wide(0, own, frac_cells) * f0_ref[...]
        + wide(1, own, frac_cells) * f1_ref[...]
        + wide(2, own, frac_cells) * f2_ref[...]
    )

    @pl.loop(0, members)
    def _(m):
        rows = pl.ds(m, 1)
        x_ref[m] = (
            wide(0, rows, y_cells) * v0_ref[m]
            + wide(1, rows, y_cells) * v1_ref[m]
            + wide(2, rows, y_cells) * v2_ref[m]
        )


def pairs_of(count, stride, phase):
    out = []
    for index in range(count):
        if (index // stride) % 2 == phase:
            mate = (index + stride) % count
            out += [(index, mate), (mate, index)]
    return out


VMEM = pl.BlockSpec(memory_space=pltpu.VMEM)
SMEM = pl.BlockSpec(memory_space=pltpu.SMEM)


def call(kernel, name, args, outs, scratch=(), scalars=0, cost=None, aliases=None):
    return pl.pallas_call(
        kernel,
        name=name,
        out_shape=[jax.ShapeDtypeStruct(shape, dtype) for shape, dtype in outs],
        in_specs=[SMEM] * scalars + [VMEM] * (len(args) - scalars),
        out_specs=[VMEM] * len(outs),
        scratch_shapes=list(scratch),
        compiler_params=pltpu.CompilerParams(vmem_limit_bytes=40 * 1024 * 1024),
        cost_estimate=cost,
        input_output_aliases=aliases or {},
    )(*args)


def per_device(
    source_matrix,
    source_fracture,
    aperture,
    storage,
    perm_class,
    class_perm,
    send_slots,
    isect_local,
    isect_other,
    isect_count,
    ov_cell,
    ov_frac,
    ov_weight,
    ov_count,
):
    members, x_cells, y_cells = source_matrix.shape
    half, frac_cells = source_fracture.shape
    slots = send_slots.shape[1]
    rows = isect_local.size
    margin = ov_cell.size
    count = lax.axis_size("gx")
    i, j = lax.axis_index("gx"), lax.axis_index("gy")
    place = jnp.stack(
        [i % 2, (i // 2) % 2, j, (i == 0).astype(jnp.int32), (i == count - 1).astype(jnp.int32)]
    ).astype(jnp.int32)

    def near(up, down):
        even = i % 2 == 0
        to_a = jnp.where(even, up, down)
        to_b = jnp.where(even, down, up)
        return (
            lax.ppermute(to_a, "gx", pairs_of(count, 1, 0)),
            lax.ppermute(to_b, "gx", pairs_of(count, 1, 1)),
        )

    def far(value):
        return (
            lax.ppermute(value, "gx", pairs_of(count, 2, 0)),
            lax.ppermute(value, "gx", pairs_of(count, 2, 1)),
        )

    def core(value):
        return lax.ppermute(value, "gy", [(0, 1), (1, 0)])

    blocks = y_cells // LANES
    frac_blocks = frac_cells // LANES
    positions = jnp.arange(LANES, dtype=jnp.int32)
    ov_live = positions[None, :] < ov_count.reshape(-1, 1)
    weight = jnp.where(ov_live, ov_weight.reshape(ov_live.shape), 0.0).reshape(1, margin)
    col = core(jnp.where(j == 0, perm_class[:, y_cells - 1 :], perm_class[:, :1]))
    near_rows = blocks * members + 2 * blocks + half
    coef, oy, ox, oslot, cond, up, down, supplied = call(
        opening_kernel,
        "opening",
        (
            place,
            class_perm,
            perm_class,
            col,
            storage,
            source_matrix,
            aperture,
            send_slots,
            ov_cell.reshape(1, margin),
            weight,
        ),
        [
            ((6, x_cells, y_cells), F32),
            ((y_cells, margin), BF16),
            ((x_cells, margin), F32),
            ((frac_cells, slots), BF16),
            ((half, frac_cells), F32),
            ((near_rows, LANES), F32),
            ((near_rows, LANES), F32),
            ((half, slots), F32),
        ],
        scalars=2,
    )
    field = (members, x_cells, y_cells)
    own = (half, frac_cells)
    hidden = pl.CostEstimate(flops=4_000_000_000, bytes_accessed=12_000_000, transcendentals=0)
    near_a, near_b = near(up, down)
    far_c, far_d = far(supplied)
    first, second, table, ghost_table, ofrac, v0, margin_in, column = call(
        inside_kernel,
        "inside",
        (
            place,
            coef,
            source_matrix,
            isect_local.reshape(1, rows),
            isect_other.reshape(1, rows),
            ov_frac.reshape(1, margin),
            oslot,
            oy,
            ox,
        ),
        [
            ((frac_cells, rows), BF16),
            ((frac_cells, rows), BF16),
            ((frac_cells, rows + slots), BF16),
            ((slots, rows), BF16),
            ((frac_cells, margin), BF16),
            (field, F32),
            ((members, margin), F32),
            ((x_cells, LANES), F32),
        ],
        scalars=1,
        cost=hidden,
    )
    core_rows = 2 * frac_blocks * half + x_cells
    edge_rows = blocks * members
    unit, f0, halo, sr, scale_f, diff, wown, sent, core_msg, v0 = call(
        first_kernel,
        "first_vector",
        (
            place,
            isect_count,
            coef,
            cond,
            source_matrix,
            source_fracture,
            weight,
            near_a,
            near_b,
            far_c,
            far_d,
            first,
            second,
            table,
            ghost_table,
            ofrac,
            oy,
            ox,
            margin_in,
            column,
            v0,
        ),
        [
            ((6, x_cells, y_cells), F32),
            (own, F32),
            ((2, edge_rows, LANES), F32),
            ((half, rows), F32),
            ((2, half, frac_cells), F32),
            ((half, rows), F32),
            (own, F32),
            ((3 * half, LANES), F32),
            ((core_rows + 8 * frac_blocks, LANES), F32),
            (field, F32),
        ],
        scratch=[pltpu.VMEM((members, frac_cells), F32)],
        scalars=2,
        aliases={20: 9},
    )
    near_rows = edge_rows + 2 * half

    def interior(power, v, before, vf, before_f, core_in):
        outs = []
        if power < 3:
            outs = [(field, F32), ((members, margin), F32), ((x_cells, LANES), F32)]
        return call(
            functools.partial(interior_kernel, power),
            f"interior_{power}",
            (place, v, before, vf, before_f, core_in, scale_f, unit, weight, ofrac, oy, ox),
            outs + [((8, members), F32)],
            scratch=[pltpu.VMEM((members, margin), F32), pltpu.VMEM((members, frac_cells), F32)]
            + [pltpu.VMEM((members, LANES), F32)] * power,
            scalars=1,
            cost=hidden,
        )

    finish_outs = [
        (own, F32),
        ((half, rows), F32),
        (own, F32),
        ((near_rows, LANES), F32),
        ((near_rows, LANES), F32),
        ((2 * half, LANES), F32),
        ((core_rows, LANES), F32),
        (field, F32),
    ]
    finish_scratch = [pltpu.VMEM((members, frac_cells), F32)]

    near_a, near_b = near(sent, sent)
    far_c, far_d = far(sent)
    core_in = core(core_msg)
    image, margin_in, column, dots1 = interior(1, v0, halo, f0, f0, core_in)
    own_f, f1, diff, wown, up, down, sent, core_msg, v1 = call(
        functools.partial(finish_kernel, 1),
        "finish_1",
        (place, f0, near_a, near_b, far_c, far_d, core_in, diff, wown, sr, scale_f, unit, table, ghost_table)
        + (halo, weight, ofrac, oy, ox, margin_in, column, image),
        [(own, F32)] + finish_outs,
        scratch=finish_scratch,
        scalars=1,
        aliases={21: 8},
    )
    near_a, near_b = near(up, down)
    far_c, far_d = far(sent)
    core_in = core(core_msg)
    image, margin_in, column, dots2 = interior(2, v1, v0, f1, f0, core_in)
    f2, diff, wown, up, down, sent, core_msg, v2 = call(
        functools.partial(finish_kernel, 2),
        "finish_2",
        (place, f1, near_a, near_b, far_c, far_d, core_in, diff, wown, sr, scale_f, unit, table, ghost_table)
        + (own_f, weight, ofrac, oy, ox, margin_in, column, image),
        finish_outs,
        scratch=finish_scratch,
        scalars=1,
        aliases={21: 7},
    )
    near_a, near_b = near(up, down)
    far_c, far_d = far(sent)
    core_in = core(core_msg)
    (dots3,) = interior(3, v2, v1, f2, f1, core_in)
    peers = count * lax.axis_size("gy")
    (moments,) = call(
        functools.partial(finish_kernel, 3),
        "finish_3",
        (place, f2, near_a, near_b, far_c, far_d, core_in, diff, wown, sr, scale_f, unit, table, ghost_table)
        + (own_f, v2, dots1, dots2, dots3),
        [((peers, 2, LANES), F32)],
        scratch=[pltpu.VMEM((members, LANES), F32)],
        scalars=1,
    )
    totals = lax.all_to_all(moments, ("gx", "gy"), 0, 0)
    return call(
        close_kernel,
        "iterate",
        (place, totals, v0, v1, v2, f0, f1, f2),
        [(field, F32), (own, F32)],
        scratch=[pltpu.VMEM((3, LANES, LANES), F32)],
        scalars=1,
    )


def solution(mesh):
    placed = (
        P("grp", "gx", "gy"),
        P(("grp", "gy"), "gx"),
        P(("grp", "gy"), "gx"),
        P("gx", "gy"),
        P("gx", "gy"),
        P(),
        P("gx", None),
        P("gx", None),
        P("gx", None),
        P("gx"),
        P("gx", "gy", None, None),
        P("gx", "gy", None, None),
        P("gx", "gy", None, None),
        P("gx", "gy", None),
    )
    return jax.shard_map(
        per_device,
        mesh=mesh,
        in_specs=placed,
        out_specs=(P("grp", "gx", "gy"), P(("grp", "gy"), "gx")),
        check_vma=False,
    )
```

time: 80.8 us -> 66.9 us (0.83)
  Pallas kernels: 26 us -> 18.5 us
  waiting for transfers between devices: 13.9 us -> 9.85 us
  starting transfers between devices: 24 us -> 22.5 us
  blocking collectives: 10.8 us -> 9.97 us
    ppermute x4, waiting for transfers between devices: 8.84 us -> 0.01 us  [far(): lax.ppermute(value, 'gx', pairs_of(count, 2, 1))]
    pallas_call x7 -> x10, Pallas kernels: 26 us -> 18.5 us  [call(): pl.pallas_call(kernel, name=name, out_shape=[jax.ShapeDtypeStruct(shape,...]
    ppermute x4, starting transfers between devices: 14.4 us -> 9.11 us  [near(): lax.ppermute(to_b, 'gx', pairs_of(count, 1, 1))]
    ppermute x4, waiting for transfers between devices: 2.67 us -> 7.21 us  [near(): lax.ppermute(to_b, 'gx', pairs_of(count, 1, 1))]
    ppermute x4, starting transfers between devices: 0.23 us -> 2.66 us  [near(): lax.ppermute(to_a, 'gx', pairs_of(count, 1, 0))]
    ppermute x4, waiting for transfers between devices: 0.58 us -> 2.61 us  [near(): lax.ppermute(to_a, 'gx', pairs_of(count, 1, 0))]
    ppermute x4, waiting for transfers between devices: 1.81 us -> 0.01 us  [far(): lax.ppermute(value, 'gx', pairs_of(count, 2, 0))]
    ppermute x4, starting transfers between devices: 1.03 us -> 2.37 us  [far(): lax.ppermute(value, 'gx', pairs_of(count, 2, 0))]
  transfers between devices with their start and end apart: 20 -> 20, of which waited for: 9 -> 7; matrix products, arithmetic and copies ran while one was open for 0% -> 0% of each run, Pallas kernels for 0% -> 14%
where the time goes in v1:
time: 66.9 us; the launch traced here: 66.6 us
  starting transfers between devices  22.5 us (34%)
  Pallas kernels  18.5 us (28%)
  blocking collectives  9.97 us (15%)
  waiting for transfers between devices  9.85 us (15%)
  local copies, waits for them, and re-layouts  3.91 us (6%)
  other arithmetic  0.92 us (1%)
  between operations  0.87 us (1%)
    pallas_call x10, Pallas kernels, call(): pl.pallas_call(kernel, name=name, out_shape=[jax.ShapeDtypeStruct(shape,...  18.5 us
    all_to_all x1, blocking collectives, per_device(): totals = lax.all_to_all(moments, ('gx', 'gy'), 0, 0)  9.97 us
    ppermute x4, starting transfers between devices, near(): lax.ppermute(to_b, 'gx', pairs_of(count, 1, 1))  9.11 us
    ppermute x4, starting transfers between devices, far(): lax.ppermute(value, 'gx', pairs_of(count, 2, 1))  7.9 us
    ppermute x4, waiting for transfers between devices, near(): lax.ppermute(to_b, 'gx', pairs_of(count, 1, 1))  7.21 us
    unnamed x30, local copies, waits for them, and re-layouts  3.82 us
    ppermute x4, starting transfers between devices, near(): lax.ppermute(to_a, 'gx', pairs_of(count, 1, 0))  2.66 us
    ppermute x4, waiting for transfers between devices, near(): lax.ppermute(to_a, 'gx', pairs_of(count, 1, 0))  2.61 us
  transfers between devices with their start and end apart: 20, of which 7 were waited for; matrix products, arithmetic and copies ran while one was open for 0% of the time, Pallas kernels for 14%

profile of v1, /device:TPU:0, one launch (start us, length us, event | category | flops | bytes accessed | tf_op | source)
XLA Modules:
  0.0 66.6 jit_solution(12291882618123694873)
XLA Ops:
  0.6 0.0 copy-start.5
  0.6 0.8 %slice_select_fusion = s32[16,1]{1,0:T(8,128)S(1)} fusion(s32[16,512]{1,0:T(8,128)} %class_ref.1, pred[]{:T(512)S(6)} %eq.24), kind=kLoop, calls=%fused_computation.6 | loop fusion | flops 16 | bytes 193 | tf_op jit(solution)/shard_map/jit(_where)/select_n | solution.py:722
  1.4 0.5 collective-permute-start
  1.9 0.0 copy-start.2
  1.9 0.0 copy-start.4
  2.0 0.6 copy-done.14
  2.6 0.1 compare_bitcast_fusion
  2.6 0.1 stack.31.place_ref
  2.7 0.0 collective-permute-done.col_ref
  2.7 0.0 copy-done.6
  2.8 0.6 copy-done.7
  3.4 1.2 %copy-done = f32[32,16,512]{2,1,0:T(8,128)S(1)} copy-done((f32[32,16,512]{2,1,0:T(8,128)S(1)}, f32[32,16,512]{2,1,0:T(8,128)}, u32[]{:S(2)}) %copy-start) | copy-done | bytes 1048600
  4.6 0.8 %opening.1 = (f32[6,16,512]{2,1,0:T(8,128)S(1)}, bf16[512,256]{1,0:T(8,128)(2,1)S(1)}, f32[16,256]{1,0:T(8,128)S(1)}, bf16[512,128]{1,0:T(8,128)(2,1)S(1)}, f32[...) custom-call(s32[5]{0:T(128)S(1)} %stack.31.place_ref, ...), custom_call_target="tpu_custom_call" | custom-call | tf_op jit(solution)/shard_map/opening/pallas_call | solution.py:659
  5.5 4.7 %collective-permute-start.4 = (f32[16,128]{1,0:T(8,128)S(1)}, f32[16,128]{1,0:T(8,128)S(1)}, u32[]{:S(2)}, u32[]{:S(2)}) collective-permute-start(f32[16,128]{1,0:T(8,128)S(1)} %get-tuple-element.57), channel_id=1, source_target_pairs={{4,8},{8,4},{6,10},{10,6},{12,0},{0,12},{14,2},{2,14},{5,9},{9,5},... | collective-permute-start | bytes 24584 | tf_op jit(solution)/shard_map/ppermute | solution.py:711
  10.1 0.0 collective-permute-start.3
  10.2 1.9 %collective-permute-start.2 = (f32[152,128]{1,0:T(8,128)S(1)}, f32[152,128]{1,0:T(8,128)S(1)}, u32[]{:S(2)}, u32[]{:S(2)}) collective-permute-start(f32[152,128]{1,0:T(8,128)S(1)} %get-tuple-element.108), channel_id=1, source_target_pairs={{2,4},{4,2},{6,8},{8,6},{10,12},{12,10},{14,0},{0,14},{3,5},{5,3},... | collective-permute-start | bytes 233480 | tf_op jit(solution)/shard_map/ppermute | solution.py:705
  12.0 1.7 %collective-permute-start.1 = (f32[152,128]{1,0:T(8,128)S(1)}, f32[152,128]{1,0:T(8,128)S(1)}, u32[]{:S(2)}, u32[]{:S(2)}) collective-permute-start(f32[152,128]{1,0:T(8,128)S(1)} %get-tuple-element.109), channel_id=1, source_target_pairs={{0,2},{2,0},{4,6},{6,4},{8,10},{10,8},{12,14},{14,12},{1,3},{3,1},... | collective-permute-start | bytes 233480 | tf_op jit(solution)/shard_map/ppermute | solution.py:704
  13.7 0.7 %copy-done.10 = s32[4,128]{1,0:T(4,128)S(1)} copy-done((s32[4,128]{1,0:T(4,128)S(1)}, s32[4,128]{1,0:T(4,128)}, u32[]{:S(2)}) %copy-start.10) | copy-done | bytes 2072
  14.4 0.0 copy-done.12
  14.4 1.8 %inside.1 = (bf16[512,512]{1,0:T(8,128)(2,1)S(1)}, bf16[512,512]{1,0:T(8,128)(2,1)S(1)}, bf16[512,640]{1,0:T(8,128)(2,1)S(1)}, bf16[128,512]{1,0:T(8,128)(2,1)S(...) custom-call(s32[5]{0:T(128)S(1)} %stack.31.place_ref, ...), custom_call_target="tpu_custom_call" | custom-call | flops 4000000000 | bytes 12000000 | tf_op jit(solution)/shard_map/inside/pallas_call | solution.py:659
  16.2 0.0 collective-permute-done.4.far_d_ref
  16.2 0.0 collective-permute-done.3.far_c_ref
  16.2 1.3 %collective-permute-done.2.near_b_ref = f32[152,128]{1,0:T(8,128)S(1)} collective-permute-done((f32[152,128]{1,0:T(8,128)S(1)}, f32[152,128]{1,0:T(8,128)S(1)}, u32[]{:S(2)}, u32[]{:S(2)}) %collective-permute-start.2) | collective-permute-done | bytes 77856 | tf_op jit(solution)/shard_map/ppermute | solution.py:705
  17.5 0.6 collective-permute-done.1.near_a_ref
  18.1 0.7 copy-done.9
  18.8 1.9 %first_vector.1 = (f32[6,16,512]{2,1,0:T(8,128)S(1)}, f32[16,512]{1,0:T(8,128)S(1)}, f32[2,128,128]{2,1,0:T(8,128)S(1)}, f32[16,512]{1,0:T(8,128)S(1)}, f32[2,16...) custom-call(s32[5]{0:T(128)S(1)} %stack.31.place_ref, ...), custom_call_target="tpu_custom_call", output_to_operand_aliasing={{9}: (20, {})} | custom-call | tf_op jit(solution)/shard_map/first_vector/pallas_call | solution.py:659
  20.6 0.0 collective-permute-start.9
  20.7 0.6 collective-permute-start.8
  21.3 0.9 %collective-permute-start.7 = (f32[48,128]{1,0:T(8,128)S(1)}, f32[48,128]{1,0:T(8,128)S(1)}, u32[]{:S(2)}, u32[]{:S(2)}) collective-permute-start(f32[48,128]{1,0:T(8,128)S(1)} %get-tuple-element.70), channel_id=1, source_target_pairs={{0,4},{4,0},{2,6},{6,2},{8,12},{12,8},{10,14},{14,10},{1,5},{5,1},... | collective-permute-start | bytes 73736 | tf_op jit(solution)/shard_map/ppermute | solution.py:710
  22.2 2.4 %collective-permute-start.6 = (f32[48,128]{1,0:T(8,128)S(1)}, f32[48,128]{1,0:T(8,128)S(1)}, u32[]{:S(2)}, u32[]{:S(2)}) collective-permute-start(f32[48,128]{1,0:T(8,128)S(1)} %get-tuple-element.70), channel_id=1, source_target_pairs={{2,4},{4,2},{6,8},{8,6},{10,12},{12,10},{14,0},{0,14},{3,5},{5,3},... | collective-permute-start | bytes 73736 | tf_op jit(solution)/shard_map/ppermute | solution.py:705
  24.7 0.1 collective-permute-start.5
  24.8 0.0 collective-permute-done.9.core_ref.core_in_ref
  24.8 2.7 %interior_1.1 = (f32[32,16,512]{2,1,0:T(8,128)S(1)}, f32[32,256]{1,0:T(8,128)S(1)}, f32[16,128]{1,0:T(8,128)S(1)}, f32[8,32]{1,0:T(8,128)S(1)}) custom-call(s32[5]{0:T(128)S(1)} %stack.31.place_ref, f32[32,16,512]{2,1,0:T(8,128)S(1)} %get-tuple-element.78.v_ref.before_ref.v0_ref, f32[2,128,128]{2,1,0:T(8,128)S(1)} %get-tuple-element.77.before_ref.refs_0_, ...), custom_call_target="tpu_custom_call" | custom-call | flops 4000000000 | bytes 12000000 | tf_op jit(solution)/shard_map/interior_1/pallas_call | solution.py:659
  27.5 0.0 collective-permute-done.8.far_d_ref
  27.5 0.0 collective-permute-done.7.far_c_ref
  27.5 1.2 %collective-permute-done.6.near_b_ref = f32[48,128]{1,0:T(8,128)S(1)} collective-permute-done((f32[48,128]{1,0:T(8,128)S(1)}, f32[48,128]{1,0:T(8,128)S(1)}, u32[]{:S(2)}, u32[]{:S(2)}) %collective-permute-start.6) | collective-permute-done | bytes 24608 | tf_op jit(solution)/shard_map/ppermute | solution.py:705
  28.8 0.0 collective-permute-done.5.near_a_ref
  28.8 1.6 %finish_1.1 = (f32[16,512]{1,0:T(8,128)S(1)}, f32[16,512]{1,0:T(8,128)S(1)}, f32[16,512]{1,0:T(8,128)S(1)}, f32[16,512]{1,0:T(8,128)S(1)}, f32[160,128]{1,0:T(8,...) custom-call(s32[5]{0:T(128)S(1)} %stack.31.place_ref, ...), custom_call_target="tpu_custom_call", output_to_operand_aliasing={{8}: (21, {})} | custom-call | tf_op jit(solution)/shard_map/finish_1/pallas_call | solution.py:659
  30.3 1.8 %collective-permute-start.13 = (f32[32,128]{1,0:T(8,128)S(1)}, f32[32,128]{1,0:T(8,128)S(1)}, u32[]{:S(2)}, u32[]{:S(2)}) collective-permute-start(f32[32,128]{1,0:T(8,128)S(1)} %get-tuple-element.85), channel_id=1, source_target_pairs={{4,8},{8,4},{6,10},{10,6},{12,0},{0,12},{14,2},{2,14},{5,9},{9,5},... | collective-permute-start | bytes 49160 | tf_op jit(solution)/shard_map/ppermute | solution.py:711
  32.1 0.6 collective-permute-start.12
  32.8 0.0 collective-permute-start.14
  32.8 2.3 %collective-permute-start.11 = (f32[160,128]{1,0:T(8,128)S(1)}, f32[160,128]{1,0:T(8,128)S(1)}, u32[]{:S(2)}, u32[]{:S(2)}) collective-permute-start(f32[160,128]{1,0:T(8,128)S(1)} %get-tuple-element.106), channel_id=1, source_target_pairs={{2,4},{4,2},{6,8},{8,6},{10,12},{12,10},{14,0},{0,14},{3,5},{5,3},... | collective-permute-start | bytes 245768 | tf_op jit(solution)/shard_map/ppermute | solution.py:705
  35.1 0.6 collective-permute-start.10
  35.7 0.0 collective-permute-done.14.core_ref.core_in_ref
  35.7 2.8 %interior_2.1 = (f32[32,16,512]{2,1,0:T(8,128)S(1)}, f32[32,256]{1,0:T(8,128)S(1)}, f32[16,128]{1,0:T(8,128)S(1)}, f32[8,32]{1,0:T(8,128)S(1)}) custom-call(s32[5]{0:T(128)S(1)} %stack.31.place_ref, f32[32,16,512]{2,1,0:T(8,128)S(1)} %get-tuple-element.90.v_ref.before_ref.v1_ref, f32[32,16,512]{2,1,0:T(8,128)S(1)} %get-tuple-element.78.v_ref.before_ref.v0_ref, ...), custom_call_target="tpu_custom_call" | custom-call | flops 4000000000 | bytes 12000000 | tf_op jit(solution)/shard_map/interior_2/pallas_call | solution.py:659
  38.5 0.0 collective-permute-done.13.far_d_ref
  38.5 0.0 collective-permute-done.12.far_c_ref
  38.5 2.0 %collective-permute-done.11.near_b_ref = f32[160,128]{1,0:T(8,128)S(1)} collective-permute-done((f32[160,128]{1,0:T(8,128)S(1)}, f32[160,128]{1,0:T(8,128)S(1)}, u32[]{:S(2)}, u32[]{:S(2)}) %collective-permute-start.11) | collective-permute-done | bytes 81952 | tf_op jit(solution)/shard_map/ppermute | solution.py:705
  40.5 0.9 %collective-permute-done.10.near_a_ref = f32[160,128]{1,0:T(8,128)S(1)} collective-permute-done((f32[160,128]{1,0:T(8,128)S(1)}, f32[160,128]{1,0:T(8,128)S(1)}, u32[]{:S(2)}, u32[]{:S(2)}) %collective-permute-start.10) | collective-permute-done | bytes 81952 | tf_op jit(solution)/shard_map/ppermute | solution.py:704
  41.4 1.5 %finish_2.1 = (f32[16,512]{1,0:T(8,128)S(1)}, f32[16,512]{1,0:T(8,128)S(1)}, f32[16,512]{1,0:T(8,128)S(1)}, f32[160,128]{1,0:T(8,128)S(1)}, f32[160,128]{1,0:T(8...) custom-call(s32[5]{0:T(128)S(1)} %stack.31.place_ref, ...), custom_call_target="tpu_custom_call", output_to_operand_aliasing={{7}: (21, {})} | custom-call | tf_op jit(solution)/shard_map/finish_2/pallas_call | solution.py:659
  42.9 0.8 %collective-permute-start.18 = (f32[32,128]{1,0:T(8,128)S(1)}, f32[32,128]{1,0:T(8,128)S(1)}, u32[]{:S(2)}, u32[]{:S(2)}) collective-permute-start(f32[32,128]{1,0:T(8,128)S(1)} %get-tuple-element.97), channel_id=1, source_target_pairs={{4,8},{8,4},{6,10},{10,6},{12,0},{0,12},{14,2},{2,14},{5,9},{9,5},... | collective-permute-start | bytes 49160 | tf_op jit(solution)/shard_map/ppermute | solution.py:711
  43.6 0.8 %collective-permute-start.17 = (f32[32,128]{1,0:T(8,128)S(1)}, f32[32,128]{1,0:T(8,128)S(1)}, u32[]{:S(2)}, u32[]{:S(2)}) collective-permute-start(f32[32,128]{1,0:T(8,128)S(1)} %get-tuple-element.97), channel_id=1, source_target_pairs={{0,4},{4,0},{2,6},{6,2},{8,12},{12,8},{10,14},{14,10},{1,5},{5,1},... | collective-permute-start | bytes 49160 | tf_op jit(solution)/shard_map/ppermute | solution.py:710
  44.5 0.0 collective-permute-start.19
  44.5 2.5 %collective-permute-start.16 = (f32[160,128]{1,0:T(8,128)S(1)}, f32[160,128]{1,0:T(8,128)S(1)}, u32[]{:S(2)}, u32[]{:S(2)}) collective-permute-start(f32[160,128]{1,0:T(8,128)S(1)} %get-tuple-element.104), channel_id=1, source_target_pairs={{2,4},{4,2},{6,8},{8,6},{10,12},{12,10},{14,0},{0,14},{3,5},{5,3},... | collective-permute-start | bytes 245768 | tf_op jit(solution)/shard_map/ppermute | solution.py:705
  47.0 0.2 collective-permute-start.15
  47.2 0.0 collective-permute-done.19.core_ref.core_in_ref
  47.2 2.2 %interior_3.1.refs_4_ = f32[8,32]{1,0:T(8,128)S(1)} custom-call(s32[5]{0:T(128)S(1)} %stack.31.place_ref, f32[32,16,512]{2,1,0:T(8,128)S(1)} %get-tuple-element.101.v_ref.refs_1_.v2_ref, f32[32,16,512]{2,1,0:T(8,128)S(1)} %get-tuple-element.90.v_ref.before_ref.v1_ref, f32[16,512]{1,0:T(8,128)S(1)} %get-tuple-element.94.vf_ref.f2_ref, ...), custom_call_target="tpu_custom_call" | custom-call | flops 4000000000 | bytes 12000000 | tf_op jit(solution)/shard_map/interior_3/pallas_call | solution.py:659
  49.4 0.0 collective-permute-done.18.far_d_ref
  49.5 0.0 collective-permute-done.17.far_c_ref
  49.5 2.8 %collective-permute-done.16.near_b_ref = f32[160,128]{1,0:T(8,128)S(1)} collective-permute-done((f32[160,128]{1,0:T(8,128)S(1)}, f32[160,128]{1,0:T(8,128)S(1)}, u32[]{:S(2)}, u32[]{:S(2)}) %collective-permute-start.16) | collective-permute-done | bytes 81952 | tf_op jit(solution)/shard_map/ppermute | solution.py:705
  52.2 1.1 %collective-permute-done.15.near_a_ref = f32[160,128]{1,0:T(8,128)S(1)} collective-permute-done((f32[160,128]{1,0:T(8,128)S(1)}, f32[160,128]{1,0:T(8,128)S(1)}, u32[]{:S(2)}, u32[]{:S(2)}) %collective-permute-start.15) | collective-permute-done | bytes 81952 | tf_op jit(solution)/shard_map/ppermute | solution.py:704
  53.3 1.1 %finish_3.1 = f32[16,2,128]{2,1,0:T(2,128)S(1)} custom-call(s32[5]{0:T(128)S(1)} %stack.31.place_ref, f32[16,512]{1,0:T(8,128)S(1)} %get-tuple-element.94.vf_ref.f2_ref, f32[160,128]{1,0:T(8,128)S(1)} %collective-permute-done.15.near_a_ref, f32[160,128]{1,0:T(8,128)S(1)} %collective-permute-done.16.near_b_ref, ...), custom_call_target="tpu_custom_call" | custom-call | tf_op jit(solution)/shard_map/finish_3/pallas_call | solution.py:659
  54.5 10.0 %all_to_all.5.totals_ref = f32[16,2,128]{2,1,0:T(2,128)S(1)} all-to-all(f32[16,2,128]{2,1,0:T(2,128)S(1)} %finish_3.1), channel_id=1, replica_groups=mesh['grp'=2,'gx'=8,'gy'=2] {'gx','gy'}, dimensions={0} | all-to-all | bytes 32768 | tf_op jit(solution)/shard_map/all_to_all | solution.py:898
  64.4 2.2 %iterate.1 = (f32[32,16,512]{2,1,0:T(8,128)}, f32[16,512]{1,0:T(8,128)}) custom-call(s32[5]{0:T(128)S(1)} %stack.31.place_ref, f32[16,2,128]{2,1,0:T(2,128)S(1)} %all_to_all.5.totals_ref, f32[32,16,512]{2,1,0:T(8,128)S(1)} %get-tuple-element.78.v_ref.before_ref.v0_ref, f32[32,16,512]{2,1,0:T(8,128)S(1)} %get-tuple-element.90.v_ref.before_ref.v1_ref, ...), custom_call_target="tpu_custom_call" | custom-call | tf_op jit(solution)/shard_map/iterate/pallas_call | solution.py:659
  (24 shorter events, 0.1 us)
Async XLA Ops:
  0.6 2.1 %copy-start.5 = (f32[16,512]{1,0:T(8,128)S(1)}, f32[16,512]{1,0:T(8,128)}, u32[]{:S(2)}) copy-start(f32[16,512]{1,0:T(8,128)} %aperture_ref.1) | copy-start | bytes 98308
  1.4 1.3 %collective-permute-start = (s32[16,1]{1,0:T(8,128)S(1)}, s32[16,1]{1,0:T(8,128)S(1)}, u32[]{:S(2)}, u32[]{:S(2)}) collective-permute-start(s32[16,1]{1,0:T(8,128)S(1)} %slice_select_fusion), channel_id=1, source_target_pairs={{0,1},{1,0},{2,3},{3,2},{4,5},{5,4},{6,7},{7,6},{8,9},{9,8},{10,11... | collective-permute-start | bytes 200 | tf_op jit(solution)/shard_map/ppermute | solution.py:715
  1.9 0.7 %copy-start.13 = (f32[1,1,2,128]{3,2,1,0:T(2,128)S(1)}, f32[1,1,2,128]{3,2,1,0:T(2,128)}, u32[]{:S(2)}) copy-start(f32[1,1,2,128]{3,2,1,0:T(2,128)} %param.26) | copy-start | bytes 3076
  1.9 0.7 %copy-start.14 = (s32[1,1,2]{2,1,0:T(1,128)S(1)}, s32[1,1,2]{2,1,0:T(1,128)}, u32[]{:S(2)}) copy-start(s32[1,1,2]{2,1,0:T(1,128)} %param.27) | copy-start | bytes 28
  1.9 0.8 %copy-start.6 = (s32[1,1,2,128]{3,2,1,0:T(2,128)S(1)}, s32[1,1,2,128]{3,2,1,0:T(2,128)}, u32[]{:S(2)}) copy-start(s32[1,1,2,128]{3,2,1,0:T(2,128)} %param.24) | copy-start | bytes 3076
  1.9 0.9 %copy-start.8 = (s32[1,128]{1,0:T(1,128)S(1)}, s32[1,128]{1,0:T(1,128)}, u32[]{:S(2)}) copy-start(s32[1,128]{1,0:T(1,128)} %slots_ref.1) | copy-start | bytes 1540
  1.9 0.9 %copy-start.2 = (s32[16,512]{1,0:T(8,128)S(1)}, s32[16,512]{1,0:T(8,128)}, u32[]{:S(2)}) copy-start(s32[16,512]{1,0:T(8,128)} %class_ref.1) | copy-start | bytes 98308
  1.9 0.9 %copy-start.4 = (f32[16,512]{1,0:T(8,128)S(1)}, f32[16,512]{1,0:T(8,128)}, u32[]{:S(2)}) copy-start(f32[16,512]{1,0:T(8,128)} %storage_ref.1) | copy-start | bytes 98308
  2.7 0.7 copy-start.7
  3.4 1.2 %copy-start = (f32[32,16,512]{2,1,0:T(8,128)S(1)}, f32[32,16,512]{2,1,0:T(8,128)}, u32[]{:S(2)}) copy-start(f32[32,16,512]{2,1,0:T(8,128)} %source_ref.5) | copy-start | bytes 3145732
  4.6 9.1 %copy-start.1 = (f32[32,16,512]{2,1,0:T(8,128)S(1)}, f32[32,16,512]{2,1,0:T(8,128)}, u32[]{:S(2)}) copy-start(f32[32,16,512]{2,1,0:T(8,128)} %source_ref.5) | copy-start | bytes 3145732
  5.5 10.8 %collective-permute-start.4 = (f32[16,128]{1,0:T(8,128)S(1)}, f32[16,128]{1,0:T(8,128)S(1)}, u32[]{:S(2)}, u32[]{:S(2)}) collective-permute-start(f32[16,128]{1,0:T(8,128)S(1)} %get-tuple-element.57), channel_id=1, source_target_pairs={{4,8},{8,4},{6,10},{10,6},{12,0},{0,12},{14,2},{2,14},{5,9},{9,5},... | collective-permute-start | bytes 24584 | tf_op jit(solution)/shard_map/ppermute | solution.py:711
  10.1 6.1 %collective-permute-start.3 = (f32[16,128]{1,0:T(8,128)S(1)}, f32[16,128]{1,0:T(8,128)S(1)}, u32[]{:S(2)}, u32[]{:S(2)}) collective-permute-start(f32[16,128]{1,0:T(8,128)S(1)} %get-tuple-element.57), channel_id=1, source_target_pairs={{0,4},{4,0},{2,6},{6,2},{8,12},{12,8},{10,14},{14,10},{1,5},{5,1},... | collective-permute-start | bytes 24584 | tf_op jit(solution)/shard_map/ppermute | solution.py:710
  10.1 3.6 %copy-start.11 = (s32[4,128]{1,0:T(4,128)S(1)}, s32[4,128]{1,0:T(4,128)}, u32[]{:S(2)}) copy-start(s32[4,128]{1,0:T(4,128)} %param.22) | copy-start | bytes 6148
  10.2 7.3 %collective-permute-start.2 = (f32[152,128]{1,0:T(8,128)S(1)}, f32[152,128]{1,0:T(8,128)S(1)}, u32[]{:S(2)}, u32[]{:S(2)}) collective-permute-start(f32[152,128]{1,0:T(8,128)S(1)} %get-tuple-element.108), channel_id=1, source_target_pairs={{2,4},{4,2},{6,8},{8,6},{10,12},{12,10},{14,0},{0,14},{3,5},{5,3},... | collective-permute-start | bytes 233480 | tf_op jit(solution)/shard_map/ppermute | solution.py:705
  12.0 6.1 %collective-permute-start.1 = (f32[152,128]{1,0:T(8,128)S(1)}, f32[152,128]{1,0:T(8,128)S(1)}, u32[]{:S(2)}, u32[]{:S(2)}) collective-permute-start(f32[152,128]{1,0:T(8,128)S(1)} %get-tuple-element.109), channel_id=1, source_target_pairs={{0,2},{2,0},{4,6},{6,4},{8,10},{10,8},{12,14},{14,12},{1,3},{3,1},... | collective-permute-start | bytes 233480 | tf_op jit(solution)/shard_map/ppermute | solution.py:704
  13.7 0.7 %copy-start.10 = (s32[4,128]{1,0:T(4,128)S(1)}, s32[4,128]{1,0:T(4,128)}, u32[]{:S(2)}) copy-start(s32[4,128]{1,0:T(4,128)} %param.21) | copy-start | bytes 6148
  13.7 0.7 %copy-start.12 = (s32[1,1,2,128]{3,2,1,0:T(2,128)S(1)}, s32[1,1,2,128]{3,2,1,0:T(2,128)}, u32[]{:S(2)}) copy-start(s32[1,1,2,128]{3,2,1,0:T(2,128)} %param.25) | copy-start | bytes 3076
  14.4 3.7 %copy-start.3 = (f32[16,512]{1,0:T(8,128)S(1)}, f32[16,512]{1,0:T(8,128)}, u32[]{:S(2)}) copy-start(f32[16,512]{1,0:T(8,128)} %source_f_ref.1) | copy-start | bytes 98308
  18.1 0.7 copy-start.9
  20.6 4.2 %collective-permute-start.9 = (f32[176,128]{1,0:T(8,128)S(1)}, f32[176,128]{1,0:T(8,128)S(1)}, u32[]{:S(2)}, u32[]{:S(2)}) collective-permute-start(f32[176,128]{1,0:T(8,128)S(1)} %get-tuple-element.71), channel_id=1, source_target_pairs={{0,1},{1,0},{2,3},{3,2},{4,5},{5,4},{6,7},{7,6},{8,9},{9,8},{10,11... | collective-permute-start | bytes 270344 | tf_op jit(solution)/shard_map/ppermute | solution.py:715
  20.7 6.9 %collective-permute-start.8 = (f32[48,128]{1,0:T(8,128)S(1)}, f32[48,128]{1,0:T(8,128)S(1)}, u32[]{:S(2)}, u32[]{:S(2)}) collective-permute-start(f32[48,128]{1,0:T(8,128)S(1)} %get-tuple-element.70), channel_id=1, source_target_pairs={{4,8},{8,4},{6,10},{10,6},{12,0},{0,12},{14,2},{2,14},{5,9},{9,5},... | collective-permute-start | bytes 73736 | tf_op jit(solution)/shard_map/ppermute | solution.py:711
  21.3 6.2 %collective-permute-start.7 = (f32[48,128]{1,0:T(8,128)S(1)}, f32[48,128]{1,0:T(8,128)S(1)}, u32[]{:S(2)}, u32[]{:S(2)}) collective-permute-start(f32[48,128]{1,0:T(8,128)S(1)} %get-tuple-element.70), channel_id=1, source_target_pairs={{0,4},{4,0},{2,6},{6,2},{8,12},{12,8},{10,14},{14,10},{1,5},{5,1},... | collective-permute-start | bytes 73736 | tf_op jit(solution)/shard_map/ppermute | solution.py:710
  22.2 6.5 %collective-permute-start.6 = (f32[48,128]{1,0:T(8,128)S(1)}, f32[48,128]{1,0:T(8,128)S(1)}, u32[]{:S(2)}, u32[]{:S(2)}) collective-permute-start(f32[48,128]{1,0:T(8,128)S(1)} %get-tuple-element.70), channel_id=1, source_target_pairs={{2,4},{4,2},{6,8},{8,6},{10,12},{12,10},{14,0},{0,14},{3,5},{5,3},... | collective-permute-start | bytes 73736 | tf_op jit(solution)/shard_map/ppermute | solution.py:705
  24.7 4.1 %collective-permute-start.5 = (f32[48,128]{1,0:T(8,128)S(1)}, f32[48,128]{1,0:T(8,128)S(1)}, u32[]{:S(2)}, u32[]{:S(2)}) collective-permute-start(f32[48,128]{1,0:T(8,128)S(1)} %get-tuple-element.70), channel_id=1, source_target_pairs={{0,2},{2,0},{4,6},{6,4},{8,10},{10,8},{12,14},{14,12},{1,3},{3,1},... | collective-permute-start | bytes 73736 | tf_op jit(solution)/shard_map/ppermute | solution.py:704
  30.3 8.2 %collective-permute-start.13 = (f32[32,128]{1,0:T(8,128)S(1)}, f32[32,128]{1,0:T(8,128)S(1)}, u32[]{:S(2)}, u32[]{:S(2)}) collective-permute-start(f32[32,128]{1,0:T(8,128)S(1)} %get-tuple-element.85), channel_id=1, source_target_pairs={{4,8},{8,4},{6,10},{10,6},{12,0},{0,12},{14,2},{2,14},{5,9},{9,5},... | collective-permute-start | bytes 49160 | tf_op jit(solution)/shard_map/ppermute | solution.py:711
  32.1 6.4 %collective-permute-start.12 = (f32[32,128]{1,0:T(8,128)S(1)}, f32[32,128]{1,0:T(8,128)S(1)}, u32[]{:S(2)}, u32[]{:S(2)}) collective-permute-start(f32[32,128]{1,0:T(8,128)S(1)} %get-tuple-element.85), channel_id=1, source_target_pairs={{0,4},{4,0},{2,6},{6,2},{8,12},{12,8},{10,14},{14,10},{1,5},{5,1},... | collective-permute-start | bytes 49160 | tf_op jit(solution)/shard_map/ppermute | solution.py:710
  32.8 3.0 %collective-permute-start.14 = (f32[144,128]{1,0:T(8,128)S(1)}, f32[144,128]{1,0:T(8,128)S(1)}, u32[]{:S(2)}, u32[]{:S(2)}) collective-permute-start(f32[144,128]{1,0:T(8,128)S(1)} %get-tuple-element.86), channel_id=1, source_target_pairs={{0,1},{1,0},{2,3},{3,2},{4,5},{5,4},{6,7},{7,6},{8,9},{9,8},{10,11... | collective-permute-start | bytes 221192 | tf_op jit(solution)/shard_map/ppermute | solution.py:715
  32.8 7.7 %collective-permute-start.11 = (f32[160,128]{1,0:T(8,128)S(1)}, f32[160,128]{1,0:T(8,128)S(1)}, u32[]{:S(2)}, u32[]{:S(2)}) collective-permute-start(f32[160,128]{1,0:T(8,128)S(1)} %get-tuple-element.106), channel_id=1, source_target_pairs={{2,4},{4,2},{6,8},{8,6},{10,12},{12,10},{14,0},{0,14},{3,5},{5,3},... | collective-permute-start | bytes 245768 | tf_op jit(solution)/shard_map/ppermute | solution.py:705
  35.1 6.3 %collective-permute-start.10 = (f32[160,128]{1,0:T(8,128)S(1)}, f32[160,128]{1,0:T(8,128)S(1)}, u32[]{:S(2)}, u32[]{:S(2)}) collective-permute-start(f32[160,128]{1,0:T(8,128)S(1)} %get-tuple-element.107), channel_id=1, source_target_pairs={{0,2},{2,0},{4,6},{6,4},{8,10},{10,8},{12,14},{14,12},{1,3},{3,1},... | collective-permute-start | bytes 245768 | tf_op jit(solution)/shard_map/ppermute | solution.py:704
  42.9 6.6 %collective-permute-start.18 = (f32[32,128]{1,0:T(8,128)S(1)}, f32[32,128]{1,0:T(8,128)S(1)}, u32[]{:S(2)}, u32[]{:S(2)}) collective-permute-start(f32[32,128]{1,0:T(8,128)S(1)} %get-tuple-element.97), channel_id=1, source_target_pairs={{4,8},{8,4},{6,10},{10,6},{12,0},{0,12},{14,2},{2,14},{5,9},{9,5},... | collective-permute-start | bytes 49160 | tf_op jit(solution)/shard_map/ppermute | solution.py:711
  43.6 5.8 %collective-permute-start.17 = (f32[32,128]{1,0:T(8,128)S(1)}, f32[32,128]{1,0:T(8,128)S(1)}, u32[]{:S(2)}, u32[]{:S(2)}) collective-permute-start(f32[32,128]{1,0:T(8,128)S(1)} %get-tuple-element.97), channel_id=1, source_target_pairs={{0,4},{4,0},{2,6},{6,2},{8,12},{12,8},{10,14},{14,10},{1,5},{5,1},... | collective-permute-start | bytes 49160 | tf_op jit(solution)/shard_map/ppermute | solution.py:710
  44.5 2.7 %collective-permute-start.19 = (f32[144,128]{1,0:T(8,128)S(1)}, f32[144,128]{1,0:T(8,128)S(1)}, u32[]{:S(2)}, u32[]{:S(2)}) collective-permute-start(f32[144,128]{1,0:T(8,128)S(1)} %get-tuple-element.98), channel_id=1, source_target_pairs={{0,1},{1,0},{2,3},{3,2},{4,5},{5,4},{6,7},{7,6},{8,9},{9,8},{10,11... | collective-permute-start | bytes 221192 | tf_op jit(solution)/shard_map/ppermute | solution.py:715
  44.5 7.7 %collective-permute-start.16 = (f32[160,128]{1,0:T(8,128)S(1)}, f32[160,128]{1,0:T(8,128)S(1)}, u32[]{:S(2)}, u32[]{:S(2)}) collective-permute-start(f32[160,128]{1,0:T(8,128)S(1)} %get-tuple-element.104), channel_id=1, source_target_pairs={{2,4},{4,2},{6,8},{8,6},{10,12},{12,10},{14,0},{0,14},{3,5},{5,3},... | collective-permute-start | bytes 245768 | tf_op jit(solution)/shard_map/ppermute | solution.py:705
  47.0 6.3 %collective-permute-start.15 = (f32[160,128]{1,0:T(8,128)S(1)}, f32[160,128]{1,0:T(8,128)S(1)}, u32[]{:S(2)}, u32[]{:S(2)}) collective-permute-start(f32[160,128]{1,0:T(8,128)S(1)} %get-tuple-element.105), channel_id=1, source_target_pairs={{0,2},{2,0},{4,6},{6,4},{8,10},{10,8},{12,14},{14,12},{1,3},{3,1},... | collective-permute-start | bytes 245768 | tf_op jit(solution)/shard_map/ppermute | solution.py:704

commit v2 on v1

--- a/solution.py
+++ b/solution.py
@@ -27,6 +27,18 @@
     dims = (((1,), (1 if transposed else 0,)), ((), ()))
     out = lax.dot_general(split3(x), table, dims, preferred_element_type=F32)
     return out[:rows] + out[rows : 2 * rows] + out[2 * rows :]
+
+
+class Place:
+    def __init__(self):
+        count = lax.axis_size("gx")
+        i = lax.axis_index("gx")
+        self.j = lax.axis_index("gy")
+        self.high_side = self.j == 0
+        self.even = lax.rem(i, 2) == 0
+        self.low_pair = lax.rem(lax.div(i, 2), 2) == 0
+        self.first = i == 0
+        self.last = i == count - 1
 
 
 def harmonic(first_perm, second_perm):
@@ -74,64 +86,27 @@
 
 
 def opening_kernel(
-    place_ref,
     perm_table_ref,
     class_ref,
-    col_ref,
-    storage_ref,
-    source_ref,
     aperture_ref,
     slots_ref,
-    cell_ref,
-    weight_ref,
-    coef_ref,
-    oy_ref,
-    ox_ref,
+    perm_ref,
+    cond_ref,
     oslot_ref,
-    cond_ref,
-    up_ref,
-    down_ref,
+    near_a_ref,
+    near_b_ref,
     far_ref,
+    border_ref,
 ):
     x_cells, y_cells = class_ref.shape
-    members = source_ref.shape[0]
     half = aperture_ref.shape[0]
-    high_side = place_ref[2] == 0
-
-    def perm_of(classes):
-        perm = jnp.zeros(classes.shape, F32)
-        for index in range(perm_table_ref.shape[0]):
-            perm = jnp.where(classes == index, perm_table_ref[index], perm)
-        return perm
-
-    perm = perm_of(class_ref[...])
-    col = perm_of(col_ref[...])
-    lane = lax.broadcasted_iota(jnp.int32, perm.shape, 1)
-    row = lax.broadcasted_iota(jnp.int32, perm.shape, 0)
-    north = jnp.concatenate([perm[:, 1:], col], axis=1)
-    south = jnp.concatenate([col, perm[:, :-1]], axis=1)
-    tn = jnp.where((lane == y_cells - 1) & jnp.logical_not(high_side), 0.0, harmonic(perm, north))
-    ts = jnp.where((lane == 0) & high_side, 0.0, harmonic(perm, south))
-    east = jnp.concatenate([perm[1:], perm[:1]], axis=0)
-    west = jnp.concatenate([perm[-1:], perm[:-1]], axis=0)
-    te = jnp.where(row == x_cells - 1, 0.0, harmonic(perm, east))
-    tw = jnp.where(row == 0, 0.0, harmonic(perm, west))
-
-    cell = cell_ref[...]
-    oy = one_hot(cell % y_cells, y_cells)
-    oy_ref[...] = oy
-    shape_x = (x_cells, cell.shape[1])
-    at_x = lax.broadcasted_iota(jnp.int32, shape_x, 0) == cell // y_cells
-    ox_ref[...] = jnp.where(at_x, 1.0, 0.0)
-    wsum = pick(jnp.where(at_x, weight_ref[...], 0.0), oy, True)
-
-    part = storage_ref[...] + te + tw + tn + ts + wsum
-    coef_ref[0] = te
-    coef_ref[1] = tw
-    coef_ref[2] = tn
-    coef_ref[3] = ts
-    coef_ref[4] = part
-    coef_ref[5] = perm
+    here = Place()
+    classes = class_ref[...]
+    perm = jnp.zeros(classes.shape, F32)
+    for index in range(perm_table_ref.shape[0]):
+        perm = jnp.where(classes == index, perm_table_ref[index], perm)
+    perm_ref[...] = perm
+    border_ref[...] = jnp.where(here.high_side, perm[:, y_cells - LANES :], perm[:, :LANES])
 
     aperture = aperture_ref[...]
     cond = aperture * aperture * aperture
@@ -140,32 +115,24 @@
     oslot_ref[...] = oslot
     supplied = pick(cond, oslot)
     far_ref[...] = supplied
-    blocks = y_cells // LANES
-    for ref, at in ((up_ref, x_cells - 1), (down_ref, 0)):
-        edge = source_ref[:, at, :]
-        ref[0 : blocks * members, :] = to_blocks(edge)
-        ref[blocks * members : blocks * members + blocks, :] = to_blocks(perm[at : at + 1])
-        ref[blocks * members + blocks : blocks * members + 2 * blocks, :] = to_blocks(part[at : at + 1])
-        ref[blocks * members + 2 * blocks : blocks * members + 2 * blocks + half, :] = supplied
-
-
-def neighbours(place_ref, near_a_ref, near_b_ref, far_c_ref, far_d_ref):
+    up, down = to_blocks(perm[x_cells - 1 :]), to_blocks(perm[:1])
+    blocks = up.shape[0]
+    pad = jnp.zeros((near_a_ref.shape[0] - half - blocks, LANES), F32)
+    for ref, edge in ((near_a_ref, jnp.where(here.even, up, down)), (near_b_ref, jnp.where(here.even, down, up))):
+        ref[...] = jnp.concatenate([supplied, edge, pad], axis=0)
+
+
+def neighbours(here, near_a_ref, near_b_ref, far_c_ref, far_d_ref):
     def reader(flag, at_zero, at_one):
         return lambda at, size: jnp.where(
-            place_ref[flag] == 0, at_zero[at : at + size, :], at_one[at : at + size, :]
+            flag, at_zero[at : at + size, :], at_one[at : at + size, :]
         )
 
     return (
-        reader(0, near_a_ref, near_b_ref),
-        reader(0, near_b_ref, near_a_ref),
-        reader(1, far_c_ref, far_d_ref),
-        reader(1, far_d_ref, far_c_ref),
-    )
-
-
-def spread(x, members):
-    return jnp.concatenate(
-        [jnp.broadcast_to(x[:, q : q + LANES], (members, LANES)) for q in range(0, x.shape[1], LANES)], axis=0
+        reader(here.even, near_a_ref, near_b_ref),
+        reader(here.even, near_b_ref, near_a_ref),
+        reader(here.low_pair, far_c_ref, far_d_ref),
+        reader(here.low_pair, far_d_ref, far_c_ref),
     )
 
 
@@ -220,15 +187,21 @@
 
 
 def inside_kernel(
-    place_ref,
-    coef_ref,
+    ov_count_ref,
+    perm_ref,
+    border_ref,
+    storage_ref,
     source_ref,
+    cell_ref,
+    ov_weight_ref,
     local_ref,
-    other_ref,
+    other_in_ref,
     frac_ref,
     oslot_ref,
+    coef_ref,
     oy_ref,
     ox_ref,
+    weight_ref,
     first_ref,
     second_ref,
     table_ref,
@@ -240,20 +213,56 @@
 ):
     members, x_cells, y_cells = source_ref.shape
     frac_cells = table_ref.shape[0]
-    rows = local_ref.shape[1]
-    other = other_ref[...]
-    first, second = one_hot(local_ref[...], frac_cells), one_hot(other, frac_cells)
+    here = Place()
+    high_side = here.high_side
+
+    def line(ref):
+        return jnp.concatenate([ref[k : k + 1, :] for k in range(ref.shape[0])], axis=1)
+
+    rows = local_ref.size
+    perm, border = perm_ref[...], border_ref[...]
+    col = jnp.where(high_side, border[:, :1], border[:, LANES - 1 :])
+    lane = lax.broadcasted_iota(jnp.int32, perm.shape, 1)
+    row = lax.broadcasted_iota(jnp.int32, perm.shape, 0)
+    north = jnp.concatenate([perm[:, 1:], col], axis=1)
+    south = jnp.concatenate([col, perm[:, :-1]], axis=1)
+    tn = jnp.where((lane == y_cells - 1) & jnp.logical_not(high_side), 0.0, harmonic(perm, north))
+    ts = jnp.where((lane == 0) & high_side, 0.0, harmonic(perm, south))
+    east = jnp.concatenate([perm[1:], perm[:1]], axis=0)
+    west = jnp.concatenate([perm[-1:], perm[:-1]], axis=0)
+    te = jnp.where(row == x_cells - 1, 0.0, harmonic(perm, east))
+    tw = jnp.where(row == 0, 0.0, harmonic(perm, west))
+    cell = line(cell_ref)
+    oy = one_hot(cell % y_cells, y_cells)
+    oy_ref[...] = oy
+    row_x = lax.broadcasted_iota(jnp.int32, ox_ref.shape, 0)
+    at_x = row_x == cell // y_cells
+    ox = jnp.where(at_x, 1.0, 0.0)
+    ox_ref[...] = ox
+    lane_w = lax.broadcasted_iota(jnp.int32, (1, LANES), 1)
+    weight = jnp.concatenate(
+        [jnp.where(lane_w < ov_count_ref[k], ov_weight_ref[k : k + 1, :], 0.0) for k in range(ov_weight_ref.shape[0])],
+        axis=1,
+    )
+    weight_ref[...] = weight
+    part = storage_ref[...] + te + tw + tn + ts + pick(jnp.where(at_x, weight, 0.0), oy, True)
+    coef_ref[0] = te
+    coef_ref[1] = tw
+    coef_ref[2] = tn
+    coef_ref[3] = ts
+    coef_ref[4] = part
+
+    other = line(other_in_ref)
+    first, second = one_hot(line(local_ref), frac_cells), one_hot(other, frac_cells)
     first_ref[...] = first
     second_ref[...] = second
     table_ref[:, :rows] = first - second
     table_ref[:, rows:] = oslot_ref[...]
     ghost_table_ref[...] = one_hot(other - frac_cells, ghost_table_ref.shape[0])
-    ofrac_ref[...] = one_hot(frac_ref[...], frac_cells)
-
-    high_side = place_ref[2] == 0
-    inverse = 1.0 / coef_ref[4]
-    row_x = lax.broadcasted_iota(jnp.int32, ox_ref.shape, 0)
-    inner_x = jnp.where((row_x == 0) | (row_x == x_cells - 1), 0.0, ox_ref[...])
+    ofrac_ref[...] = one_hot(line(frac_ref), frac_cells)
+
+    inverse = 1.0 / part
+    inner_x = jnp.where((row_x == 0) | (row_x == x_cells - 1), 0.0, ox)
     lane_c = lax.broadcasted_iota(jnp.int32, (x_cells, LANES), 1)
     column_ref[...] = jnp.zeros_like(column_ref)
 
@@ -273,9 +282,9 @@
 
 
 def first_kernel(
-    place_ref,
     count_ref,
     coef_ref,
+    perm_ref,
     cond_ref,
     source_ref,
     source_f_ref,
@@ -296,11 +305,12 @@
     v_in_ref,
     unit_ref,
     vf_ref,
-    halo_ref,
     sr_ref,
     scale_f_ref,
     diff_ref,
     wown_ref,
+    to_a_ref,
+    to_b_ref,
     sent_ref,
     core_ref,
     v_ref,
@@ -309,13 +319,12 @@
     members, x_cells, y_cells = source_ref.shape
     half, frac_cells = source_f_ref.shape
     blocks = y_cells // LANES
-    j = place_ref[2]
-    high_side = j == 0
+    here = Place()
+    j, high_side = here.j, here.high_side
     base = blocks * members
-    plus1, minus1, plus2, minus2 = neighbours(place_ref, near_a_ref, near_b_ref, far_c_ref, far_d_ref)
-
-    slot_at = base + 2 * blocks
-    ghosts = by_group(minus1(slot_at, half), plus1(slot_at, half), minus2(0, half), plus2(0, half))
+    plus1, minus1, plus2, minus2 = neighbours(here, near_a_ref, near_b_ref, far_c_ref, far_d_ref)
+
+    ghosts = by_group(minus1(0, half), plus1(0, half), minus2(0, half), plus2(0, half))
     table, ghost_table = table_ref[...], ghost_table_ref[...]
     cond = cond_ref[...]
     cond_first = pick(cond, first_ref[...])
@@ -333,17 +342,18 @@
     scale_f_ref[1] = diag_f
     vf = source_f_ref[...] * inverse_f
     vf_ref[...] = vf
-    send_network(vf, sr, table, ghost_table, diff_ref, [(sent_ref, 0)])
-    sent_ref[2 * half : 3 * half, :] = pick(sr, ghost_table, True)
-
-    perm, part = coef_ref[5], coef_ref[4]
+    refs = [(to_a_ref, base), (to_b_ref, base), (sent_ref, 0)]
+    send_network(vf, sr, table, ghost_table, diff_ref, refs)
+    slot_sums = pick(sr, ghost_table, True)
+    for ref, at in refs:
+        ref[at + 2 * half : at + 3 * half, :] = slot_sums
+
+    perm, part = perm_ref[...], coef_ref[4]
     row = lax.broadcasted_iota(jnp.int32, perm.shape, 0)
-    perm_plus = from_blocks(plus1(base, blocks), 1)
-    perm_minus = from_blocks(minus1(base, blocks), 1)
-    part_plus = from_blocks(plus1(base + blocks, blocks), 1)
-    part_minus = from_blocks(minus1(base + blocks, blocks), 1)
-    te_edge = jnp.where(place_ref[4] == 1, 0.0, harmonic(perm[x_cells - 1 :], perm_plus))
-    tw_edge = jnp.where(place_ref[3] == 1, 0.0, harmonic(perm[:1], perm_minus))
+    perm_plus = from_blocks(plus1(half, blocks), 1)
+    perm_minus = from_blocks(minus1(half, blocks), 1)
+    te_edge = jnp.where(here.last, 0.0, harmonic(perm[x_cells - 1 :], perm_plus))
+    tw_edge = jnp.where(here.first, 0.0, harmonic(perm[:1], perm_minus))
     te = jnp.where(row == x_cells - 1, te_edge, coef_ref[0])
     tw = jnp.where(row == 0, tw_edge, coef_ref[1])
     diag = part + jnp.where(row == x_cells - 1, te_edge, 0.0) + jnp.where(row == 0, tw_edge, 0.0)
@@ -354,12 +364,12 @@
     unit_ref[3] = coef_ref[3] * inverse
     unit_ref[4] = inverse
     unit_ref[5] = diag
-    halo_ref[0] = plus1(0, base) * spread(1.0 / (part_plus + te_edge), members)
-    halo_ref[1] = minus1(0, base) * spread(1.0 / (part_minus + tw_edge), members)
     high_rows = source_ref[:, x_cells - 1, :] * inverse[x_cells - 1 :]
     low_rows = source_ref[:, 0, :] * inverse[:1]
     v_ref[:, x_cells - 1, :] = high_rows
     v_ref[:, 0, :] = low_rows
+    to_a_ref[0:base, :] = to_blocks(jnp.where(here.even, high_rows, low_rows))
+    to_b_ref[0:base, :] = to_blocks(jnp.where(here.even, low_rows, high_rows))
     margin, column = finish_edges(
         high_rows, low_rows, inner_margin_ref, inner_column_ref[...], high_side, oy_ref[...], ox_ref[...]
     )
@@ -372,7 +382,6 @@
 
 def interior_kernel(
     power,
-    place_ref,
     v_ref,
     before_ref,
     vf_ref,
@@ -393,8 +402,8 @@
     members, x_cells, y_cells = v_ref.shape
     half, frac_cells = vf_ref.shape
     blocks = y_cells // LANES
-    j = place_ref[2]
-    high_side = j == 0
+    here = Place()
+    j, high_side = here.j, here.high_side
     size = frac_cells // LANES * half
     theirs = from_blocks(core_ref[0:size, :], half)
     column_in = core_ref[2 * size : 2 * size + x_cells, :]
@@ -466,7 +475,6 @@
 
 def finish_kernel(
     power,
-    place_ref,
     vf_ref,
     near_a_ref,
     near_b_ref,
@@ -484,7 +492,6 @@
 ):
     if power == 1:
         (
-            halo_ref,
             weight_ref,
             ofrac_ref,
             oy_ref,
@@ -508,18 +515,18 @@
             *refs,
         ) = refs
     if power < 3:
-        out_f_ref, diff_ref, wown_ref, up_ref, down_ref, sent_ref, core_ref, image_ref, work_ref = refs
+        out_f_ref, diff_ref, wown_ref, to_a_ref, to_b_ref, sent_ref, core_ref, image_ref, work_ref = refs
     else:
         own_f_in_ref, v_ref, dots1_ref, dots2_ref, dots3_ref, moments_ref, acc_ref = refs
     half, frac_cells = vf_ref.shape
     x_cells, y_cells = unit_ref.shape[1:]
-    members = (near_a_ref.shape[0] - 2 * half) // (y_cells // LANES) if power > 1 else image_ref.shape[0]
+    members = v_ref.shape[0] if power == 3 else image_ref.shape[0]
     blocks = y_cells // LANES
     frac_blocks = frac_cells // LANES
-    j = place_ref[2]
-    high_side = j == 0
-    base = 0 if power == 1 else blocks * members
-    plus1, minus1, plus2, minus2 = neighbours(place_ref, near_a_ref, near_b_ref, far_c_ref, far_d_ref)
+    here = Place()
+    j, high_side = here.j, here.high_side
+    base = blocks * members
+    plus1, minus1, plus2, minus2 = neighbours(here, near_a_ref, near_b_ref, far_c_ref, far_d_ref)
     rows = sr_ref.shape[1]
 
     table, ghost_table = table_ref[...], ghost_table_ref[...]
@@ -570,29 +577,23 @@
     next_f = image_f * scale_f_ref[0]
     out_f_ref[...] = next_f
     at = blocks * members
-    send_network(next_f, sr, table, ghost_table, diff_ref, [(up_ref, at), (down_ref, at), (sent_ref, 0)])
+    send_network(next_f, sr, table, ghost_table, diff_ref, [(to_a_ref, at), (to_b_ref, at), (sent_ref, 0)])
 
     edges = []
-    for side, at, reader, ref in ((0, x_cells - 1, plus1, up_ref), (1, 0, minus1, down_ref)):
-        factor = unit_ref[side, at : at + 1, :]
-        old = image_in_ref[:, at, :]
-        pieces = []
-        for q in range(blocks):
-            beyond = halo_ref[side, q * members : (q + 1) * members, :] if power == 1 else reader(q * members, members)
-            cut = slice(q * LANES, (q + 1) * LANES)
-            piece = old[:, cut] - factor[:, cut] * beyond
-            ref[q * members : (q + 1) * members, :] = piece
-            pieces.append(piece)
-        edge = jnp.concatenate(pieces, axis=1)
+    for side, at, reader in ((0, x_cells - 1, plus1), (1, 0, minus1)):
+        beyond = from_blocks(reader(0, base), members)
+        edge = image_in_ref[:, at, :] - unit_ref[side, at : at + 1, :] * beyond
         image_ref[:, at, :] = edge
         edges.append(edge)
+    to_a_ref[0:base, :] = to_blocks(jnp.where(here.even, edges[0], edges[1]))
+    to_b_ref[0:base, :] = to_blocks(jnp.where(here.even, edges[1], edges[0]))
     margin, column = finish_edges(
         edges[0], edges[1], inner_margin_ref, inner_column_ref[...], high_side, oy_ref[...], ox_ref[...]
     )
     send_core(core_ref, next_f, margin, weight_ref[...], ofrac_ref[...], column, j, work_ref, wown_ref)
 
 
-def close_kernel(place_ref, totals_ref, v0_ref, v1_ref, v2_ref, f0_ref, f1_ref, f2_ref, x_ref, xf_ref, c_ref):
+def close_kernel(totals_ref, v0_ref, v1_ref, v2_ref, f0_ref, f1_ref, f2_ref, x_ref, xf_ref, c_ref):
     members, x_cells, y_cells = v0_ref.shape
     half, frac_cells = f0_ref.shape
 
@@ -620,7 +621,7 @@
     for k, row in enumerate((c0, c1, c2)):
         row = jnp.concatenate([row, jnp.zeros((1, LANES - members), F32)], axis=1)
         c_ref[k] = jnp.transpose(jnp.broadcast_to(row, (LANES, LANES)))
-    j = place_ref[2]
+    j = lax.axis_index("gy")
     own = pl.ds(pl.multiple_of(j * half, half), half)
 
     def wide(k, rows, width):
@@ -691,15 +692,8 @@
     rows = isect_local.size
     margin = ov_cell.size
     count = lax.axis_size("gx")
-    i, j = lax.axis_index("gx"), lax.axis_index("gy")
-    place = jnp.stack(
-        [i % 2, (i // 2) % 2, j, (i == 0).astype(jnp.int32), (i == count - 1).astype(jnp.int32)]
-    ).astype(jnp.int32)
-
-    def near(up, down):
-        even = i % 2 == 0
-        to_a = jnp.where(even, up, down)
-        to_b = jnp.where(even, down, up)
+
+    def near(to_a, to_b):
         return (
             lax.ppermute(to_a, "gx", pairs_of(count, 1, 0)),
             lax.ppermute(to_b, "gx", pairs_of(count, 1, 1)),
@@ -716,58 +710,54 @@
 
     blocks = y_cells // LANES
     frac_blocks = frac_cells // LANES
-    positions = jnp.arange(LANES, dtype=jnp.int32)
-    ov_live = positions[None, :] < ov_count.reshape(-1, 1)
-    weight = jnp.where(ov_live, ov_weight.reshape(ov_live.shape), 0.0).reshape(1, margin)
-    col = core(jnp.where(j == 0, perm_class[:, y_cells - 1 :], perm_class[:, :1]))
-    near_rows = blocks * members + 2 * blocks + half
-    coef, oy, ox, oslot, cond, up, down, supplied = call(
-        opening_kernel,
-        "opening",
-        (
-            place,
-            class_perm,
-            perm_class,
-            col,
-            storage,
-            source_matrix,
-            aperture,
-            send_slots,
-            ov_cell.reshape(1, margin),
-            weight,
-        ),
-        [
-            ((6, x_cells, y_cells), F32),
-            ((y_cells, margin), BF16),
-            ((x_cells, margin), F32),
-            ((frac_cells, slots), BF16),
-            ((half, frac_cells), F32),
-            ((near_rows, LANES), F32),
-            ((near_rows, LANES), F32),
-            ((half, slots), F32),
-        ],
-        scalars=2,
-    )
     field = (members, x_cells, y_cells)
     own = (half, frac_cells)
     hidden = pl.CostEstimate(flops=4_000_000_000, bytes_accessed=12_000_000, transcendentals=0)
-    near_a, near_b = near(up, down)
-    far_c, far_d = far(supplied)
-    first, second, table, ghost_table, ofrac, v0, margin_in, column = call(
+    perm, cond, oslot, to_a, to_b, sent, border = call(
+        opening_kernel,
+        "opening",
+        (class_perm, perm_class, aperture, send_slots),
+        [
+            ((x_cells, y_cells), F32),
+            (own, F32),
+            ((frac_cells, slots), BF16),
+            ((half + 8 * (-(-blocks // 8)), LANES), F32),
+            ((half + 8 * (-(-blocks // 8)), LANES), F32),
+            ((half, slots), F32),
+            ((x_cells, LANES), F32),
+        ],
+        scalars=1,
+    )
+
+    def exchange(to_a, to_b, sent, to_core):
+        near_a, near_b = near(to_a, to_b)
+        core_in = core(to_core)
+        sent, core_in = lax.optimization_barrier((sent, core_in))
+        far_c, far_d = far(sent)
+        return near_a, near_b, far_c, far_d, core_in
+
+    near_a, near_b, far_c, far_d, border = exchange(to_a, to_b, sent, border)
+    coef, oy, ox, weight, first, second, table, ghost_table, ofrac, v0, margin_in, column = call(
         inside_kernel,
         "inside",
         (
-            place,
-            coef,
+            ov_count.reshape(-1),
+            perm,
+            border,
+            storage,
             source_matrix,
-            isect_local.reshape(1, rows),
-            isect_other.reshape(1, rows),
-            ov_frac.reshape(1, margin),
+            ov_cell.reshape(-1, LANES),
+            ov_weight.reshape(-1, LANES),
+            isect_local,
+            isect_other,
+            ov_frac.reshape(-1, LANES),
             oslot,
-            oy,
-            ox,
         ),
         [
+            ((5, x_cells, y_cells), F32),
+            ((y_cells, margin), BF16),
+            ((x_cells, margin), F32),
+            ((1, margin), F32),
             ((frac_cells, rows), BF16),
             ((frac_cells, rows), BF16),
             ((frac_cells, rows + slots), BF16),
@@ -782,13 +772,13 @@
     )
     core_rows = 2 * frac_blocks * half + x_cells
     edge_rows = blocks * members
-    unit, f0, halo, sr, scale_f, diff, wown, sent, core_msg, v0 = call(
+    unit, f0, sr, scale_f, diff, wown, to_a, to_b, sent, core_msg, v0 = call(
         first_kernel,
         "first_vector",
         (
-            place,
             isect_count,
             coef,
+            perm,
             cond,
             source_matrix,
             source_fracture,
@@ -811,18 +801,19 @@
         [
             ((6, x_cells, y_cells), F32),
             (own, F32),
-            ((2, edge_rows, LANES), F32),
             ((half, rows), F32),
             ((2, half, frac_cells), F32),
             ((half, rows), F32),
             (own, F32),
+            ((edge_rows + 3 * half, LANES), F32),
+            ((edge_rows + 3 * half, LANES), F32),
             ((3 * half, LANES), F32),
             ((core_rows + 8 * frac_blocks, LANES), F32),
             (field, F32),
         ],
         scratch=[pltpu.VMEM((members, frac_cells), F32)],
-        scalars=2,
-        aliases={20: 9},
+        scalars=1,
+        aliases={20: 10},
     )
     near_rows = edge_rows + 2 * half
 
@@ -833,11 +824,10 @@
         return call(
             functools.partial(interior_kernel, power),
             f"interior_{power}",
-            (place, v, before, vf, before_f, core_in, scale_f, unit, weight, ofrac, oy, ox),
+            (v, before, vf, before_f, core_in, scale_f, unit, weight, ofrac, oy, ox),
             outs + [((8, members), F32)],
             scratch=[pltpu.VMEM((members, margin), F32), pltpu.VMEM((members, frac_cells), F32)]
             + [pltpu.VMEM((members, LANES), F32)] * power,
-            scalars=1,
             cost=hidden,
         )
 
@@ -853,56 +843,46 @@
     ]
     finish_scratch = [pltpu.VMEM((members, frac_cells), F32)]
 
-    near_a, near_b = near(sent, sent)
-    far_c, far_d = far(sent)
-    core_in = core(core_msg)
-    image, margin_in, column, dots1 = interior(1, v0, halo, f0, f0, core_in)
-    own_f, f1, diff, wown, up, down, sent, core_msg, v1 = call(
+    near_a, near_b, far_c, far_d, core_in = exchange(to_a, to_b, sent, core_msg)
+    image, margin_in, column, dots1 = interior(1, v0, v0, f0, f0, core_in)
+    own_f, f1, diff, wown, to_a, to_b, sent, core_msg, v1 = call(
         functools.partial(finish_kernel, 1),
         "finish_1",
-        (place, f0, near_a, near_b, far_c, far_d, core_in, diff, wown, sr, scale_f, unit, table, ghost_table)
-        + (halo, weight, ofrac, oy, ox, margin_in, column, image),
+        (f0, near_a, near_b, far_c, far_d, core_in, diff, wown, sr, scale_f, unit, table, ghost_table)
+        + (weight, ofrac, oy, ox, margin_in, column, image),
         [(own, F32)] + finish_outs,
         scratch=finish_scratch,
-        scalars=1,
-        aliases={21: 8},
-    )
-    near_a, near_b = near(up, down)
-    far_c, far_d = far(sent)
-    core_in = core(core_msg)
+        aliases={19: 8},
+    )
+    near_a, near_b, far_c, far_d, core_in = exchange(to_a, to_b, sent, core_msg)
     image, margin_in, column, dots2 = interior(2, v1, v0, f1, f0, core_in)
-    f2, diff, wown, up, down, sent, core_msg, v2 = call(
+    f2, diff, wown, to_a, to_b, sent, core_msg, v2 = call(
         functools.partial(finish_kernel, 2),
         "finish_2",
-        (place, f1, near_a, near_b, far_c, far_d, core_in, diff, wown, sr, scale_f, unit, table, ghost_table)
+        (f1, near_a, near_b, far_c, far_d, core_in, diff, wown, sr, scale_f, unit, table, ghost_table)
         + (own_f, weight, ofrac, oy, ox, margin_in, column, image),
         finish_outs,
         scratch=finish_scratch,
-        scalars=1,
-        aliases={21: 7},
-    )
-    near_a, near_b = near(up, down)
-    far_c, far_d = far(sent)
-    core_in = core(core_msg)
+        aliases={20: 7},
+    )
+    near_a, near_b, far_c, far_d, core_in = exchange(to_a, to_b, sent, core_msg)
     (dots3,) = interior(3, v2, v1, f2, f1, core_in)
     peers = count * lax.axis_size("gy")
     (moments,) = call(
         functools.partial(finish_kernel, 3),
         "finish_3",
-        (place, f2, near_a, near_b, far_c, far_d, core_in, diff, wown, sr, scale_f, unit, table, ghost_table)
+        (f2, near_a, near_b, far_c, far_d, core_in, diff, wown, sr, scale_f, unit, table, ghost_table)
         + (own_f, v2, dots1, dots2, dots3),
         [((peers, 2, LANES), F32)],
         scratch=[pltpu.VMEM((members, LANES), F32)],
-        scalars=1,
     )
     totals = lax.all_to_all(moments, ("gx", "gy"), 0, 0)
     return call(
         close_kernel,
         "iterate",
-        (place, totals, v0, v1, v2, f0, f1, f2),
+        (totals, v0, v1, v2, f0, f1, f2),
         [(field, F32), (own, F32)],
         scratch=[pltpu.VMEM((3, LANES, LANES), F32)],
-        scalars=1,
     )
 
 

time: 66.9 us -> 61.3 us (0.916)
  Pallas kernels: 18.5 us -> 14.8 us
  local copies, waits for them, and re-layouts: 3.91 us -> 5.4 us
  starting transfers between devices: 22.5 us -> 21.2 us
  waiting for transfers between devices: 9.85 us -> 8.84 us
  other arithmetic: 0.92 us -> 0 us
    ppermute x4, starting transfers between devices: 7.9 us -> 3.25 us  [far(): lax.ppermute(value, 'gx', pairs_of(count, 2, 1))]
    pallas_call x10, Pallas kernels: 18.5 us -> 14.8 us  [call(): pl.pallas_call(kernel, name=name, out_shape=[jax.ShapeDtypeStruct(shape,...]
    ppermute x4, waiting for transfers between devices: 0.01 us -> 3.08 us  [far(): lax.ppermute(value, 'gx', pairs_of(count, 2, 1))]
    ppermute x4, starting transfers between devices: 9.11 us -> 12.1 us  [near(): lax.ppermute(to_b, 'gx', pairs_of(count, 1, 1))]
    ppermute x4, waiting for transfers between devices: 2.61 us -> 0.01 us  [near(): lax.ppermute(to_a, 'gx', pairs_of(count, 1, 0))]
    ppermute x4, starting transfers between devices: 2.66 us -> 4.96 us  [near(): lax.ppermute(to_a, 'gx', pairs_of(count, 1, 0))]
    ppermute x4, starting transfers between devices: 2.37 us -> 0.23 us  [far(): lax.ppermute(value, 'gx', pairs_of(count, 2, 0))]
    ppermute x4, waiting for transfers between devices: 7.21 us -> 5.47 us  [near(): lax.ppermute(to_b, 'gx', pairs_of(count, 1, 1))]
  transfers between devices with their start and end apart: 20 -> 20, of which waited for: 7 -> 8; matrix products, arithmetic and copies ran while one was open for 0% -> 0% of each run, Pallas kernels for 14% -> 13%
where the time goes in v2:
time: 61.3 us; the launch traced here: 60.9 us
  starting transfers between devices  21.2 us (35%)
  Pallas kernels  14.8 us (24%)
  blocking collectives  9.77 us (16%)
  waiting for transfers between devices  8.84 us (14%)
  local copies, waits for them, and re-layouts  5.4 us (9%)
  between operations  0.81 us (1%)
    pallas_call x10, Pallas kernels, call(): pl.pallas_call(kernel, name=name, out_shape=[jax.ShapeDtypeStruct(shape,...  14.8 us
    ppermute x4, starting transfers between devices, near(): lax.ppermute(to_b, 'gx', pairs_of(count, 1, 1))  12.1 us
    all_to_all x1, blocking collectives, per_device(): totals = lax.all_to_all(moments, ('gx', 'gy'), 0, 0)  9.77 us
    ppermute x4, waiting for transfers between devices, near(): lax.ppermute(to_b, 'gx', pairs_of(count, 1, 1))  5.47 us
    unnamed x30, local copies, waits for them, and re-layouts  5.4 us
    ppermute x4, starting transfers between devices, near(): lax.ppermute(to_a, 'gx', pairs_of(count, 1, 0))  4.96 us
    ppermute x4, starting transfers between devices, far(): lax.ppermute(value, 'gx', pairs_of(count, 2, 1))  3.25 us
    ppermute x4, waiting for transfers between devices, far(): lax.ppermute(value, 'gx', pairs_of(count, 2, 1))  3.08 us
  transfers between devices with their start and end apart: 20, of which 8 were waited for; matrix products, arithmetic and copies ran while one was open for 0% of the time, Pallas kernels for 13%

profile of v2, /device:TPU:0, one launch (start us, length us, event | category | flops | bytes accessed | tf_op | source)
XLA Modules:
  0.0 60.9 jit_solution(10305902422010118896)
XLA Ops:
  0.6 0.7 %copy-done.3 = s32[16,512]{1,0:T(8,128)S(1)} copy-done((s32[16,512]{1,0:T(8,128)S(1)}, s32[16,512]{1,0:T(8,128)}, u32[]{:S(2)}) %copy-start.3) | copy-done | bytes 32792
  1.4 0.8 %copy-done.4 = f32[16,512]{1,0:T(8,128)S(1)} copy-done((f32[16,512]{1,0:T(8,128)S(1)}, f32[16,512]{1,0:T(8,128)}, u32[]{:S(2)}) %copy-start.4) | copy-done | bytes 32792
  2.2 0.7 %copy-done.5 = f32[8]{0:T(128)S(1)} copy-done((f32[8]{0:T(128)S(1)}, f32[8]{0:T(128)}, u32[]{:S(2)}) %copy-start.5) | copy-done | bytes 56
  2.8 0.7 %copy-done.6 = s32[1,128]{1,0:T(1,128)S(1)} copy-done((s32[1,128]{1,0:T(1,128)S(1)}, s32[1,128]{1,0:T(1,128)}, u32[]{:S(2)}) %copy-start.6) | copy-done | bytes 536
  3.5 0.7 %opening.1 = (f32[16,512]{1,0:T(8,128)S(1)}, f32[16,512]{1,0:T(8,128)S(1)}, bf16[512,128]{1,0:T(8,128)(2,1)S(1)}, f32[24,128]{1,0:T(8,128)S(1)}, f32[24,128]{1,0...) custom-call(f32[8]{0:T(128)S(1)} %copy-done.5, s32[16,512]{1,0:T(8,128)S(1)} %copy-done.3, ...), custom_call_target="tpu_custom_call" | custom-call | tf_op jit(solution)/shard_map/opening/pallas_call | solution.py:660
  4.2 0.5 collective-permute-start
  4.7 2.6 %collective-permute-start.1 = (f32[24,128]{1,0:T(8,128)S(1)}, f32[24,128]{1,0:T(8,128)S(1)}, u32[]{:S(2)}, u32[]{:S(2)}) collective-permute-start(f32[24,128]{1,0:T(8,128)S(1)} %get-tuple-element.73), channel_id=1, source_target_pairs={{0,2},{2,0},{4,6},{6,4},{8,10},{10,8},{12,14},{14,12},{1,3},{3,1},... | collective-permute-start | bytes 36872 | tf_op jit(solution)/shard_map/ppermute | solution.py:698
  7.3 3.6 %collective-permute-start.2 = (f32[24,128]{1,0:T(8,128)S(1)}, f32[24,128]{1,0:T(8,128)S(1)}, u32[]{:S(2)}, u32[]{:S(2)}) collective-permute-start(f32[24,128]{1,0:T(8,128)S(1)} %get-tuple-element.74), channel_id=1, source_target_pairs={{2,4},{4,2},{6,8},{8,6},{10,12},{12,10},{14,0},{0,14},{3,5},{5,3},... | collective-permute-start | bytes 36872 | tf_op jit(solution)/shard_map/ppermute | solution.py:699
  10.8 0.0 collective-permute-done.border_ref
  10.8 0.5 collective-permute-start.4
  11.3 0.0 collective-permute-start.3
  11.3 0.0 copy-start.9
  11.3 0.0 copy-start.11
  11.3 0.0 copy-start.14
  11.4 0.6 %copy-done.12 = f32[1,1,2,128]{3,2,1,0:T(2,128)S(1)} copy-done((f32[1,1,2,128]{3,2,1,0:T(2,128)S(1)}, f32[1,1,2,128]{3,2,1,0:T(2,128)}, u32[]{:S(2)}) %copy-start.12) | copy-done | bytes 1048
  12.0 0.0 copy-done.13
  12.0 0.0 copy-done.10
  12.0 0.0 copy-done.9
  12.0 0.0 copy-done.11
  12.0 1.2 %copy-done = f32[32,16,512]{2,1,0:T(8,128)S(1)} copy-done((f32[32,16,512]{2,1,0:T(8,128)S(1)}, f32[32,16,512]{2,1,0:T(8,128)}, u32[]{:S(2)}) %copy-start) | copy-done | bytes 1048600
  13.3 1.9 %inside.1 = (f32[5,16,512]{2,1,0:T(8,128)S(1)}, bf16[512,256]{1,0:T(8,128)(2,1)S(1)}, f32[16,256]{1,0:T(8,128)S(1)}, f32[1,256]{1,0:T(1,128)S(1)}, bf16[512,512]...) custom-call(s32[2]{0:T(128)S(1)} %bitcast.7, ...), custom_call_target="tpu_custom_call" | custom-call | flops 4000000000 | bytes 12000000 | tf_op jit(solution)/shard_map/inside/pallas_call | solution.py:660
  15.2 0.0 collective-permute-done.1.near_a_ref
  15.2 0.0 collective-permute-done.2.near_b_ref
  15.2 1.1 %collective-permute-done.4.far_d_ref = f32[16,128]{1,0:T(8,128)S(1)} collective-permute-done((f32[16,128]{1,0:T(8,128)S(1)}, f32[16,128]{1,0:T(8,128)S(1)}, u32[]{:S(2)}, u32[]{:S(2)}) %collective-permute-start.4) | collective-permute-done | bytes 8224 | tf_op jit(solution)/shard_map/ppermute | solution.py:705
  16.3 0.0 collective-permute-done.3.far_c_ref
  16.3 0.6 %copy-done.7 = s32[4]{0:T(128)S(1)} copy-done((s32[4]{0:T(128)S(1)}, s32[4]{0:T(128)}, u32[]{:S(2)}) %copy-start.7) | copy-done | bytes 40
  17.0 1.9 %first_vector.1 = (f32[6,16,512]{2,1,0:T(8,128)S(1)}, f32[16,512]{1,0:T(8,128)S(1)}, f32[16,512]{1,0:T(8,128)S(1)}, f32[2,16,512]{2,1,0:T(8,128)S(1)}, f32[16,51...) custom-call(s32[4]{0:T(128)S(1)} %copy-done.7, ...), custom_call_target="tpu_custom_call", output_to_operand_aliasing={{10}: (20, {})} | custom-call | tf_op jit(solution)/shard_map/first_vector/pallas_call | solution.py:660
  18.8 0.0 collective-permute-start.7
  18.9 1.2 %collective-permute-start.5 = (f32[176,128]{1,0:T(8,128)S(1)}, f32[176,128]{1,0:T(8,128)S(1)}, u32[]{:S(2)}, u32[]{:S(2)}) collective-permute-start(f32[176,128]{1,0:T(8,128)S(1)} %get-tuple-element.87), channel_id=1, source_target_pairs={{0,2},{2,0},{4,6},{6,4},{8,10},{10,8},{12,14},{14,12},{1,3},{3,1},... | collective-permute-start | bytes 270344 | tf_op jit(solution)/shard_map/ppermute | solution.py:698
  20.0 2.7 %collective-permute-start.6 = (f32[176,128]{1,0:T(8,128)S(1)}, f32[176,128]{1,0:T(8,128)S(1)}, u32[]{:S(2)}, u32[]{:S(2)}) collective-permute-start(f32[176,128]{1,0:T(8,128)S(1)} %get-tuple-element.88), channel_id=1, source_target_pairs={{2,4},{4,2},{6,8},{8,6},{10,12},{12,10},{14,0},{0,14},{3,5},{5,3},... | collective-permute-start | bytes 270344 | tf_op jit(solution)/shard_map/ppermute | solution.py:699
  22.7 0.0 collective-permute-done.7.core_ref.core_in_ref
  22.7 2.0 %collective-permute-start.9 = (f32[48,128]{1,0:T(8,128)S(1)}, f32[48,128]{1,0:T(8,128)S(1)}, u32[]{:S(2)}, u32[]{:S(2)}) collective-permute-start(f32[48,128]{1,0:T(8,128)S(1)} %get-tuple-element.91), channel_id=1, source_target_pairs={{4,8},{8,4},{6,10},{10,6},{12,0},{0,12},{14,2},{2,14},{5,9},{9,5},... | collective-permute-start | bytes 73736 | tf_op jit(solution)/shard_map/ppermute | solution.py:705
  24.7 0.0 collective-permute-start.8
  24.7 2.2 %interior_1.1 = (f32[32,16,512]{2,1,0:T(8,128)S(1)}, f32[32,256]{1,0:T(8,128)S(1)}, f32[16,128]{1,0:T(8,128)S(1)}, f32[8,32]{1,0:T(8,128)S(1)}) custom-call(f32[32,16,512]{2,1,0:T(8,128)S(1)} %get-tuple-element.98.v_ref.before_ref.v0_ref, f32[32,16,512]{2,1,0:T(8,128)S(1)} %get-tuple-element.98.v_ref.before_ref.v0_ref, ...), custom_call_target="tpu_custom_call" | custom-call | flops 4000000000 | bytes 12000000 | tf_op jit(solution)/shard_map/interior_1/pallas_call | solution.py:660
  26.9 0.0 collective-permute-done.5.near_a_ref
  26.9 1.1 %collective-permute-done.6.near_b_ref = f32[176,128]{1,0:T(8,128)S(1)} collective-permute-done((f32[176,128]{1,0:T(8,128)S(1)}, f32[176,128]{1,0:T(8,128)S(1)}, u32[]{:S(2)}, u32[]{:S(2)}) %collective-permute-start.6) | collective-permute-done | bytes 90144 | tf_op jit(solution)/shard_map/ppermute | solution.py:699
  28.0 0.3 collective-permute-done.9.far_d_ref
  28.3 0.3 collective-permute-done.8.far_c_ref
  28.6 1.0 %finish_1.1 = (f32[16,512]{1,0:T(8,128)S(1)}, f32[16,512]{1,0:T(8,128)S(1)}, f32[16,512]{1,0:T(8,128)S(1)}, f32[16,512]{1,0:T(8,128)S(1)}, f32[160,128]{1,0:T(8,...) custom-call(f32[16,512]{1,0:T(8,128)S(1)} %get-tuple-element.86.vf_r, ...), custom_call_target="tpu_custom_call", output_to_operand_aliasing={{8}: (19, {})} | custom-call | tf_op jit(solution)/shard_map/finish_1/pallas_call | solution.py:660
  29.6 0.1 collective-permute-start.12
  29.7 0.6 %collective-permute-start.10 = (f32[160,128]{1,0:T(8,128)S(1)}, f32[160,128]{1,0:T(8,128)S(1)}, u32[]{:S(2)}, u32[]{:S(2)}) collective-permute-start(f32[160,128]{1,0:T(8,128)S(1)} %get-tuple-element.103), channel_id=1, source_target_pairs={{0,2},{2,0},{4,6},{6,4},{8,10},{10,8},{12,14},{14,12},{1,3},{3,1},... | collective-permute-start | bytes 245768 | tf_op jit(solution)/shard_map/ppermute | solution.py:698
  30.3 2.9 %collective-permute-start.11 = (f32[160,128]{1,0:T(8,128)S(1)}, f32[160,128]{1,0:T(8,128)S(1)}, u32[]{:S(2)}, u32[]{:S(2)}) collective-permute-start(f32[160,128]{1,0:T(8,128)S(1)} %get-tuple-element.104), channel_id=1, source_target_pairs={{2,4},{4,2},{6,8},{8,6},{10,12},{12,10},{14,0},{0,14},{3,5},{5,3},... | collective-permute-start | bytes 245768 | tf_op jit(solution)/shard_map/ppermute | solution.py:699
  33.2 0.0 collective-permute-done.12.core_ref.core_in_ref
  33.2 0.2 collective-permute-start.14
  33.4 0.2 collective-permute-start.13
  33.7 2.3 %interior_2.1 = (f32[32,16,512]{2,1,0:T(8,128)S(1)}, f32[32,256]{1,0:T(8,128)S(1)}, f32[16,128]{1,0:T(8,128)S(1)}, f32[8,32]{1,0:T(8,128)S(1)}) custom-call(f32[32,16,512]{2,1,0:T(8,128)S(1)} %get-tuple-element.112.v_ref.before_ref.v1_ref, f32[32,16,512]{2,1,0:T(8,128)S(1)} %get-tuple-element.98.v_ref.before_ref.v0_ref, ...), custom_call_target="tpu_custom_call" | custom-call | flops 4000000000 | bytes 12000000 | tf_op jit(solution)/shard_map/interior_2/pallas_call | solution.py:660
  35.9 0.0 collective-permute-done.10.near_a_ref
  35.9 2.0 %collective-permute-done.11.near_b_ref = f32[160,128]{1,0:T(8,128)S(1)} collective-permute-done((f32[160,128]{1,0:T(8,128)S(1)}, f32[160,128]{1,0:T(8,128)S(1)}, u32[]{:S(2)}, u32[]{:S(2)}) %collective-permute-start.11) | collective-permute-done | bytes 81952 | tf_op jit(solution)/shard_map/ppermute | solution.py:699
  38.0 0.8 %collective-permute-done.14.far_d_ref = f32[32,128]{1,0:T(8,128)S(1)} collective-permute-done((f32[32,128]{1,0:T(8,128)S(1)}, f32[32,128]{1,0:T(8,128)S(1)}, u32[]{:S(2)}, u32[]{:S(2)}) %collective-permute-start.14) | collective-permute-done | bytes 16416 | tf_op jit(solution)/shard_map/ppermute | solution.py:705
  38.8 0.0 collective-permute-done.13.far_c_ref
  38.8 0.9 %finish_2.1 = (f32[16,512]{1,0:T(8,128)S(1)}, f32[16,512]{1,0:T(8,128)S(1)}, f32[16,512]{1,0:T(8,128)S(1)}, f32[160,128]{1,0:T(8,128)S(1)}, f32[160,128]{1,0:T(8...) custom-call(f32[16,512]{1,0:T(8,128)S(1)} %get-tuple-element.102.vf_, ...), custom_call_target="tpu_custom_call", output_to_operand_aliasing={{7}: (20, {})} | custom-call | tf_op jit(solution)/shard_map/finish_2/pallas_call | solution.py:660
  39.7 0.1 collective-permute-start.17
  39.8 0.6 %collective-permute-start.15 = (f32[160,128]{1,0:T(8,128)S(1)}, f32[160,128]{1,0:T(8,128)S(1)}, u32[]{:S(2)}, u32[]{:S(2)}) collective-permute-start(f32[160,128]{1,0:T(8,128)S(1)} %get-tuple-element.117), channel_id=1, source_target_pairs={{0,2},{2,0},{4,6},{6,4},{8,10},{10,8},{12,14},{14,12},{1,3},{3,1},... | collective-permute-start | bytes 245768 | tf_op jit(solution)/shard_map/ppermute | solution.py:698
  40.4 2.9 %collective-permute-start.16 = (f32[160,128]{1,0:T(8,128)S(1)}, f32[160,128]{1,0:T(8,128)S(1)}, u32[]{:S(2)}, u32[]{:S(2)}) collective-permute-start(f32[160,128]{1,0:T(8,128)S(1)} %get-tuple-element.118), channel_id=1, source_target_pairs={{2,4},{4,2},{6,8},{8,6},{10,12},{12,10},{14,0},{0,14},{3,5},{5,3},... | collective-permute-start | bytes 245768 | tf_op jit(solution)/shard_map/ppermute | solution.py:699
  43.3 0.0 collective-permute-done.17.core_ref.core_in_ref
  43.4 0.6 collective-permute-start.19
  43.9 0.0 collective-permute-start.18
  44.0 1.7 %interior_3.1.refs_4_ = f32[8,32]{1,0:T(8,128)S(1)} custom-call(f32[32,16,512]{2,1,0:T(8,128)S(1)} %get-tuple-element.125.v_ref.refs_1_.v2_ref, f32[32,16,512]{2,1,0:T(8,128)S(1)} %get-tuple-element.112.v_ref.before_ref.v1_ref, f32[16,512]{1,0:T(8,128)S(1)} %get-tuple-element.116.vf_ref.f2_ref, f32[16,512]{1,0:T(8,128)S(1)} %get-tuple-element.102.vf_ref.before_f_ref.f1_ref, ...), custom_call_target="tpu_custom_call" | custom-call | flops 4000000000 | bytes 12000000 | tf_op jit(solution)/shard_map/interior_3/pallas_call | solution.py:660
  45.7 0.0 collective-permute-done.15.near_a_ref
  45.7 2.4 %collective-permute-done.16.near_b_ref = f32[160,128]{1,0:T(8,128)S(1)} collective-permute-done((f32[160,128]{1,0:T(8,128)S(1)}, f32[160,128]{1,0:T(8,128)S(1)}, u32[]{:S(2)}, u32[]{:S(2)}) %collective-permute-start.16) | collective-permute-done | bytes 81952 | tf_op jit(solution)/shard_map/ppermute | solution.py:699
  48.1 0.8 %collective-permute-done.19.far_d_ref = f32[32,128]{1,0:T(8,128)S(1)} collective-permute-done((f32[32,128]{1,0:T(8,128)S(1)}, f32[32,128]{1,0:T(8,128)S(1)}, u32[]{:S(2)}, u32[]{:S(2)}) %collective-permute-start.19) | collective-permute-done | bytes 16416 | tf_op jit(solution)/shard_map/ppermute | solution.py:705
  48.9 0.6 finish_3.1
  49.5 9.8 %all_to_all.5.totals_ref = f32[16,2,128]{2,1,0:T(2,128)S(1)} all-to-all(f32[16,2,128]{2,1,0:T(2,128)S(1)} %finish_3.1), channel_id=1, replica_groups=mesh['grp'=2,'gx'=8,'gy'=2] {'gx','gy'}, dimensions={0} | all-to-all | bytes 32768 | tf_op jit(solution)/shard_map/all_to_all | solution.py:879
  59.3 1.6 %iterate.1 = (f32[32,16,512]{2,1,0:T(8,128)}, f32[16,512]{1,0:T(8,128)}) custom-call(f32[16,2,128]{2,1,0:T(2,128)S(1)} %all_to_all.5.totals_ref, f32[32,16,512]{2,1,0:T(8,128)S(1)} %get-tuple-element.98.v_ref.before_ref.v0_ref, f32[32,16,512]{2,1,0:T(8,128)S(1)} %get-tuple-element.112.v_ref.before_ref.v1_ref, ...), custom_call_target="tpu_custom_call" | custom-call | tf_op jit(solution)/shard_map/iterate/pallas_call | solution.py:660
  (17 shorter events, 0.0 us)
Async XLA Ops:
  0.6 0.8 %copy-start.3 = (s32[16,512]{1,0:T(8,128)S(1)}, s32[16,512]{1,0:T(8,128)}, u32[]{:S(2)}) copy-start(s32[16,512]{1,0:T(8,128)} %class_ref.1) | copy-start | bytes 98308
  1.4 0.8 %copy-start.4 = (f32[16,512]{1,0:T(8,128)S(1)}, f32[16,512]{1,0:T(8,128)}, u32[]{:S(2)}) copy-start(f32[16,512]{1,0:T(8,128)} %aperture_ref.1) | copy-start | bytes 98308
  2.1 0.7 %copy-start.5 = (f32[8]{0:T(128)S(1)}, f32[8]{0:T(128)}, u32[]{:S(2)}) copy-start(f32[8]{0:T(128)} %perm_table_ref.1) | copy-start | bytes 100
  2.8 0.7 %copy-start.6 = (s32[1,128]{1,0:T(1,128)S(1)}, s32[1,128]{1,0:T(1,128)}, u32[]{:S(2)}) copy-start(s32[1,128]{1,0:T(1,128)} %slots_ref.1) | copy-start | bytes 1540
  3.5 7.9 %copy-start.8 = (f32[16,512]{1,0:T(8,128)S(1)}, f32[16,512]{1,0:T(8,128)}, u32[]{:S(2)}) copy-start(f32[16,512]{1,0:T(8,128)} %storage_ref.1) | copy-start | bytes 98308
  4.2 6.7 %collective-permute-start = (f32[16,128]{1,0:T(8,128)S(1)}, f32[16,128]{1,0:T(8,128)S(1)}, u32[]{:S(2)}, u32[]{:S(2)}) collective-permute-start(f32[16,128]{1,0:T(8,128)S(1)} %get-tuple-element.67), channel_id=1, source_target_pairs={{0,1},{1,0},{2,3},{3,2},{4,5},{5,4},{6,7},{7,6},{8,9},{9,8},{10,11... | collective-permute-start | bytes 24584 | tf_op jit(solution)/shard_map/ppermute | solution.py:709
  4.7 10.5 %collective-permute-start.1 = (f32[24,128]{1,0:T(8,128)S(1)}, f32[24,128]{1,0:T(8,128)S(1)}, u32[]{:S(2)}, u32[]{:S(2)}) collective-permute-start(f32[24,128]{1,0:T(8,128)S(1)} %get-tuple-element.73), channel_id=1, source_target_pairs={{0,2},{2,0},{4,6},{6,4},{8,10},{10,8},{12,14},{14,12},{1,3},{3,1},... | collective-permute-start | bytes 36872 | tf_op jit(solution)/shard_map/ppermute | solution.py:698
  7.3 7.9 %collective-permute-start.2 = (f32[24,128]{1,0:T(8,128)S(1)}, f32[24,128]{1,0:T(8,128)S(1)}, u32[]{:S(2)}, u32[]{:S(2)}) collective-permute-start(f32[24,128]{1,0:T(8,128)S(1)} %get-tuple-element.74), channel_id=1, source_target_pairs={{2,4},{4,2},{6,8},{8,6},{10,12},{12,10},{14,0},{0,14},{3,5},{5,3},... | collective-permute-start | bytes 36872 | tf_op jit(solution)/shard_map/ppermute | solution.py:699
  10.8 5.4 %collective-permute-start.4 = (f32[16,128]{1,0:T(8,128)S(1)}, f32[16,128]{1,0:T(8,128)S(1)}, u32[]{:S(2)}, u32[]{:S(2)}) collective-permute-start(f32[16,128]{1,0:T(8,128)S(1)} %get-tuple-element.75), channel_id=1, source_target_pairs={{4,8},{8,4},{6,10},{10,6},{12,0},{0,12},{14,2},{2,14},{5,9},{9,5},... | collective-permute-start | bytes 24584 | tf_op jit(solution)/shard_map/ppermute | solution.py:705
  11.3 5.0 %collective-permute-start.3 = (f32[16,128]{1,0:T(8,128)S(1)}, f32[16,128]{1,0:T(8,128)S(1)}, u32[]{:S(2)}, u32[]{:S(2)}) collective-permute-start(f32[16,128]{1,0:T(8,128)S(1)} %get-tuple-element.75), channel_id=1, source_target_pairs={{0,4},{4,0},{2,6},{6,2},{8,12},{12,8},{10,14},{14,10},{1,5},{5,1},... | collective-permute-start | bytes 24584 | tf_op jit(solution)/shard_map/ppermute | solution.py:704
  11.3 0.7 %copy-start.12 = (f32[1,1,2,128]{3,2,1,0:T(2,128)S(1)}, f32[1,1,2,128]{3,2,1,0:T(2,128)}, u32[]{:S(2)}) copy-start(f32[1,1,2,128]{3,2,1,0:T(2,128)} %param.26) | copy-start | bytes 3076
  11.3 0.7 %copy-start.13 = (s32[1,1,2,128]{3,2,1,0:T(2,128)S(1)}, s32[1,1,2,128]{3,2,1,0:T(2,128)}, u32[]{:S(2)}) copy-start(s32[1,1,2,128]{3,2,1,0:T(2,128)} %param.25) | copy-start | bytes 3076
  11.3 0.7 %copy-start.10 = (s32[4,128]{1,0:T(4,128)S(1)}, s32[4,128]{1,0:T(4,128)}, u32[]{:S(2)}) copy-start(s32[4,128]{1,0:T(4,128)} %other_in_ref.1) | copy-start | bytes 6148
  11.3 0.7 %copy-start.9 = (s32[4,128]{1,0:T(4,128)S(1)}, s32[4,128]{1,0:T(4,128)}, u32[]{:S(2)}) copy-start(s32[4,128]{1,0:T(4,128)} %local_ref.1) | copy-start | bytes 6148
  11.3 0.7 %copy-start.11 = (s32[1,1,2,128]{3,2,1,0:T(2,128)S(1)}, s32[1,1,2,128]{3,2,1,0:T(2,128)}, u32[]{:S(2)}) copy-start(s32[1,1,2,128]{3,2,1,0:T(2,128)} %param.24) | copy-start | bytes 3076
  11.3 0.7 %copy-start.14 = (s32[1,1,2]{2,1,0:T(1,128)S(1)}, s32[1,1,2]{2,1,0:T(1,128)}, u32[]{:S(2)}) copy-start(s32[1,1,2]{2,1,0:T(1,128)} %param.27) | copy-start | bytes 28
  12.0 1.2 %copy-start = (f32[32,16,512]{2,1,0:T(8,128)S(1)}, f32[32,16,512]{2,1,0:T(8,128)}, u32[]{:S(2)}) copy-start(f32[32,16,512]{2,1,0:T(8,128)} %source_ref.3) | copy-start | bytes 3145732
  13.3 3.0 %copy-start.1 = (f32[32,16,512]{2,1,0:T(8,128)S(1)}, f32[32,16,512]{2,1,0:T(8,128)}, u32[]{:S(2)}) copy-start(f32[32,16,512]{2,1,0:T(8,128)} %source_ref.3) | copy-start | bytes 3145732
  13.3 3.0 %copy-start.2 = (f32[16,512]{1,0:T(8,128)S(1)}, f32[16,512]{1,0:T(8,128)}, u32[]{:S(2)}) copy-start(f32[16,512]{1,0:T(8,128)} %source_f_ref.1) | copy-start | bytes 98308
  16.3 0.7 %copy-start.7 = (s32[4]{0:T(128)S(1)}, s32[4]{0:T(128)}, u32[]{:S(2)}) copy-start(s32[4]{0:T(128)} %count_ref.1) | copy-start | bytes 52
  18.8 3.9 %collective-permute-start.7 = (f32[176,128]{1,0:T(8,128)S(1)}, f32[176,128]{1,0:T(8,128)S(1)}, u32[]{:S(2)}, u32[]{:S(2)}) collective-permute-start(f32[176,128]{1,0:T(8,128)S(1)} %get-tuple-element.90), channel_id=1, source_target_pairs={{0,1},{1,0},{2,3},{3,2},{4,5},{5,4},{6,7},{7,6},{8,9},{9,8},{10,11... | collective-permute-start | bytes 270344 | tf_op jit(solution)/shard_map/ppermute | solution.py:709
  18.9 8.0 %collective-permute-start.5 = (f32[176,128]{1,0:T(8,128)S(1)}, f32[176,128]{1,0:T(8,128)S(1)}, u32[]{:S(2)}, u32[]{:S(2)}) collective-permute-start(f32[176,128]{1,0:T(8,128)S(1)} %get-tuple-element.87), channel_id=1, source_target_pairs={{0,2},{2,0},{4,6},{6,4},{8,10},{10,8},{12,14},{14,12},{1,3},{3,1},... | collective-permute-start | bytes 270344 | tf_op jit(solution)/shard_map/ppermute | solution.py:698
  20.0 8.0 %collective-permute-start.6 = (f32[176,128]{1,0:T(8,128)S(1)}, f32[176,128]{1,0:T(8,128)S(1)}, u32[]{:S(2)}, u32[]{:S(2)}) collective-permute-start(f32[176,128]{1,0:T(8,128)S(1)} %get-tuple-element.88), channel_id=1, source_target_pairs={{2,4},{4,2},{6,8},{8,6},{10,12},{12,10},{14,0},{0,14},{3,5},{5,3},... | collective-permute-start | bytes 270344 | tf_op jit(solution)/shard_map/ppermute | solution.py:699
  22.7 5.6 %collective-permute-start.9 = (f32[48,128]{1,0:T(8,128)S(1)}, f32[48,128]{1,0:T(8,128)S(1)}, u32[]{:S(2)}, u32[]{:S(2)}) collective-permute-start(f32[48,128]{1,0:T(8,128)S(1)} %get-tuple-element.91), channel_id=1, source_target_pairs={{4,8},{8,4},{6,10},{10,6},{12,0},{0,12},{14,2},{2,14},{5,9},{9,5},... | collective-permute-start | bytes 73736 | tf_op jit(solution)/shard_map/ppermute | solution.py:705
  24.7 3.9 %collective-permute-start.8 = (f32[48,128]{1,0:T(8,128)S(1)}, f32[48,128]{1,0:T(8,128)S(1)}, u32[]{:S(2)}, u32[]{:S(2)}) collective-permute-start(f32[48,128]{1,0:T(8,128)S(1)} %get-tuple-element.91), channel_id=1, source_target_pairs={{0,4},{4,0},{2,6},{6,2},{8,12},{12,8},{10,14},{14,10},{1,5},{5,1},... | collective-permute-start | bytes 73736 | tf_op jit(solution)/shard_map/ppermute | solution.py:704
  29.6 3.6 %collective-permute-start.12 = (f32[144,128]{1,0:T(8,128)S(1)}, f32[144,128]{1,0:T(8,128)S(1)}, u32[]{:S(2)}, u32[]{:S(2)}) collective-permute-start(f32[144,128]{1,0:T(8,128)S(1)} %get-tuple-element.106), channel_id=1, source_target_pairs={{0,1},{1,0},{2,3},{3,2},{4,5},{5,4},{6,7},{7,6},{8,9},{9,8},{10,11... | collective-permute-start | bytes 221192 | tf_op jit(solution)/shard_map/ppermute | solution.py:709
  29.7 6.2 %collective-permute-start.10 = (f32[160,128]{1,0:T(8,128)S(1)}, f32[160,128]{1,0:T(8,128)S(1)}, u32[]{:S(2)}, u32[]{:S(2)}) collective-permute-start(f32[160,128]{1,0:T(8,128)S(1)} %get-tuple-element.103), channel_id=1, source_target_pairs={{0,2},{2,0},{4,6},{6,4},{8,10},{10,8},{12,14},{14,12},{1,3},{3,1},... | collective-permute-start | bytes 245768 | tf_op jit(solution)/shard_map/ppermute | solution.py:698
  30.3 7.6 %collective-permute-start.11 = (f32[160,128]{1,0:T(8,128)S(1)}, f32[160,128]{1,0:T(8,128)S(1)}, u32[]{:S(2)}, u32[]{:S(2)}) collective-permute-start(f32[160,128]{1,0:T(8,128)S(1)} %get-tuple-element.104), channel_id=1, source_target_pairs={{2,4},{4,2},{6,8},{8,6},{10,12},{12,10},{14,0},{0,14},{3,5},{5,3},... | collective-permute-start | bytes 245768 | tf_op jit(solution)/shard_map/ppermute | solution.py:699
  33.2 5.5 %collective-permute-start.14 = (f32[32,128]{1,0:T(8,128)S(1)}, f32[32,128]{1,0:T(8,128)S(1)}, u32[]{:S(2)}, u32[]{:S(2)}) collective-permute-start(f32[32,128]{1,0:T(8,128)S(1)} %get-tuple-element.107), channel_id=1, source_target_pairs={{4,8},{8,4},{6,10},{10,6},{12,0},{0,12},{14,2},{2,14},{5,9},{9,5},... | collective-permute-start | bytes 49160 | tf_op jit(solution)/shard_map/ppermute | solution.py:705
  33.4 5.4 %collective-permute-start.13 = (f32[32,128]{1,0:T(8,128)S(1)}, f32[32,128]{1,0:T(8,128)S(1)}, u32[]{:S(2)}, u32[]{:S(2)}) collective-permute-start(f32[32,128]{1,0:T(8,128)S(1)} %get-tuple-element.107), channel_id=1, source_target_pairs={{0,4},{4,0},{2,6},{6,2},{8,12},{12,8},{10,14},{14,10},{1,5},{5,1},... | collective-permute-start | bytes 49160 | tf_op jit(solution)/shard_map/ppermute | solution.py:704
  39.7 3.6 %collective-permute-start.17 = (f32[144,128]{1,0:T(8,128)S(1)}, f32[144,128]{1,0:T(8,128)S(1)}, u32[]{:S(2)}, u32[]{:S(2)}) collective-permute-start(f32[144,128]{1,0:T(8,128)S(1)} %get-tuple-element.120), channel_id=1, source_target_pairs={{0,1},{1,0},{2,3},{3,2},{4,5},{5,4},{6,7},{7,6},{8,9},{9,8},{10,11... | collective-permute-start | bytes 221192 | tf_op jit(solution)/shard_map/ppermute | solution.py:709
  39.8 5.9 %collective-permute-start.15 = (f32[160,128]{1,0:T(8,128)S(1)}, f32[160,128]{1,0:T(8,128)S(1)}, u32[]{:S(2)}, u32[]{:S(2)}) collective-permute-start(f32[160,128]{1,0:T(8,128)S(1)} %get-tuple-element.117), channel_id=1, source_target_pairs={{0,2},{2,0},{4,6},{6,4},{8,10},{10,8},{12,14},{14,12},{1,3},{3,1},... | collective-permute-start | bytes 245768 | tf_op jit(solution)/shard_map/ppermute | solution.py:698
  40.4 7.6 %collective-permute-start.16 = (f32[160,128]{1,0:T(8,128)S(1)}, f32[160,128]{1,0:T(8,128)S(1)}, u32[]{:S(2)}, u32[]{:S(2)}) collective-permute-start(f32[160,128]{1,0:T(8,128)S(1)} %get-tuple-element.118), channel_id=1, source_target_pairs={{2,4},{4,2},{6,8},{8,6},{10,12},{12,10},{14,0},{0,14},{3,5},{5,3},... | collective-permute-start | bytes 245768 | tf_op jit(solution)/shard_map/ppermute | solution.py:699
  43.4 5.5 %collective-permute-start.19 = (f32[32,128]{1,0:T(8,128)S(1)}, f32[32,128]{1,0:T(8,128)S(1)}, u32[]{:S(2)}, u32[]{:S(2)}) collective-permute-start(f32[32,128]{1,0:T(8,128)S(1)} %get-tuple-element.121), channel_id=1, source_target_pairs={{4,8},{8,4},{6,10},{10,6},{12,0},{0,12},{14,2},{2,14},{5,9},{9,5},... | collective-permute-start | bytes 49160 | tf_op jit(solution)/shard_map/ppermute | solution.py:705
  43.9 4.9 %collective-permute-start.18 = (f32[32,128]{1,0:T(8,128)S(1)}, f32[32,128]{1,0:T(8,128)S(1)}, u32[]{:S(2)}, u32[]{:S(2)}) collective-permute-start(f32[32,128]{1,0:T(8,128)S(1)} %get-tuple-element.121), channel_id=1, source_target_pairs={{0,4},{4,0},{2,6},{6,2},{8,12},{12,8},{10,14},{14,10},{1,5},{5,1},... | collective-permute-start | bytes 49160 | tf_op jit(solution)/shard_map/ppermute | solution.py:704

commit v3 on v2

--- a/solution.py
+++ b/solution.py
@@ -27,6 +27,13 @@
     dims = (((1,), (1 if transposed else 0,)), ((), ()))
     out = lax.dot_general(split3(x), table, dims, preferred_element_type=F32)
     return out[:rows] + out[rows : 2 * rows] + out[2 * rows :]
+
+
+def fetch(sources, targets, sems):
+    copies = [pltpu.make_async_copy(a, b, sems.at[k]) for k, (a, b) in enumerate(zip(sources, targets))]
+    for copy in copies:
+        copy.start()
+    return copies
 
 
 class Place:
@@ -86,10 +93,10 @@
 
 
 def opening_kernel(
-    perm_table_ref,
-    class_ref,
-    aperture_ref,
-    slots_ref,
+    perm_table_hbm,
+    class_hbm,
+    aperture_hbm,
+    slots_hbm,
     perm_ref,
     cond_ref,
     oslot_ref,
@@ -97,7 +104,19 @@
     near_b_ref,
     far_ref,
     border_ref,
+    perm_table_ref,
+    class_ref,
+    aperture_ref,
+    slots_ref,
+    sems,
 ):
+    copies = fetch(
+        (class_hbm, perm_table_hbm, aperture_hbm, slots_hbm),
+        (class_ref, perm_table_ref, aperture_ref, slots_ref),
+        sems,
+    )
+    for copy in copies:
+        copy.wait()
     x_cells, y_cells = class_ref.shape
     half = aperture_ref.shape[0]
     here = Place()
@@ -187,17 +206,22 @@
 
 
 def inside_kernel(
-    ov_count_ref,
+    ov_count_hbm,
+    isect_count_hbm,
+    storage_hbm,
+    source_hbm,
+    source_f_hbm,
+    cell_hbm,
+    ov_weight_hbm,
+    local_hbm,
+    other_hbm,
+    frac_hbm,
     perm_ref,
     border_ref,
-    storage_ref,
-    source_ref,
-    cell_ref,
-    ov_weight_ref,
-    local_ref,
-    other_in_ref,
-    frac_ref,
     oslot_ref,
+    source_f_ref,
+    live_ref,
+    edge_ref,
     coef_ref,
     oy_ref,
     ox_ref,
@@ -210,11 +234,48 @@
     v_ref,
     margin_ref,
     column_ref,
+    ov_count_ref,
+    isect_count_ref,
+    storage_ref,
+    source_ref,
+    cell_ref,
+    ov_weight_ref,
+    local_ref,
+    other_in_ref,
+    frac_ref,
+    sems,
 ):
     members, x_cells, y_cells = source_ref.shape
     frac_cells = table_ref.shape[0]
     here = Place()
     high_side = here.high_side
+    copies = fetch(
+        (
+            cell_hbm,
+            local_hbm,
+            other_hbm,
+            frac_hbm,
+            ov_weight_hbm,
+            ov_count_hbm,
+            isect_count_hbm,
+            storage_hbm,
+            source_f_hbm,
+            source_hbm,
+        ),
+        (
+            cell_ref,
+            local_ref,
+            other_in_ref,
+            frac_ref,
+            ov_weight_ref,
+            ov_count_ref,
+            isect_count_ref,
+            storage_ref,
+            source_f_ref,
+            source_ref,
+        ),
+        sems,
+    )
 
     def line(ref):
         return jnp.concatenate([ref[k : k + 1, :] for k in range(ref.shape[0])], axis=1)
@@ -232,6 +293,8 @@
     west = jnp.concatenate([perm[-1:], perm[:-1]], axis=0)
     te = jnp.where(row == x_cells - 1, 0.0, harmonic(perm, east))
     tw = jnp.where(row == 0, 0.0, harmonic(perm, west))
+    for copy in copies[:-1]:
+        copy.wait()
     cell = line(cell_ref)
     oy = one_hot(cell % y_cells, y_cells)
     oy_ref[...] = oy
@@ -245,6 +308,9 @@
         axis=1,
     )
     weight_ref[...] = weight
+    for block in range(local_ref.shape[0]):
+        at = slice(block * LANES, (block + 1) * LANES)
+        live_ref[:, at] = jnp.where(lane_w < isect_count_ref[block], 1.0, 0.0)
     part = storage_ref[...] + te + tw + tn + ts + pick(jnp.where(at_x, weight, 0.0), oy, True)
     coef_ref[0] = te
     coef_ref[1] = tw
@@ -265,6 +331,9 @@
     inner_x = jnp.where((row_x == 0) | (row_x == x_cells - 1), 0.0, ox)
     lane_c = lax.broadcasted_iota(jnp.int32, (x_cells, LANES), 1)
     column_ref[...] = jnp.zeros_like(column_ref)
+    copies[-1].wait()
+    edge_ref[0] = source_ref[:, x_cells - 1, :]
+    edge_ref[1] = source_ref[:, 0, :]
 
     @pl.loop(0, members // GROUP)
     def _(index):
@@ -282,11 +351,11 @@
 
 
 def first_kernel(
-    count_ref,
+    live_ref,
     coef_ref,
     perm_ref,
     cond_ref,
-    source_ref,
+    edge_ref,
     source_f_ref,
     weight_ref,
     near_a_ref,
@@ -316,7 +385,7 @@
     v_ref,
     work_ref,
 ):
-    members, x_cells, y_cells = source_ref.shape
+    members, x_cells, y_cells = v_ref.shape
     half, frac_cells = source_f_ref.shape
     blocks = y_cells // LANES
     here = Place()
@@ -329,12 +398,7 @@
     cond = cond_ref[...]
     cond_first = pick(cond, first_ref[...])
     cond_second = pick(cond, second_ref[...]) + pick(ghosts, ghost_table)
-    lane = lax.broadcasted_iota(jnp.int32, cond_first.shape, 1)
-    live = jnp.zeros(cond_first.shape, jnp.bool_)
-    for block in range(cond_first.shape[1] // LANES):
-        start = block * LANES
-        live = live | ((lane >= start) & (lane < start + count_ref[block]))
-    sr = jnp.where(live, harmonic(cond_first, cond_second), 0.0)
+    sr = jnp.where(live_ref[...] > 0.0, harmonic(cond_first, cond_second), 0.0)
     sr_ref[...] = sr
     diag_f = FRACTURE_STORAGE + pick(sr, first_ref[...], True)
     inverse_f = 1.0 / diag_f
@@ -364,8 +428,8 @@
     unit_ref[3] = coef_ref[3] * inverse
     unit_ref[4] = inverse
     unit_ref[5] = diag
-    high_rows = source_ref[:, x_cells - 1, :] * inverse[x_cells - 1 :]
-    low_rows = source_ref[:, 0, :] * inverse[:1]
+    high_rows = edge_ref[0] * inverse[x_cells - 1 :]
+    low_rows = edge_ref[1] * inverse[:1]
     v_ref[:, x_cells - 1, :] = high_rows
     v_ref[:, 0, :] = low_rows
     to_a_ref[0:base, :] = to_blocks(jnp.where(here.even, high_rows, low_rows))
@@ -593,7 +657,7 @@
     send_core(core_ref, next_f, margin, weight_ref[...], ofrac_ref[...], column, j, work_ref, wown_ref)
 
 
-def close_kernel(totals_ref, v0_ref, v1_ref, v2_ref, f0_ref, f1_ref, f2_ref, x_ref, xf_ref, c_ref):
+def close_kernel(totals_ref, v0_ref, v1_ref, v2_ref, f0_ref, f1_ref, f2_ref, x_hbm, xf_hbm, c_ref, x_ref, xf_ref, sems):
     members, x_cells, y_cells = v0_ref.shape
     half, frac_cells = f0_ref.shape
 
@@ -633,14 +697,25 @@
         + wide(2, own, frac_cells) * f2_ref[...]
     )
 
-    @pl.loop(0, members)
-    def _(m):
-        rows = pl.ds(m, 1)
-        x_ref[m] = (
-            wide(0, rows, y_cells) * v0_ref[m]
-            + wide(1, rows, y_cells) * v1_ref[m]
-            + wide(2, rows, y_cells) * v2_ref[m]
-        )
+    copies = fetch((xf_ref,), (xf_hbm,), sems)
+    pieces = sems.shape[0] - 1
+    piece = members // pieces
+    for index in range(pieces):
+
+        @pl.loop(index * piece, (index + 1) * piece)
+        def _(m):
+            rows = pl.ds(m, 1)
+            x_ref[m] = (
+                wide(0, rows, y_cells) * v0_ref[m]
+                + wide(1, rows, y_cells) * v1_ref[m]
+                + wide(2, rows, y_cells) * v2_ref[m]
+            )
+
+        part = pl.ds(index * piece, piece)
+        copies.append(pltpu.make_async_copy(x_ref.at[part], x_hbm.at[part], sems.at[1 + index]))
+        copies[-1].start()
+    for copy in copies:
+        copy.wait()
 
 
 def pairs_of(count, stride, phase):
@@ -653,16 +728,19 @@
 
 
 VMEM = pl.BlockSpec(memory_space=pltpu.VMEM)
-SMEM = pl.BlockSpec(memory_space=pltpu.SMEM)
-
-
-def call(kernel, name, args, outs, scratch=(), scalars=0, cost=None, aliases=None):
+
+
+HBM = pl.BlockSpec(memory_space=pltpu.HBM)
+
+
+def call(kernel, name, args, outs, scratch=(), far_in=0, far_out=False, cost=None, aliases=None):
+    args = [pltpu.with_memory_space_constraint(arg, pltpu.HBM) for arg in args[:far_in]] + list(args[far_in:])
     return pl.pallas_call(
         kernel,
         name=name,
         out_shape=[jax.ShapeDtypeStruct(shape, dtype) for shape, dtype in outs],
-        in_specs=[SMEM] * scalars + [VMEM] * (len(args) - scalars),
-        out_specs=[VMEM] * len(outs),
+        in_specs=[HBM] * far_in + [VMEM] * (len(args) - far_in),
+        out_specs=[HBM if far_out else VMEM] * len(outs),
         scratch_shapes=list(scratch),
         compiler_params=pltpu.CompilerParams(vmem_limit_bytes=40 * 1024 * 1024),
         cost_estimate=cost,
@@ -726,7 +804,14 @@
             ((half, slots), F32),
             ((x_cells, LANES), F32),
         ],
-        scalars=1,
+        scratch=[
+            pltpu.SMEM(class_perm.shape, F32),
+            pltpu.VMEM(perm_class.shape, jnp.int32),
+            pltpu.VMEM(aperture.shape, F32),
+            pltpu.VMEM(send_slots.shape, jnp.int32),
+            pltpu.SemaphoreType.DMA((4,)),
+        ],
+        far_in=4,
     )
 
     def exchange(to_a, to_b, sent, to_core):
@@ -737,23 +822,28 @@
         return near_a, near_b, far_c, far_d, core_in
 
     near_a, near_b, far_c, far_d, border = exchange(to_a, to_b, sent, border)
-    coef, oy, ox, weight, first, second, table, ghost_table, ofrac, v0, margin_in, column = call(
+    source_f, live, edges, coef, oy, ox, weight, first, second, table, ghost_table, ofrac, v0, margin_in, column = call(
         inside_kernel,
         "inside",
         (
             ov_count.reshape(-1),
-            perm,
-            border,
+            isect_count,
             storage,
             source_matrix,
+            source_fracture,
             ov_cell.reshape(-1, LANES),
             ov_weight.reshape(-1, LANES),
             isect_local,
             isect_other,
             ov_frac.reshape(-1, LANES),
+            perm,
+            border,
             oslot,
         ),
         [
+            (own, F32),
+            ((1, rows), F32),
+            ((2, members, y_cells), F32),
             ((5, x_cells, y_cells), F32),
             ((y_cells, margin), BF16),
             ((x_cells, margin), F32),
@@ -767,7 +857,19 @@
             ((members, margin), F32),
             ((x_cells, LANES), F32),
         ],
-        scalars=1,
+        scratch=[
+            pltpu.SMEM((ov_count.size,), jnp.int32),
+            pltpu.SMEM(isect_count.shape, jnp.int32),
+            pltpu.VMEM(storage.shape, F32),
+            pltpu.VMEM(field, F32),
+            pltpu.VMEM((margin // LANES, LANES), jnp.int32),
+            pltpu.VMEM((margin // LANES, LANES), F32),
+            pltpu.VMEM(isect_local.shape, jnp.int32),
+            pltpu.VMEM(isect_other.shape, jnp.int32),
+            pltpu.VMEM((margin // LANES, LANES), jnp.int32),
+            pltpu.SemaphoreType.DMA((10,)),
+        ],
+        far_in=10,
         cost=hidden,
     )
     core_rows = 2 * frac_blocks * half + x_cells
@@ -776,12 +878,12 @@
         first_kernel,
         "first_vector",
         (
-            isect_count,
+            live,
             coef,
             perm,
             cond,
-            source_matrix,
-            source_fracture,
+            edges,
+            source_f,
             weight,
             near_a,
             near_b,
@@ -812,7 +914,6 @@
             (field, F32),
         ],
         scratch=[pltpu.VMEM((members, frac_cells), F32)],
-        scalars=1,
         aliases={20: 10},
     )
     near_rows = edge_rows + 2 * half
@@ -882,7 +983,13 @@
         "iterate",
         (totals, v0, v1, v2, f0, f1, f2),
         [(field, F32), (own, F32)],
-        scratch=[pltpu.VMEM((3, LANES, LANES), F32)],
+        scratch=[
+            pltpu.VMEM((3, LANES, LANES), F32),
+            pltpu.VMEM(field, F32),
+            pltpu.VMEM(own, F32),
+            pltpu.SemaphoreType.DMA((5,)),
+        ],
+        far_out=True,
     )
 
 

time: 61.3 us -> 56.6 us (0.923)
  local copies, waits for them, and re-layouts: 5.4 us -> 0 us
  waiting for transfers between devices: 8.84 us -> 11.1 us
  starting transfers between devices: 21.2 us -> 19.9 us
    unnamed x30 -> x0, local copies, waits for them, and re-layouts: 5.4 us -> none
    ppermute x4, waiting for transfers between devices: 3.08 us -> 5.68 us  [far(): lax.ppermute(value, 'gx', pairs_of(count, 2, 1))]
    ppermute x4, starting transfers between devices: 4.96 us -> 3.28 us  [near(): lax.ppermute(to_a, 'gx', pairs_of(count, 1, 0))]
    ppermute x4, starting transfers between devices: 12.1 us -> 13.5 us  [near(): lax.ppermute(to_b, 'gx', pairs_of(count, 1, 1))]
    ppermute x4, starting transfers between devices: 3.25 us -> 2.37 us  [far(): lax.ppermute(value, 'gx', pairs_of(count, 2, 1))]
  transfers between devices with their start and end apart: 20 -> 20, of which waited for: 8 -> 7; matrix products, arithmetic and copies ran while one was open for 0% -> 0% of each run, Pallas kernels for 13% -> 15%
where the time goes in v3:
time: 56.6 us; the launch traced here: 56.4 us
  starting transfers between devices  19.9 us (35%)
  Pallas kernels  14.9 us (26%)
  waiting for transfers between devices  11.1 us (20%)
  blocking collectives  9.77 us (17%)
  between operations  0.76 us (1%)
    pallas_call x10, Pallas kernels, call(): pl.pallas_call(kernel, name=name, out_shape=[jax.ShapeDtypeStruct(shape,...  14.9 us
    ppermute x4, starting transfers between devices, near(): lax.ppermute(to_b, 'gx', pairs_of(count, 1, 1))  13.5 us
    all_to_all x1, blocking collectives, per_device(): totals = lax.all_to_all(moments, ('gx', 'gy'), 0, 0)  9.77 us
    ppermute x4, waiting for transfers between devices, far(): lax.ppermute(value, 'gx', pairs_of(count, 2, 1))  5.68 us
    ppermute x4, waiting for transfers between devices, near(): lax.ppermute(to_b, 'gx', pairs_of(count, 1, 1))  5.41 us
    ppermute x4, starting transfers between devices, near(): lax.ppermute(to_a, 'gx', pairs_of(count, 1, 0))  3.28 us
    ppermute x4, starting transfers between devices, far(): lax.ppermute(value, 'gx', pairs_of(count, 2, 1))  2.37 us
  transfers between devices with their start and end apart: 20, of which 7 were waited for; matrix products, arithmetic and copies ran while one was open for 0% of the time, Pallas kernels for 15%

profile of v3, /device:TPU:0, one launch (start us, length us, event | category | flops | bytes accessed | tf_op | source)
XLA Modules:
  0.0 56.4 jit_solution(8388201563464189559)
XLA Ops:
  0.6 1.0 %opening.1 = (f32[16,512]{1,0:T(8,128)S(1)}, f32[16,512]{1,0:T(8,128)S(1)}, bf16[512,128]{1,0:T(8,128)(2,1)S(1)}, f32[24,128]{1,0:T(8,128)S(1)}, f32[24,128]{1,0...) custom-call(f32[8]{0:T(128)} %perm_table_hbm.1, s32[16,512]{1,0:T(8,128)} %class_hbm.1, ...), custom_call_target="tpu_custom_call" | custom-call | tf_op jit(solution)/shard_map/opening/pallas_call | solution.py:738
  1.7 0.5 collective-permute-start
  2.2 2.6 %collective-permute-start.1 = (f32[24,128]{1,0:T(8,128)S(1)}, f32[24,128]{1,0:T(8,128)S(1)}, u32[]{:S(2)}, u32[]{:S(2)}) collective-permute-start(f32[24,128]{1,0:T(8,128)S(1)} %get-tuple-element.79), channel_id=1, source_target_pairs={{0,2},{2,0},{4,6},{6,4},{8,10},{10,8},{12,14},{14,12},{1,3},{3,1},... | collective-permute-start | bytes 36872 | tf_op jit(solution)/shard_map/ppermute | solution.py:776
  4.7 3.6 %collective-permute-start.2 = (f32[24,128]{1,0:T(8,128)S(1)}, f32[24,128]{1,0:T(8,128)S(1)}, u32[]{:S(2)}, u32[]{:S(2)}) collective-permute-start(f32[24,128]{1,0:T(8,128)S(1)} %get-tuple-element.80), channel_id=1, source_target_pairs={{2,4},{4,2},{6,8},{8,6},{10,12},{12,10},{14,0},{0,14},{3,5},{5,3},... | collective-permute-start | bytes 36872 | tf_op jit(solution)/shard_map/ppermute | solution.py:777
  8.3 0.0 collective-permute-done.border_ref
  8.3 0.5 collective-permute-start.4
  8.8 0.0 collective-permute-start.3
  8.8 2.5 %inside.1 = (f32[16,512]{1,0:T(8,128)S(1)}, f32[1,512]{1,0:T(1,128)S(1)}, f32[2,32,512]{2,1,0:T(8,128)S(1)}, f32[5,16,512]{2,1,0:T(8,128)S(1)}, bf16[512,256]{1,...) custom-call(s32[2]{0:T(128)} %bitcast.7, ...), custom_call_target="tpu_custom_call" | custom-call | flops 4000000000 | bytes 12000000 | tf_op jit(solution)/shard_map/inside/pallas_call | solution.py:738
  11.2 0.0 collective-permute-done.1.near_a_ref
  11.2 0.0 collective-permute-done.2.near_b_ref
  11.2 2.5 %collective-permute-done.4.far_d_ref = f32[16,128]{1,0:T(8,128)S(1)} collective-permute-done((f32[16,128]{1,0:T(8,128)S(1)}, f32[16,128]{1,0:T(8,128)S(1)}, u32[]{:S(2)}, u32[]{:S(2)}) %collective-permute-start.4) | collective-permute-done | bytes 8224 | tf_op jit(solution)/shard_map/ppermute | solution.py:783
  13.8 0.0 collective-permute-done.3.far_c_ref
  13.8 1.3 %first_vector.1 = (f32[6,16,512]{2,1,0:T(8,128)S(1)}, f32[16,512]{1,0:T(8,128)S(1)}, f32[16,512]{1,0:T(8,128)S(1)}, f32[2,16,512]{2,1,0:T(8,128)S(1)}, f32[16,51...) custom-call(f32[1,512]{1,0:T(1,128)S(1)} %get-tuple-element.73.live_, ...), custom_call_target="tpu_custom_call", output_to_operand_aliasing={{10}: (20, {})} | custom-call | tf_op jit(solution)/shard_map/first_vector/pallas_call | solution.py:738
  15.1 0.0 collective-permute-start.7
  15.1 0.1 collective-permute-start.5
  15.2 3.5 %collective-permute-start.6 = (f32[176,128]{1,0:T(8,128)S(1)}, f32[176,128]{1,0:T(8,128)S(1)}, u32[]{:S(2)}, u32[]{:S(2)}) collective-permute-start(f32[176,128]{1,0:T(8,128)S(1)} %get-tuple-element.94), channel_id=1, source_target_pairs={{2,4},{4,2},{6,8},{8,6},{10,12},{12,10},{14,0},{0,14},{3,5},{5,3},... | collective-permute-start | bytes 270344 | tf_op jit(solution)/shard_map/ppermute | solution.py:777
  18.7 0.0 collective-permute-done.7.core_ref.core_in_ref
  18.7 0.9 %collective-permute-start.9 = (f32[48,128]{1,0:T(8,128)S(1)}, f32[48,128]{1,0:T(8,128)S(1)}, u32[]{:S(2)}, u32[]{:S(2)}) collective-permute-start(f32[48,128]{1,0:T(8,128)S(1)} %get-tuple-element.97), channel_id=1, source_target_pairs={{4,8},{8,4},{6,10},{10,6},{12,0},{0,12},{14,2},{2,14},{5,9},{9,5},... | collective-permute-start | bytes 73736 | tf_op jit(solution)/shard_map/ppermute | solution.py:783
  19.6 0.0 collective-permute-start.8
  19.6 2.2 %interior_1.1 = (f32[32,16,512]{2,1,0:T(8,128)S(1)}, f32[32,256]{1,0:T(8,128)S(1)}, f32[16,128]{1,0:T(8,128)S(1)}, f32[8,32]{1,0:T(8,128)S(1)}) custom-call(f32[32,16,512]{2,1,0:T(8,128)S(1)} %get-tuple-element.104.v_ref.before_ref.v0_ref, f32[32,16,512]{2,1,0:T(8,128)S(1)} %get-tuple-element.104.v_ref.before_ref.v0_ref, ...), custom_call_target="tpu_custom_call" | custom-call | flops 4000000000 | bytes 12000000 | tf_op jit(solution)/shard_map/interior_1/pallas_call | solution.py:738
  21.8 0.0 collective-permute-done.5.near_a_ref
  21.8 1.6 %collective-permute-done.6.near_b_ref = f32[176,128]{1,0:T(8,128)S(1)} collective-permute-done((f32[176,128]{1,0:T(8,128)S(1)}, f32[176,128]{1,0:T(8,128)S(1)}, u32[]{:S(2)}, u32[]{:S(2)}) %collective-permute-start.6) | collective-permute-done | bytes 90144 | tf_op jit(solution)/shard_map/ppermute | solution.py:777
  23.4 0.9 %collective-permute-done.9.far_d_ref = f32[48,128]{1,0:T(8,128)S(1)} collective-permute-done((f32[48,128]{1,0:T(8,128)S(1)}, f32[48,128]{1,0:T(8,128)S(1)}, u32[]{:S(2)}, u32[]{:S(2)}) %collective-permute-start.9) | collective-permute-done | bytes 24608 | tf_op jit(solution)/shard_map/ppermute | solution.py:783
  24.3 0.0 collective-permute-done.8.far_c_ref
  24.3 1.0 %finish_1.1 = (f32[16,512]{1,0:T(8,128)S(1)}, f32[16,512]{1,0:T(8,128)S(1)}, f32[16,512]{1,0:T(8,128)S(1)}, f32[16,512]{1,0:T(8,128)S(1)}, f32[160,128]{1,0:T(8,...) custom-call(f32[16,512]{1,0:T(8,128)S(1)} %get-tuple-element.92.vf_r, ...), custom_call_target="tpu_custom_call", output_to_operand_aliasing={{8}: (19, {})} | custom-call | tf_op jit(solution)/shard_map/finish_1/pallas_call | solution.py:738
  25.3 0.1 collective-permute-start.12
  25.4 0.3 collective-permute-start.10
  25.7 3.2 %collective-permute-start.11 = (f32[160,128]{1,0:T(8,128)S(1)}, f32[160,128]{1,0:T(8,128)S(1)}, u32[]{:S(2)}, u32[]{:S(2)}) collective-permute-start(f32[160,128]{1,0:T(8,128)S(1)} %get-tuple-element.110), channel_id=1, source_target_pairs={{2,4},{4,2},{6,8},{8,6},{10,12},{12,10},{14,0},{0,14},{3,5},{5,3},... | collective-permute-start | bytes 245768 | tf_op jit(solution)/shard_map/ppermute | solution.py:777
  29.0 0.0 collective-permute-done.12.core_ref.core_in_ref
  29.0 0.4 collective-permute-start.14
  29.4 0.0 collective-permute-start.13
  29.4 2.2 %interior_2.1 = (f32[32,16,512]{2,1,0:T(8,128)S(1)}, f32[32,256]{1,0:T(8,128)S(1)}, f32[16,128]{1,0:T(8,128)S(1)}, f32[8,32]{1,0:T(8,128)S(1)}) custom-call(f32[32,16,512]{2,1,0:T(8,128)S(1)} %get-tuple-element.118.v_ref.before_ref.v1_ref, f32[32,16,512]{2,1,0:T(8,128)S(1)} %get-tuple-element.104.v_ref.before_ref.v0_ref, ...), custom_call_target="tpu_custom_call" | custom-call | flops 4000000000 | bytes 12000000 | tf_op jit(solution)/shard_map/interior_2/pallas_call | solution.py:738
  31.7 0.0 collective-permute-done.10.near_a_ref
  31.7 1.7 %collective-permute-done.11.near_b_ref = f32[160,128]{1,0:T(8,128)S(1)} collective-permute-done((f32[160,128]{1,0:T(8,128)S(1)}, f32[160,128]{1,0:T(8,128)S(1)}, u32[]{:S(2)}, u32[]{:S(2)}) %collective-permute-start.11) | collective-permute-done | bytes 81952 | tf_op jit(solution)/shard_map/ppermute | solution.py:777
  33.4 1.1 %collective-permute-done.14.far_d_ref = f32[32,128]{1,0:T(8,128)S(1)} collective-permute-done((f32[32,128]{1,0:T(8,128)S(1)}, f32[32,128]{1,0:T(8,128)S(1)}, u32[]{:S(2)}, u32[]{:S(2)}) %collective-permute-start.14) | collective-permute-done | bytes 16416 | tf_op jit(solution)/shard_map/ppermute | solution.py:783
  34.5 0.0 collective-permute-done.13.far_c_ref
  34.5 0.9 %finish_2.1 = (f32[16,512]{1,0:T(8,128)S(1)}, f32[16,512]{1,0:T(8,128)S(1)}, f32[16,512]{1,0:T(8,128)S(1)}, f32[160,128]{1,0:T(8,128)S(1)}, f32[160,128]{1,0:T(8...) custom-call(f32[16,512]{1,0:T(8,128)S(1)} %get-tuple-element.108.vf_, ...), custom_call_target="tpu_custom_call", output_to_operand_aliasing={{7}: (20, {})} | custom-call | tf_op jit(solution)/shard_map/finish_2/pallas_call | solution.py:738
  35.4 0.1 collective-permute-start.17
  35.5 0.3 collective-permute-start.15
  35.8 3.2 %collective-permute-start.16 = (f32[160,128]{1,0:T(8,128)S(1)}, f32[160,128]{1,0:T(8,128)S(1)}, u32[]{:S(2)}, u32[]{:S(2)}) collective-permute-start(f32[160,128]{1,0:T(8,128)S(1)} %get-tuple-element.124), channel_id=1, source_target_pairs={{2,4},{4,2},{6,8},{8,6},{10,12},{12,10},{14,0},{0,14},{3,5},{5,3},... | collective-permute-start | bytes 245768 | tf_op jit(solution)/shard_map/ppermute | solution.py:777
  39.1 0.0 collective-permute-done.17.core_ref.core_in_ref
  39.1 0.6 %collective-permute-start.19 = (f32[32,128]{1,0:T(8,128)S(1)}, f32[32,128]{1,0:T(8,128)S(1)}, u32[]{:S(2)}, u32[]{:S(2)}) collective-permute-start(f32[32,128]{1,0:T(8,128)S(1)} %get-tuple-element.127), channel_id=1, source_target_pairs={{4,8},{8,4},{6,10},{10,6},{12,0},{0,12},{14,2},{2,14},{5,9},{9,5},... | collective-permute-start | bytes 49160 | tf_op jit(solution)/shard_map/ppermute | solution.py:783
  39.7 0.0 collective-permute-start.18
  39.7 1.7 %interior_3.1.refs_4_ = f32[8,32]{1,0:T(8,128)S(1)} custom-call(f32[32,16,512]{2,1,0:T(8,128)S(1)} %get-tuple-element.131.v_ref.refs_1_.v2_ref, f32[32,16,512]{2,1,0:T(8,128)S(1)} %get-tuple-element.118.v_ref.before_ref.v1_ref, f32[16,512]{1,0:T(8,128)S(1)} %get-tuple-element.122.vf_ref.f2_ref, f32[16,512]{1,0:T(8,128)S(1)} %get-tuple-element.108.vf_ref.before_f_ref.f1_ref, ...), custom_call_target="tpu_custom_call" | custom-call | flops 4000000000 | bytes 12000000 | tf_op jit(solution)/shard_map/interior_3/pallas_call | solution.py:738
  41.4 0.0 collective-permute-done.15.near_a_ref
  41.4 2.1 %collective-permute-done.16.near_b_ref = f32[160,128]{1,0:T(8,128)S(1)} collective-permute-done((f32[160,128]{1,0:T(8,128)S(1)}, f32[160,128]{1,0:T(8,128)S(1)}, u32[]{:S(2)}, u32[]{:S(2)}) %collective-permute-start.16) | collective-permute-done | bytes 81952 | tf_op jit(solution)/shard_map/ppermute | solution.py:777
  43.5 1.1 %collective-permute-done.19.far_d_ref = f32[32,128]{1,0:T(8,128)S(1)} collective-permute-done((f32[32,128]{1,0:T(8,128)S(1)}, f32[32,128]{1,0:T(8,128)S(1)}, u32[]{:S(2)}, u32[]{:S(2)}) %collective-permute-start.19) | collective-permute-done | bytes 16416 | tf_op jit(solution)/shard_map/ppermute | solution.py:783
  44.6 0.0 collective-permute-done.18.far_c_ref
  44.6 0.6 %finish_3.1 = f32[16,2,128]{2,1,0:T(2,128)S(1)} custom-call(f32[16,512]{1,0:T(8,128)S(1)} %get-tuple-element.122.vf_ref.f2_ref, f32[160,128]{1,0:T(8,128)S(1)} %collective-permute-done.15.near_a_ref, f32[160,128]{1,0:T(8,128)S(1)} %collective-permute-done.16.near_b_ref, f32[32,128]{1,0:T(8,128)S(1)} %collective-permute-done.18.far_c_ref, ...), custom_call_target="tpu_custom_call" | custom-call | tf_op jit(solution)/shard_map/finish_3/pallas_call | solution.py:738
  45.2 9.8 %all_to_all.5.totals_ref = f32[16,2,128]{2,1,0:T(2,128)S(1)} all-to-all(f32[16,2,128]{2,1,0:T(2,128)S(1)} %finish_3.1), channel_id=1, replica_groups=mesh['grp'=2,'gx'=8,'gy'=2] {'gx','gy'}, dimensions={0} | all-to-all | bytes 32768 | tf_op jit(solution)/shard_map/all_to_all | solution.py:980
  55.0 1.4 %iterate.1 = (f32[32,16,512]{2,1,0:T(8,128)}, f32[16,512]{1,0:T(8,128)}) custom-call(f32[16,2,128]{2,1,0:T(2,128)S(1)} %all_to_all.5.totals_ref, f32[32,16,512]{2,1,0:T(8,128)S(1)} %get-tuple-element.104.v_ref.before_ref.v0_ref, f32[32,16,512]{2,1,0:T(8,128)S(1)} %get-tuple-element.118.v_ref.before_ref.v1_ref, ...), custom_call_target="tpu_custom_call" | custom-call | tf_op jit(solution)/shard_map/iterate/pallas_call | solution.py:738
Async XLA Ops:
  1.7 6.7 %collective-permute-start = (f32[16,128]{1,0:T(8,128)S(1)}, f32[16,128]{1,0:T(8,128)S(1)}, u32[]{:S(2)}, u32[]{:S(2)}) collective-permute-start(f32[16,128]{1,0:T(8,128)S(1)} %get-tuple-element.70), channel_id=1, source_target_pairs={{0,1},{1,0},{2,3},{3,2},{4,5},{5,4},{6,7},{7,6},{8,9},{9,8},{10,11... | collective-permute-start | bytes 24584 | tf_op jit(solution)/shard_map/ppermute | solution.py:787
  2.2 9.1 %collective-permute-start.1 = (f32[24,128]{1,0:T(8,128)S(1)}, f32[24,128]{1,0:T(8,128)S(1)}, u32[]{:S(2)}, u32[]{:S(2)}) collective-permute-start(f32[24,128]{1,0:T(8,128)S(1)} %get-tuple-element.79), channel_id=1, source_target_pairs={{0,2},{2,0},{4,6},{6,4},{8,10},{10,8},{12,14},{14,12},{1,3},{3,1},... | collective-permute-start | bytes 36872 | tf_op jit(solution)/shard_map/ppermute | solution.py:776
  4.7 6.5 %collective-permute-start.2 = (f32[24,128]{1,0:T(8,128)S(1)}, f32[24,128]{1,0:T(8,128)S(1)}, u32[]{:S(2)}, u32[]{:S(2)}) collective-permute-start(f32[24,128]{1,0:T(8,128)S(1)} %get-tuple-element.80), channel_id=1, source_target_pairs={{2,4},{4,2},{6,8},{8,6},{10,12},{12,10},{14,0},{0,14},{3,5},{5,3},... | collective-permute-start | bytes 36872 | tf_op jit(solution)/shard_map/ppermute | solution.py:777
  8.3 5.4 %collective-permute-start.4 = (f32[16,128]{1,0:T(8,128)S(1)}, f32[16,128]{1,0:T(8,128)S(1)}, u32[]{:S(2)}, u32[]{:S(2)}) collective-permute-start(f32[16,128]{1,0:T(8,128)S(1)} %get-tuple-element.81), channel_id=1, source_target_pairs={{4,8},{8,4},{6,10},{10,6},{12,0},{0,12},{14,2},{2,14},{5,9},{9,5},... | collective-permute-start | bytes 24584 | tf_op jit(solution)/shard_map/ppermute | solution.py:783
  8.8 5.0 %collective-permute-start.3 = (f32[16,128]{1,0:T(8,128)S(1)}, f32[16,128]{1,0:T(8,128)S(1)}, u32[]{:S(2)}, u32[]{:S(2)}) collective-permute-start(f32[16,128]{1,0:T(8,128)S(1)} %get-tuple-element.81), channel_id=1, source_target_pairs={{0,4},{4,0},{2,6},{6,2},{8,12},{12,8},{10,14},{14,10},{1,5},{5,1},... | collective-permute-start | bytes 24584 | tf_op jit(solution)/shard_map/ppermute | solution.py:782
  15.1 3.6 %collective-permute-start.7 = (f32[176,128]{1,0:T(8,128)S(1)}, f32[176,128]{1,0:T(8,128)S(1)}, u32[]{:S(2)}, u32[]{:S(2)}) collective-permute-start(f32[176,128]{1,0:T(8,128)S(1)} %get-tuple-element.96), channel_id=1, source_target_pairs={{0,1},{1,0},{2,3},{3,2},{4,5},{5,4},{6,7},{7,6},{8,9},{9,8},{10,11... | collective-permute-start | bytes 270344 | tf_op jit(solution)/shard_map/ppermute | solution.py:787
  15.1 6.6 %collective-permute-start.5 = (f32[176,128]{1,0:T(8,128)S(1)}, f32[176,128]{1,0:T(8,128)S(1)}, u32[]{:S(2)}, u32[]{:S(2)}) collective-permute-start(f32[176,128]{1,0:T(8,128)S(1)} %get-tuple-element.93), channel_id=1, source_target_pairs={{0,2},{2,0},{4,6},{6,4},{8,10},{10,8},{12,14},{14,12},{1,3},{3,1},... | collective-permute-start | bytes 270344 | tf_op jit(solution)/shard_map/ppermute | solution.py:776
  15.2 8.2 %collective-permute-start.6 = (f32[176,128]{1,0:T(8,128)S(1)}, f32[176,128]{1,0:T(8,128)S(1)}, u32[]{:S(2)}, u32[]{:S(2)}) collective-permute-start(f32[176,128]{1,0:T(8,128)S(1)} %get-tuple-element.94), channel_id=1, source_target_pairs={{2,4},{4,2},{6,8},{8,6},{10,12},{12,10},{14,0},{0,14},{3,5},{5,3},... | collective-permute-start | bytes 270344 | tf_op jit(solution)/shard_map/ppermute | solution.py:777
  18.7 5.6 %collective-permute-start.9 = (f32[48,128]{1,0:T(8,128)S(1)}, f32[48,128]{1,0:T(8,128)S(1)}, u32[]{:S(2)}, u32[]{:S(2)}) collective-permute-start(f32[48,128]{1,0:T(8,128)S(1)} %get-tuple-element.97), channel_id=1, source_target_pairs={{4,8},{8,4},{6,10},{10,6},{12,0},{0,12},{14,2},{2,14},{5,9},{9,5},... | collective-permute-start | bytes 73736 | tf_op jit(solution)/shard_map/ppermute | solution.py:783
  19.6 4.7 %collective-permute-start.8 = (f32[48,128]{1,0:T(8,128)S(1)}, f32[48,128]{1,0:T(8,128)S(1)}, u32[]{:S(2)}, u32[]{:S(2)}) collective-permute-start(f32[48,128]{1,0:T(8,128)S(1)} %get-tuple-element.97), channel_id=1, source_target_pairs={{0,4},{4,0},{2,6},{6,2},{8,12},{12,8},{10,14},{14,10},{1,5},{5,1},... | collective-permute-start | bytes 73736 | tf_op jit(solution)/shard_map/ppermute | solution.py:782
  25.3 3.6 %collective-permute-start.12 = (f32[144,128]{1,0:T(8,128)S(1)}, f32[144,128]{1,0:T(8,128)S(1)}, u32[]{:S(2)}, u32[]{:S(2)}) collective-permute-start(f32[144,128]{1,0:T(8,128)S(1)} %get-tuple-element.112), channel_id=1, source_target_pairs={{0,1},{1,0},{2,3},{3,2},{4,5},{5,4},{6,7},{7,6},{8,9},{9,8},{10,11... | collective-permute-start | bytes 221192 | tf_op jit(solution)/shard_map/ppermute | solution.py:787
  25.4 6.2 %collective-permute-start.10 = (f32[160,128]{1,0:T(8,128)S(1)}, f32[160,128]{1,0:T(8,128)S(1)}, u32[]{:S(2)}, u32[]{:S(2)}) collective-permute-start(f32[160,128]{1,0:T(8,128)S(1)} %get-tuple-element.109), channel_id=1, source_target_pairs={{0,2},{2,0},{4,6},{6,4},{8,10},{10,8},{12,14},{14,12},{1,3},{3,1},... | collective-permute-start | bytes 245768 | tf_op jit(solution)/shard_map/ppermute | solution.py:776
  25.7 7.6 %collective-permute-start.11 = (f32[160,128]{1,0:T(8,128)S(1)}, f32[160,128]{1,0:T(8,128)S(1)}, u32[]{:S(2)}, u32[]{:S(2)}) collective-permute-start(f32[160,128]{1,0:T(8,128)S(1)} %get-tuple-element.110), channel_id=1, source_target_pairs={{2,4},{4,2},{6,8},{8,6},{10,12},{12,10},{14,0},{0,14},{3,5},{5,3},... | collective-permute-start | bytes 245768 | tf_op jit(solution)/shard_map/ppermute | solution.py:777
  29.0 5.5 %collective-permute-start.14 = (f32[32,128]{1,0:T(8,128)S(1)}, f32[32,128]{1,0:T(8,128)S(1)}, u32[]{:S(2)}, u32[]{:S(2)}) collective-permute-start(f32[32,128]{1,0:T(8,128)S(1)} %get-tuple-element.113), channel_id=1, source_target_pairs={{4,8},{8,4},{6,10},{10,6},{12,0},{0,12},{14,2},{2,14},{5,9},{9,5},... | collective-permute-start | bytes 49160 | tf_op jit(solution)/shard_map/ppermute | solution.py:783
  29.4 5.1 %collective-permute-start.13 = (f32[32,128]{1,0:T(8,128)S(1)}, f32[32,128]{1,0:T(8,128)S(1)}, u32[]{:S(2)}, u32[]{:S(2)}) collective-permute-start(f32[32,128]{1,0:T(8,128)S(1)} %get-tuple-element.113), channel_id=1, source_target_pairs={{0,4},{4,0},{2,6},{6,2},{8,12},{12,8},{10,14},{14,10},{1,5},{5,1},... | collective-permute-start | bytes 49160 | tf_op jit(solution)/shard_map/ppermute | solution.py:782
  35.4 3.6 %collective-permute-start.17 = (f32[144,128]{1,0:T(8,128)S(1)}, f32[144,128]{1,0:T(8,128)S(1)}, u32[]{:S(2)}, u32[]{:S(2)}) collective-permute-start(f32[144,128]{1,0:T(8,128)S(1)} %get-tuple-element.126), channel_id=1, source_target_pairs={{0,1},{1,0},{2,3},{3,2},{4,5},{5,4},{6,7},{7,6},{8,9},{9,8},{10,11... | collective-permute-start | bytes 221192 | tf_op jit(solution)/shard_map/ppermute | solution.py:787
  35.5 5.9 %collective-permute-start.15 = (f32[160,128]{1,0:T(8,128)S(1)}, f32[160,128]{1,0:T(8,128)S(1)}, u32[]{:S(2)}, u32[]{:S(2)}) collective-permute-start(f32[160,128]{1,0:T(8,128)S(1)} %get-tuple-element.123), channel_id=1, source_target_pairs={{0,2},{2,0},{4,6},{6,4},{8,10},{10,8},{12,14},{14,12},{1,3},{3,1},... | collective-permute-start | bytes 245768 | tf_op jit(solution)/shard_map/ppermute | solution.py:776
  35.8 7.7 %collective-permute-start.16 = (f32[160,128]{1,0:T(8,128)S(1)}, f32[160,128]{1,0:T(8,128)S(1)}, u32[]{:S(2)}, u32[]{:S(2)}) collective-permute-start(f32[160,128]{1,0:T(8,128)S(1)} %get-tuple-element.124), channel_id=1, source_target_pairs={{2,4},{4,2},{6,8},{8,6},{10,12},{12,10},{14,0},{0,14},{3,5},{5,3},... | collective-permute-start | bytes 245768 | tf_op jit(solution)/shard_map/ppermute | solution.py:777
  39.1 5.5 %collective-permute-start.19 = (f32[32,128]{1,0:T(8,128)S(1)}, f32[32,128]{1,0:T(8,128)S(1)}, u32[]{:S(2)}, u32[]{:S(2)}) collective-permute-start(f32[32,128]{1,0:T(8,128)S(1)} %get-tuple-element.127), channel_id=1, source_target_pairs={{4,8},{8,4},{6,10},{10,6},{12,0},{0,12},{14,2},{2,14},{5,9},{9,5},... | collective-permute-start | bytes 49160 | tf_op jit(solution)/shard_map/ppermute | solution.py:783
  39.7 5.0 %collective-permute-start.18 = (f32[32,128]{1,0:T(8,128)S(1)}, f32[32,128]{1,0:T(8,128)S(1)}, u32[]{:S(2)}, u32[]{:S(2)}) collective-permute-start(f32[32,128]{1,0:T(8,128)S(1)} %get-tuple-element.127), channel_id=1, source_target_pairs={{0,4},{4,0},{2,6},{6,2},{8,12},{12,8},{10,14},{14,10},{1,5},{5,1},... | collective-permute-start | bytes 49160 | tf_op jit(solution)/shard_map/ppermute | solution.py:782

commit v4 on v3

--- a/solution.py
+++ b/solution.py
@@ -185,9 +185,13 @@
 
 def send_network(vf, sr, table, ghost_table, diff_ref, refs):
     half = vf.shape[0]
-    rows = sr.shape[1]
+    rows = diff_ref.shape[1]
     found = pick(vf, table)
     diff_ref[...] = found[:, :rows]
+    if sr is None:
+        for ref, at in refs:
+            ref[at : at + half, :] = found[:, rows:]
+        return
     sums = pick(sr * found[:, :rows], ghost_table, True)
     for ref, at in refs:
         ref[at : at + half, :] = found[:, rows:]
@@ -220,6 +224,7 @@
     border_ref,
     oslot_ref,
     source_f_ref,
+    storage_ref,
     live_ref,
     edge_ref,
     coef_ref,
@@ -236,7 +241,6 @@
     column_ref,
     ov_count_ref,
     isect_count_ref,
-    storage_ref,
     source_ref,
     cell_ref,
     ov_weight_ref,
@@ -459,10 +463,7 @@
     ox_ref,
     *refs,
 ):
-    if power < 3:
-        image_ref, margin_ref, column_ref, dots_ref, flow_ref, work_ref, *acc_refs = refs
-    else:
-        dots_ref, flow_ref, work_ref, *acc_refs = refs
+    image_ref, margin_ref, column_ref, dots_ref, flow_ref, work_ref, *acc_refs = refs
     members, x_cells, y_cells = v_ref.shape
     half, frac_cells = vf_ref.shape
     blocks = y_cells // LANES
@@ -492,8 +493,7 @@
     inner_x = jnp.where((row_x == 0) | (row_x == x_cells - 1), 0.0, ox)
     te = jnp.where(row == x_cells - 1, 0.0, unit_ref[0])
     tw = jnp.where(row == 0, 0.0, unit_ref[1])
-    if power < 3:
-        column_ref[...] = jnp.zeros_like(column_ref)
+    column_ref[...] = jnp.zeros_like(column_ref)
 
     @pl.loop(0, members // GROUP)
     def _(index):
@@ -502,8 +502,7 @@
         for k in range(GROUP):
             parts.append(ox * flow_ref[pl.ds(start + k, 1), :])
         coupled = pick(jnp.concatenate(parts, axis=0), oy, True)
-        if power < 3:
-            column = column_ref[...]
+        column = column_ref[...]
         for k in range(GROUP):
             m = start + k
             value = v_ref[m]
@@ -520,17 +519,13 @@
             acc_refs[0][at, :] += jnp.sum(fold_lanes(value * heavy), axis=0, keepdims=True)
             if power > 1:
                 acc_refs[1][at, :] += jnp.sum(fold_lanes(before_ref[m] * heavy), axis=0, keepdims=True)
-            if power < 3:
-                image_ref[m] = image
-                shifted = border_column(image[:, :LANES], image[:, y_cells - LANES :], high_side, m)
-                column = jnp.where(lane_c == m, shifted, column)
-            else:
-                acc_refs[2][at, :] += jnp.sum(fold_lanes(image * heavy), axis=0, keepdims=True)
-        if power < 3:
-            column_ref[...] = column
-            block = image_ref[pl.ds(start, GROUP)]
-            found = pick(block.reshape(GROUP * x_cells, y_cells), oy)
-            margin_ref[pl.ds(start, GROUP), :] = margin_values(found, inner_x)
+            image_ref[m] = image
+            shifted = border_column(image[:, :LANES], image[:, y_cells - LANES :], high_side, m)
+            column = jnp.where(lane_c == m, shifted, column)
+        column_ref[...] = column
+        block = image_ref[pl.ds(start, GROUP)]
+        found = pick(block.reshape(GROUP * x_cells, y_cells), oy)
+        margin_ref[pl.ds(start, GROUP), :] = margin_values(found, inner_x)
 
     dots = [total_rows(ref[...]) for ref in acc_refs]
     dots.append(jnp.zeros((8 - len(dots), members), F32))
@@ -554,37 +549,16 @@
     ghost_table_ref,
     *refs,
 ):
+    if power == 2:
+        own_f_in_ref, *refs = refs
+    weight_ref, ofrac_ref, oy_ref, ox_ref, inner_margin_ref, inner_column_ref, image_in_ref, *refs = refs
     if power == 1:
-        (
-            weight_ref,
-            ofrac_ref,
-            oy_ref,
-            ox_ref,
-            inner_margin_ref,
-            inner_column_ref,
-            image_in_ref,
-            own_f_ref,
-            *refs,
-        ) = refs
-    elif power == 2:
-        (
-            own_f_in_ref,
-            weight_ref,
-            ofrac_ref,
-            oy_ref,
-            ox_ref,
-            inner_margin_ref,
-            inner_column_ref,
-            image_in_ref,
-            *refs,
-        ) = refs
-    if power < 3:
-        out_f_ref, diff_ref, wown_ref, to_a_ref, to_b_ref, sent_ref, core_ref, image_ref, work_ref = refs
+        own_f_ref, out_f_ref, diff_ref, wown_ref, to_a_ref, to_b_ref, sent_ref, core_ref, image_ref, work_ref = refs
     else:
-        own_f_in_ref, v_ref, dots1_ref, dots2_ref, dots3_ref, moments_ref, acc_ref = refs
+        out_f_ref, diff_ref, margin_ref, to_a_ref, to_b_ref, sent_ref, core_ref, image_ref = refs
     half, frac_cells = vf_ref.shape
     x_cells, y_cells = unit_ref.shape[1:]
-    members = v_ref.shape[0] if power == 3 else image_ref.shape[0]
+    members = image_ref.shape[0]
     blocks = y_cells // LANES
     frac_blocks = frac_cells // LANES
     here = Place()
@@ -619,29 +593,11 @@
     image_f = own_f * vf + pick(jnp.concatenate([flux, -sums], axis=1), table, True)
     image_f = image_f - wown_in_ref[...] - their_sums
 
-    if power == 3:
-        acc_ref[...] = jnp.zeros_like(acc_ref)
-        acc_ref[pl.ds(pl.multiple_of(j * half, half), half), :] = fold_lanes(vf * image_f)
-        for side, at, reader in ((0, x_cells - 1, plus1), (1, 0, minus1)):
-            factor = unit_ref[side, at : at + 1, :] * unit_ref[5, at : at + 1, :]
-            edge = v_ref[:, at, :] * factor
-            for q in range(blocks):
-                beyond = reader(q * members, members)
-                acc_ref[...] -= edge[:, q * LANES : (q + 1) * LANES] * beyond
-        last = total_rows(acc_ref[...]) + dots3_ref[2:3, :]
-        gap = jnp.zeros((1, LANES - 3 * members), F32)
-        lines = [
-            jnp.concatenate([dots1_ref[0:1, :], dots2_ref[1:2, :], dots2_ref[0:1, :], gap], axis=1),
-            jnp.concatenate([dots3_ref[1:2, :], dots3_ref[0:1, :], last, gap], axis=1),
-        ]
-        lines = jnp.concatenate(lines, axis=0)
-        moments_ref[...] = jnp.broadcast_to(lines[None], moments_ref.shape)
-        return
-
     next_f = image_f * scale_f_ref[0]
     out_f_ref[...] = next_f
-    at = blocks * members
-    send_network(next_f, sr, table, ghost_table, diff_ref, [(to_a_ref, at), (to_b_ref, at), (sent_ref, 0)])
+    edge_size = base if power == 1 else base // 2
+    refs = [(to_a_ref, edge_size), (to_b_ref, edge_size), (sent_ref, 0)]
+    send_network(next_f, sr if power == 1 else None, table, ghost_table, diff_ref, refs)
 
     edges = []
     for side, at, reader in ((0, x_cells - 1, plus1), (1, 0, minus1)):
@@ -649,12 +605,128 @@
         edge = image_in_ref[:, at, :] - unit_ref[side, at : at + 1, :] * beyond
         image_ref[:, at, :] = edge
         edges.append(edge)
-    to_a_ref[0:base, :] = to_blocks(jnp.where(here.even, edges[0], edges[1]))
-    to_b_ref[0:base, :] = to_blocks(jnp.where(here.even, edges[1], edges[0]))
+    up, down = edges
+    if power == 2:
+        up, down = up[:, : y_cells // 2], down[:, y_cells // 2 :]
+    to_a_ref[0:edge_size, :] = to_blocks(jnp.where(here.even, up, down))
+    to_b_ref[0:edge_size, :] = to_blocks(jnp.where(here.even, down, up))
     margin, column = finish_edges(
         edges[0], edges[1], inner_margin_ref, inner_column_ref[...], high_side, oy_ref[...], ox_ref[...]
     )
-    send_core(core_ref, next_f, margin, weight_ref[...], ofrac_ref[...], column, j, work_ref, wown_ref)
+    if power == 1:
+        send_core(core_ref, next_f, margin, weight_ref[...], ofrac_ref[...], column, j, work_ref, wown_ref)
+    else:
+        margin_ref[...] = margin
+        core_ref[0:size, :] = to_blocks(next_f)
+        core_ref[size : size + x_cells, :] = column
+
+
+def energy_kernel(
+    v_ref,
+    before_ref,
+    vf_ref,
+    before_f_ref,
+    core_ref,
+    scale_f_ref,
+    unit_ref,
+    coef_ref,
+    storage_ref,
+    weight_ref,
+    ofrac_ref,
+    margin_ref,
+    dots_ref,
+    work_ref,
+    acc0_ref,
+    acc1_ref,
+    acc2_ref,
+):
+    members, x_cells, y_cells = v_ref.shape
+    half, frac_cells = vf_ref.shape
+    blocks = y_cells // LANES
+    here = Place()
+    size = frac_cells // LANES * half
+    theirs = from_blocks(core_ref[0:size, :], half)
+    column_in = core_ref[size : size + x_cells, :]
+    vf = vf_ref[...]
+    own_rows = pl.ds(pl.multiple_of(here.j * half, half), half)
+    work_ref[own_rows, :] = vf
+    work_ref[pl.ds(pl.multiple_of((1 - here.j) * half, half), half), :] = theirs
+    gap = margin_ref[...] - pick(work_ref[...], ofrac_ref[...])
+    acc2_ref[...] = fold_lanes(weight_ref[...] * gap * gap)
+    heavy_f = vf * scale_f_ref[1]
+    acc0_ref[...] = jnp.zeros_like(acc0_ref)
+    acc1_ref[...] = jnp.zeros_like(acc1_ref)
+    acc0_ref[own_rows, :] = fold_lanes(vf * heavy_f)
+    acc1_ref[own_rows, :] = fold_lanes(before_f_ref[...] * heavy_f)
+    lane = lax.broadcasted_iota(jnp.int32, (x_cells, y_cells), 1)
+    diag, te, tn, storage = unit_ref[5], coef_ref[0], coef_ref[2], storage_ref[...]
+
+    @pl.loop(0, members // GROUP)
+    def _(index):
+        start = index * GROUP
+        for k in range(GROUP):
+            m = start + k
+            value = v_ref[m]
+            east = value - pltpu.roll(value, x_cells - 1, 0)
+            moved = pltpu.roll(column_in, LANES - 1 - m, 1)
+            moved = jnp.concatenate([moved] * blocks, axis=1)
+            north = value - jnp.where(lane == y_cells - 1, moved, pltpu.roll(value, y_cells - 1, 1))
+            energy = storage * value * value + te * east * east + tn * north * north
+            heavy = value * diag
+            at = pl.ds(m, 1)
+            acc0_ref[at, :] += jnp.sum(fold_lanes(value * heavy), axis=0, keepdims=True)
+            acc1_ref[at, :] += jnp.sum(fold_lanes(before_ref[m] * heavy), axis=0, keepdims=True)
+            acc2_ref[at, :] += jnp.sum(fold_lanes(energy), axis=0, keepdims=True)
+
+    dots = [total_rows(ref[...]) for ref in (acc0_ref, acc1_ref, acc2_ref)]
+    dots.append(jnp.zeros((8 - len(dots), members), F32))
+    dots_ref[...] = jnp.concatenate(dots, axis=0)
+
+
+def moments_kernel(
+    vf_ref,
+    near_a_ref,
+    near_b_ref,
+    far_c_ref,
+    far_d_ref,
+    diff_in_ref,
+    sr_ref,
+    unit_ref,
+    ghost_table_ref,
+    v_ref,
+    dots1_ref,
+    dots2_ref,
+    dots3_ref,
+    moments_ref,
+    acc_ref,
+):
+    half = vf_ref.shape[0]
+    members, x_cells, y_cells = v_ref.shape
+    middle = y_cells // 2
+    base = middle // LANES * members
+    here = Place()
+    plus1, minus1, plus2, minus2 = neighbours(here, near_a_ref, near_b_ref, far_c_ref, far_d_ref)
+    vf = vf_ref[...]
+    ghosts = by_group(minus1(base, half), plus1(base, half), minus2(0, half), plus2(0, half))
+    gap = diff_in_ref[...] - pick(ghosts, ghost_table_ref[...])
+    acc_ref[...] = jnp.zeros_like(acc_ref)
+    own_rows = pl.ds(pl.multiple_of(here.j * half, half), half)
+    acc_ref[own_rows, :] = fold_lanes(sr_ref[...] * gap * gap) + fold_lanes(FRACTURE_STORAGE * vf * vf)
+    for side, at, reader, cut in (
+        (0, x_cells - 1, plus1, slice(middle, y_cells)),
+        (1, 0, minus1, slice(0, middle)),
+    ):
+        trans = unit_ref[side, at : at + 1, cut] * unit_ref[5, at : at + 1, cut]
+        edge = v_ref[:, at, cut] - from_blocks(reader(0, base), members)
+        acc_ref[...] += fold_lanes(trans * edge * edge)
+    last = total_rows(acc_ref[...]) + dots3_ref[2:3, :]
+    blank = jnp.zeros((1, LANES - 3 * members), F32)
+    lines = [
+        jnp.concatenate([dots1_ref[0:1, :], dots2_ref[1:2, :], dots2_ref[0:1, :], blank], axis=1),
+        jnp.concatenate([dots3_ref[1:2, :], dots3_ref[0:1, :], last, blank], axis=1),
+    ]
+    lines = jnp.concatenate(lines, axis=0)
+    moments_ref[...] = jnp.broadcast_to(lines[None], moments_ref.shape)
 
 
 def close_kernel(totals_ref, v0_ref, v1_ref, v2_ref, f0_ref, f1_ref, f2_ref, x_hbm, xf_hbm, c_ref, x_ref, xf_ref, sems):
@@ -822,7 +894,7 @@
         return near_a, near_b, far_c, far_d, core_in
 
     near_a, near_b, far_c, far_d, border = exchange(to_a, to_b, sent, border)
-    source_f, live, edges, coef, oy, ox, weight, first, second, table, ghost_table, ofrac, v0, margin_in, column = call(
+    source_f, storage_in, live, edges, coef, oy, ox, weight, first, second, table, ghost_table, ofrac, v0, margin_in, column = call(
         inside_kernel,
         "inside",
         (
@@ -842,6 +914,7 @@
         ),
         [
             (own, F32),
+            ((x_cells, y_cells), F32),
             ((1, rows), F32),
             ((2, members, y_cells), F32),
             ((5, x_cells, y_cells), F32),
@@ -860,7 +933,6 @@
         scratch=[
             pltpu.SMEM((ov_count.size,), jnp.int32),
             pltpu.SMEM(isect_count.shape, jnp.int32),
-            pltpu.VMEM(storage.shape, F32),
             pltpu.VMEM(field, F32),
             pltpu.VMEM((margin // LANES, LANES), jnp.int32),
             pltpu.VMEM((margin // LANES, LANES), F32),
@@ -919,9 +991,7 @@
     near_rows = edge_rows + 2 * half
 
     def interior(power, v, before, vf, before_f, core_in):
-        outs = []
-        if power < 3:
-            outs = [(field, F32), ((members, margin), F32), ((x_cells, LANES), F32)]
+        outs = [(field, F32), ((members, margin), F32), ((x_cells, LANES), F32)]
         return call(
             functools.partial(interior_kernel, power),
             f"interior_{power}",
@@ -957,23 +1027,37 @@
     )
     near_a, near_b, far_c, far_d, core_in = exchange(to_a, to_b, sent, core_msg)
     image, margin_in, column, dots2 = interior(2, v1, v0, f1, f0, core_in)
-    f2, diff, wown, to_a, to_b, sent, core_msg, v2 = call(
+    f2, diff, margin_in, to_a, to_b, sent, core_msg, v2 = call(
         functools.partial(finish_kernel, 2),
         "finish_2",
         (f1, near_a, near_b, far_c, far_d, core_in, diff, wown, sr, scale_f, unit, table, ghost_table)
         + (own_f, weight, ofrac, oy, ox, margin_in, column, image),
-        finish_outs,
-        scratch=finish_scratch,
+        [
+            (own, F32),
+            ((half, rows), F32),
+            ((members, margin), F32),
+            ((edge_rows // 2 + half, LANES), F32),
+            ((edge_rows // 2 + half, LANES), F32),
+            ((half, LANES), F32),
+            ((frac_blocks * half + x_cells, LANES), F32),
+            (field, F32),
+        ],
         aliases={20: 7},
     )
     near_a, near_b, far_c, far_d, core_in = exchange(to_a, to_b, sent, core_msg)
-    (dots3,) = interior(3, v2, v1, f2, f1, core_in)
+    (dots3,) = call(
+        energy_kernel,
+        "energy",
+        (v2, v1, f2, f1, core_in, scale_f, unit, coef, storage_in, weight, ofrac, margin_in),
+        [((8, members), F32)],
+        scratch=[pltpu.VMEM((members, frac_cells), F32)] + [pltpu.VMEM((members, LANES), F32)] * 3,
+        cost=hidden,
+    )
     peers = count * lax.axis_size("gy")
     (moments,) = call(
-        functools.partial(finish_kernel, 3),
-        "finish_3",
-        (f2, near_a, near_b, far_c, far_d, core_in, diff, wown, sr, scale_f, unit, table, ghost_table)
-        + (own_f, v2, dots1, dots2, dots3),
+        moments_kernel,
+        "moments",
+        (f2, near_a, near_b, far_c, far_d, diff, sr, unit, ghost_table, v2, dots1, dots2, dots3),
         [((peers, 2, LANES), F32)],
         scratch=[pltpu.VMEM((members, LANES), F32)],
     )

time: 56.6 us -> 56 us (0.989)
  Pallas kernels: 14.9 us -> 13.8 us
  waiting for transfers between devices: 11.1 us -> 11.7 us
    pallas_call x10, Pallas kernels: 14.9 us -> 13.8 us  [call(): pl.pallas_call(kernel, name=name, out_shape=[jax.ShapeDtypeStruct(shape,...]
    ppermute x4, waiting for transfers between devices: 5.68 us -> 6.54 us  [far(): lax.ppermute(value, 'gx', pairs_of(count, 2, 1))]
  transfers between devices with their start and end apart: 20 -> 20, of which waited for: 7 -> 7; matrix products, arithmetic and copies ran while one was open for 0% -> 0% of each run, Pallas kernels for 15% -> 14%
where the time goes in v4:
time: 56 us; the launch traced here: 55.8 us
  starting transfers between devices  19.8 us (35%)
  Pallas kernels  13.8 us (25%)
  waiting for transfers between devices  11.7 us (21%)
  blocking collectives  9.7 us (17%)
  between operations  0.76 us (1%)
    pallas_call x10, Pallas kernels, call(): pl.pallas_call(kernel, name=name, out_shape=[jax.ShapeDtypeStruct(shape,...  13.8 us
    ppermute x4, starting transfers between devices, near(): lax.ppermute(to_b, 'gx', pairs_of(count, 1, 1))  13.5 us
    all_to_all x1, blocking collectives, per_device(): totals = lax.all_to_all(moments, ('gx', 'gy'), 0, 0)  9.7 us
    ppermute x4, waiting for transfers between devices, far(): lax.ppermute(value, 'gx', pairs_of(count, 2, 1))  6.54 us
    ppermute x4, waiting for transfers between devices, near(): lax.ppermute(to_b, 'gx', pairs_of(count, 1, 1))  5.09 us
    ppermute x4, starting transfers between devices, near(): lax.ppermute(to_a, 'gx', pairs_of(count, 1, 0))  3.29 us
    ppermute x4, starting transfers between devices, far(): lax.ppermute(value, 'gx', pairs_of(count, 2, 1))  2.37 us
  transfers between devices with their start and end apart: 20, of which 7 were waited for; matrix products, arithmetic and copies ran while one was open for 0% of the time, Pallas kernels for 14%

profile of v4, /device:TPU:0, one launch (start us, length us, event | category | flops | bytes accessed | tf_op | source)
XLA Modules:
  0.0 55.8 jit_solution(2469724318221022966)
XLA Ops:
  0.6 1.0 %opening.1 = (f32[16,512]{1,0:T(8,128)S(1)}, f32[16,512]{1,0:T(8,128)S(1)}, bf16[512,128]{1,0:T(8,128)(2,1)S(1)}, f32[24,128]{1,0:T(8,128)S(1)}, f32[24,128]{1,0...) custom-call(f32[8]{0:T(128)} %perm_table_hbm.1, s32[16,512]{1,0:T(8,128)} %class_hbm.1, ...), custom_call_target="tpu_custom_call" | custom-call | tf_op jit(solution)/shard_map/opening/pallas_call | solution.py:810
  1.7 0.5 collective-permute-start
  2.2 2.6 %collective-permute-start.1 = (f32[24,128]{1,0:T(8,128)S(1)}, f32[24,128]{1,0:T(8,128)S(1)}, u32[]{:S(2)}, u32[]{:S(2)}) collective-permute-start(f32[24,128]{1,0:T(8,128)S(1)} %get-tuple-element.80), channel_id=1, source_target_pairs={{0,2},{2,0},{4,6},{6,4},{8,10},{10,8},{12,14},{14,12},{1,3},{3,1},... | collective-permute-start | bytes 36872 | tf_op jit(solution)/shard_map/ppermute | solution.py:848
  4.7 3.6 %collective-permute-start.2 = (f32[24,128]{1,0:T(8,128)S(1)}, f32[24,128]{1,0:T(8,128)S(1)}, u32[]{:S(2)}, u32[]{:S(2)}) collective-permute-start(f32[24,128]{1,0:T(8,128)S(1)} %get-tuple-element.81), channel_id=1, source_target_pairs={{2,4},{4,2},{6,8},{8,6},{10,12},{12,10},{14,0},{0,14},{3,5},{5,3},... | collective-permute-start | bytes 36872 | tf_op jit(solution)/shard_map/ppermute | solution.py:849
  8.3 0.0 collective-permute-done.border_ref
  8.3 0.5 collective-permute-start.4
  8.8 0.0 collective-permute-start.3
  8.8 2.4 %inside.1 = (f32[16,512]{1,0:T(8,128)S(1)}, f32[16,512]{1,0:T(8,128)S(1)}, f32[1,512]{1,0:T(1,128)S(1)}, f32[2,32,512]{2,1,0:T(8,128)S(1)}, f32[5,16,512]{2,1,0:...) custom-call(s32[2]{0:T(128)} %bitcast.7, ...), custom_call_target="tpu_custom_call" | custom-call | flops 4000000000 | bytes 12000000 | tf_op jit(solution)/shard_map/inside/pallas_call | solution.py:810
  11.2 0.0 collective-permute-done.1.near_a_ref
  11.2 0.0 collective-permute-done.2.near_b_ref
  11.2 2.5 %collective-permute-done.4.far_d_ref = f32[16,128]{1,0:T(8,128)S(1)} collective-permute-done((f32[16,128]{1,0:T(8,128)S(1)}, f32[16,128]{1,0:T(8,128)S(1)}, u32[]{:S(2)}, u32[]{:S(2)}) %collective-permute-start.4) | collective-permute-done | bytes 8224 | tf_op jit(solution)/shard_map/ppermute | solution.py:855
  13.8 0.0 collective-permute-done.3.far_c_ref
  13.8 1.3 %first_vector.1 = (f32[6,16,512]{2,1,0:T(8,128)S(1)}, f32[16,512]{1,0:T(8,128)S(1)}, f32[16,512]{1,0:T(8,128)S(1)}, f32[2,16,512]{2,1,0:T(8,128)S(1)}, f32[16,51...) custom-call(f32[1,512]{1,0:T(1,128)S(1)} %get-tuple-element.74.live_, ...), custom_call_target="tpu_custom_call", output_to_operand_aliasing={{10}: (20, {})} | custom-call | tf_op jit(solution)/shard_map/first_vector/pallas_call | solution.py:810
  15.1 0.0 collective-permute-start.7
  15.1 0.1 collective-permute-start.5
  15.2 3.5 %collective-permute-start.6 = (f32[176,128]{1,0:T(8,128)S(1)}, f32[176,128]{1,0:T(8,128)S(1)}, u32[]{:S(2)}, u32[]{:S(2)}) collective-permute-start(f32[176,128]{1,0:T(8,128)S(1)} %get-tuple-element.95), channel_id=1, source_target_pairs={{2,4},{4,2},{6,8},{8,6},{10,12},{12,10},{14,0},{0,14},{3,5},{5,3},... | collective-permute-start | bytes 270344 | tf_op jit(solution)/shard_map/ppermute | solution.py:849
  18.7 0.0 collective-permute-done.7.core_ref.core_in_ref
  18.7 0.9 %collective-permute-start.9 = (f32[48,128]{1,0:T(8,128)S(1)}, f32[48,128]{1,0:T(8,128)S(1)}, u32[]{:S(2)}, u32[]{:S(2)}) collective-permute-start(f32[48,128]{1,0:T(8,128)S(1)} %get-tuple-element.98), channel_id=1, source_target_pairs={{4,8},{8,4},{6,10},{10,6},{12,0},{0,12},{14,2},{2,14},{5,9},{9,5},... | collective-permute-start | bytes 73736 | tf_op jit(solution)/shard_map/ppermute | solution.py:855
  19.6 0.0 collective-permute-start.8
  19.6 2.2 %interior_1.1 = (f32[32,16,512]{2,1,0:T(8,128)S(1)}, f32[32,256]{1,0:T(8,128)S(1)}, f32[16,128]{1,0:T(8,128)S(1)}, f32[8,32]{1,0:T(8,128)S(1)}) custom-call(f32[32,16,512]{2,1,0:T(8,128)S(1)} %get-tuple-element.105.v_ref.before_ref.v0_ref, f32[32,16,512]{2,1,0:T(8,128)S(1)} %get-tuple-element.105.v_ref.before_ref.v0_ref, ...), custom_call_target="tpu_custom_call" | custom-call | flops 4000000000 | bytes 12000000 | tf_op jit(solution)/shard_map/interior_1/pallas_call | solution.py:810
  21.8 0.0 collective-permute-done.5.near_a_ref
  21.8 1.6 %collective-permute-done.6.near_b_ref = f32[176,128]{1,0:T(8,128)S(1)} collective-permute-done((f32[176,128]{1,0:T(8,128)S(1)}, f32[176,128]{1,0:T(8,128)S(1)}, u32[]{:S(2)}, u32[]{:S(2)}) %collective-permute-start.6) | collective-permute-done | bytes 90144 | tf_op jit(solution)/shard_map/ppermute | solution.py:849
  23.4 0.9 %collective-permute-done.9.far_d_ref = f32[48,128]{1,0:T(8,128)S(1)} collective-permute-done((f32[48,128]{1,0:T(8,128)S(1)}, f32[48,128]{1,0:T(8,128)S(1)}, u32[]{:S(2)}, u32[]{:S(2)}) %collective-permute-start.9) | collective-permute-done | bytes 24608 | tf_op jit(solution)/shard_map/ppermute | solution.py:855
  24.3 0.0 collective-permute-done.8.far_c_ref
  24.3 1.0 %finish_1.1 = (f32[16,512]{1,0:T(8,128)S(1)}, f32[16,512]{1,0:T(8,128)S(1)}, f32[16,512]{1,0:T(8,128)S(1)}, f32[16,512]{1,0:T(8,128)S(1)}, f32[160,128]{1,0:T(8,...) custom-call(f32[16,512]{1,0:T(8,128)S(1)} %get-tuple-element.93.vf_r, ...), custom_call_target="tpu_custom_call", output_to_operand_aliasing={{8}: (19, {})} | custom-call | tf_op jit(solution)/shard_map/finish_1/pallas_call | solution.py:810
  25.3 0.1 collective-permute-start.12
  25.4 0.3 collective-permute-start.10
  25.7 3.2 %collective-permute-start.11 = (f32[160,128]{1,0:T(8,128)S(1)}, f32[160,128]{1,0:T(8,128)S(1)}, u32[]{:S(2)}, u32[]{:S(2)}) collective-permute-start(f32[160,128]{1,0:T(8,128)S(1)} %get-tuple-element.111), channel_id=1, source_target_pairs={{2,4},{4,2},{6,8},{8,6},{10,12},{12,10},{14,0},{0,14},{3,5},{5,3},... | collective-permute-start | bytes 245768 | tf_op jit(solution)/shard_map/ppermute | solution.py:849
  29.0 0.0 collective-permute-done.12.core_ref.core_in_ref
  29.0 0.4 collective-permute-start.14
  29.4 0.0 collective-permute-start.13
  29.4 2.2 %interior_2.1 = (f32[32,16,512]{2,1,0:T(8,128)S(1)}, f32[32,256]{1,0:T(8,128)S(1)}, f32[16,128]{1,0:T(8,128)S(1)}, f32[8,32]{1,0:T(8,128)S(1)}) custom-call(f32[32,16,512]{2,1,0:T(8,128)S(1)} %get-tuple-element.119.v_ref.before_ref.v1_ref, f32[32,16,512]{2,1,0:T(8,128)S(1)} %get-tuple-element.105.v_ref.before_ref.v0_ref, ...), custom_call_target="tpu_custom_call" | custom-call | flops 4000000000 | bytes 12000000 | tf_op jit(solution)/shard_map/interior_2/pallas_call | solution.py:810
  31.7 0.0 collective-permute-done.10.near_a_ref
  31.7 1.7 %collective-permute-done.11.near_b_ref = f32[160,128]{1,0:T(8,128)S(1)} collective-permute-done((f32[160,128]{1,0:T(8,128)S(1)}, f32[160,128]{1,0:T(8,128)S(1)}, u32[]{:S(2)}, u32[]{:S(2)}) %collective-permute-start.11) | collective-permute-done | bytes 81952 | tf_op jit(solution)/shard_map/ppermute | solution.py:849
  33.4 1.1 %collective-permute-done.14.far_d_ref = f32[32,128]{1,0:T(8,128)S(1)} collective-permute-done((f32[32,128]{1,0:T(8,128)S(1)}, f32[32,128]{1,0:T(8,128)S(1)}, u32[]{:S(2)}, u32[]{:S(2)}) %collective-permute-start.14) | collective-permute-done | bytes 16416 | tf_op jit(solution)/shard_map/ppermute | solution.py:855
  34.5 0.0 collective-permute-done.13.far_c_ref
  34.5 0.8 %finish_2.1 = (f32[16,512]{1,0:T(8,128)S(1)}, f32[16,512]{1,0:T(8,128)S(1)}, f32[32,256]{1,0:T(8,128)S(1)}, f32[80,128]{1,0:T(8,128)S(1)}, f32[80,128]{1,0:T(8,1...) custom-call(f32[16,512]{1,0:T(8,128)S(1)} %get-tuple-element.109.vf_, ...), custom_call_target="tpu_custom_call", output_to_operand_aliasing={{7}: (20, {})} | custom-call | tf_op jit(solution)/shard_map/finish_2/pallas_call | solution.py:810
  35.3 0.1 collective-permute-start.17
  35.4 0.3 collective-permute-start.15
  35.7 3.2 %collective-permute-start.16 = (f32[80,128]{1,0:T(8,128)S(1)}, f32[80,128]{1,0:T(8,128)S(1)}, u32[]{:S(2)}, u32[]{:S(2)}) collective-permute-start(f32[80,128]{1,0:T(8,128)S(1)} %get-tuple-element.125), channel_id=1, source_target_pairs={{2,4},{4,2},{6,8},{8,6},{10,12},{12,10},{14,0},{0,14},{3,5},{5,3},... | collective-permute-start | bytes 122888 | tf_op jit(solution)/shard_map/ppermute | solution.py:849
  38.9 0.0 collective-permute-done.17.core_ref
  38.9 0.6 %collective-permute-start.19 = (f32[16,128]{1,0:T(8,128)S(1)}, f32[16,128]{1,0:T(8,128)S(1)}, u32[]{:S(2)}, u32[]{:S(2)}) collective-permute-start(f32[16,128]{1,0:T(8,128)S(1)} %get-tuple-element.128), channel_id=1, source_target_pairs={{4,8},{8,4},{6,10},{10,6},{12,0},{0,12},{14,2},{2,14},{5,9},{9,5},... | collective-permute-start | bytes 24584 | tf_op jit(solution)/shard_map/ppermute | solution.py:855
  39.5 0.0 collective-permute-start.18
  39.5 1.1 %energy.1.dots3_ref = f32[8,32]{1,0:T(8,128)S(1)} custom-call(f32[32,16,512]{2,1,0:T(8,128)S(1)} %get-tuple-element.130.v_ref.v2_ref, f32[32,16,512]{2,1,0:T(8,128)S(1)} %get-tuple-element.119.v_ref.before_ref.v1_ref, f32[16,512]{1,0:T(8,128)S(1)} %get-tuple-element.123.vf_ref.f2_ref, f32[16,512]{1,0:T(8,128)S(1)} %get-tuple-element.109.vf_ref.before_f_ref.f1_ref, ...), custom_call_target="tpu_custom_call" | custom-call | flops 4000000000 | bytes 12000000 | tf_op jit(solution)/shard_map/energy/pallas_call | solution.py:810
  40.6 0.0 collective-permute-done.15.near_a_ref
  40.7 1.8 %collective-permute-done.16.near_b_ref = f32[80,128]{1,0:T(8,128)S(1)} collective-permute-done((f32[80,128]{1,0:T(8,128)S(1)}, f32[80,128]{1,0:T(8,128)S(1)}, u32[]{:S(2)}, u32[]{:S(2)}) %collective-permute-start.16) | collective-permute-done | bytes 40992 | tf_op jit(solution)/shard_map/ppermute | solution.py:849
  42.4 2.0 %collective-permute-done.19.far_d_ref = f32[16,128]{1,0:T(8,128)S(1)} collective-permute-done((f32[16,128]{1,0:T(8,128)S(1)}, f32[16,128]{1,0:T(8,128)S(1)}, u32[]{:S(2)}, u32[]{:S(2)}) %collective-permute-start.19) | collective-permute-done | bytes 8224 | tf_op jit(solution)/shard_map/ppermute | solution.py:855
  44.4 0.0 collective-permute-done.18.far_c_ref
  44.4 0.3 moments.1
  44.7 9.7 %all_to_all.5.totals_ref = f32[16,2,128]{2,1,0:T(2,128)S(1)} all-to-all(f32[16,2,128]{2,1,0:T(2,128)S(1)} %moments.1), channel_id=1, replica_groups=mesh['grp'=2,'gx'=8,'gy'=2] {'gx','gy'}, dimensions={0} | all-to-all | bytes 32768 | tf_op jit(solution)/shard_map/all_to_all | solution.py:1064
  54.4 1.4 %iterate.1 = (f32[32,16,512]{2,1,0:T(8,128)}, f32[16,512]{1,0:T(8,128)}) custom-call(f32[16,2,128]{2,1,0:T(2,128)S(1)} %all_to_all.5.totals_ref, f32[32,16,512]{2,1,0:T(8,128)S(1)} %get-tuple-element.105.v_ref.before_ref.v0_ref, f32[32,16,512]{2,1,0:T(8,128)S(1)} %get-tuple-element.119.v_ref.before_ref.v1_ref, ...), custom_call_target="tpu_custom_call" | custom-call | tf_op jit(solution)/shard_map/iterate/pallas_call | solution.py:810
Async XLA Ops:
  1.7 6.7 %collective-permute-start = (f32[16,128]{1,0:T(8,128)S(1)}, f32[16,128]{1,0:T(8,128)S(1)}, u32[]{:S(2)}, u32[]{:S(2)}) collective-permute-start(f32[16,128]{1,0:T(8,128)S(1)} %get-tuple-element.71), channel_id=1, source_target_pairs={{0,1},{1,0},{2,3},{3,2},{4,5},{5,4},{6,7},{7,6},{8,9},{9,8},{10,11... | collective-permute-start | bytes 24584 | tf_op jit(solution)/shard_map/ppermute | solution.py:859
  2.2 9.1 %collective-permute-start.1 = (f32[24,128]{1,0:T(8,128)S(1)}, f32[24,128]{1,0:T(8,128)S(1)}, u32[]{:S(2)}, u32[]{:S(2)}) collective-permute-start(f32[24,128]{1,0:T(8,128)S(1)} %get-tuple-element.80), channel_id=1, source_target_pairs={{0,2},{2,0},{4,6},{6,4},{8,10},{10,8},{12,14},{14,12},{1,3},{3,1},... | collective-permute-start | bytes 36872 | tf_op jit(solution)/shard_map/ppermute | solution.py:848
  4.7 6.5 %collective-permute-start.2 = (f32[24,128]{1,0:T(8,128)S(1)}, f32[24,128]{1,0:T(8,128)S(1)}, u32[]{:S(2)}, u32[]{:S(2)}) collective-permute-start(f32[24,128]{1,0:T(8,128)S(1)} %get-tuple-element.81), channel_id=1, source_target_pairs={{2,4},{4,2},{6,8},{8,6},{10,12},{12,10},{14,0},{0,14},{3,5},{5,3},... | collective-permute-start | bytes 36872 | tf_op jit(solution)/shard_map/ppermute | solution.py:849
  8.3 5.4 %collective-permute-start.4 = (f32[16,128]{1,0:T(8,128)S(1)}, f32[16,128]{1,0:T(8,128)S(1)}, u32[]{:S(2)}, u32[]{:S(2)}) collective-permute-start(f32[16,128]{1,0:T(8,128)S(1)} %get-tuple-element.82), channel_id=1, source_target_pairs={{4,8},{8,4},{6,10},{10,6},{12,0},{0,12},{14,2},{2,14},{5,9},{9,5},... | collective-permute-start | bytes 24584 | tf_op jit(solution)/shard_map/ppermute | solution.py:855
  8.8 5.0 %collective-permute-start.3 = (f32[16,128]{1,0:T(8,128)S(1)}, f32[16,128]{1,0:T(8,128)S(1)}, u32[]{:S(2)}, u32[]{:S(2)}) collective-permute-start(f32[16,128]{1,0:T(8,128)S(1)} %get-tuple-element.82), channel_id=1, source_target_pairs={{0,4},{4,0},{2,6},{6,2},{8,12},{12,8},{10,14},{14,10},{1,5},{5,1},... | collective-permute-start | bytes 24584 | tf_op jit(solution)/shard_map/ppermute | solution.py:854
  15.1 3.6 %collective-permute-start.7 = (f32[176,128]{1,0:T(8,128)S(1)}, f32[176,128]{1,0:T(8,128)S(1)}, u32[]{:S(2)}, u32[]{:S(2)}) collective-permute-start(f32[176,128]{1,0:T(8,128)S(1)} %get-tuple-element.97), channel_id=1, source_target_pairs={{0,1},{1,0},{2,3},{3,2},{4,5},{5,4},{6,7},{7,6},{8,9},{9,8},{10,11... | collective-permute-start | bytes 270344 | tf_op jit(solution)/shard_map/ppermute | solution.py:859
  15.1 6.6 %collective-permute-start.5 = (f32[176,128]{1,0:T(8,128)S(1)}, f32[176,128]{1,0:T(8,128)S(1)}, u32[]{:S(2)}, u32[]{:S(2)}) collective-permute-start(f32[176,128]{1,0:T(8,128)S(1)} %get-tuple-element.94), channel_id=1, source_target_pairs={{0,2},{2,0},{4,6},{6,4},{8,10},{10,8},{12,14},{14,12},{1,3},{3,1},... | collective-permute-start | bytes 270344 | tf_op jit(solution)/shard_map/ppermute | solution.py:848
  15.2 8.2 %collective-permute-start.6 = (f32[176,128]{1,0:T(8,128)S(1)}, f32[176,128]{1,0:T(8,128)S(1)}, u32[]{:S(2)}, u32[]{:S(2)}) collective-permute-start(f32[176,128]{1,0:T(8,128)S(1)} %get-tuple-element.95), channel_id=1, source_target_pairs={{2,4},{4,2},{6,8},{8,6},{10,12},{12,10},{14,0},{0,14},{3,5},{5,3},... | collective-permute-start | bytes 270344 | tf_op jit(solution)/shard_map/ppermute | solution.py:849
  18.7 5.6 %collective-permute-start.9 = (f32[48,128]{1,0:T(8,128)S(1)}, f32[48,128]{1,0:T(8,128)S(1)}, u32[]{:S(2)}, u32[]{:S(2)}) collective-permute-start(f32[48,128]{1,0:T(8,128)S(1)} %get-tuple-element.98), channel_id=1, source_target_pairs={{4,8},{8,4},{6,10},{10,6},{12,0},{0,12},{14,2},{2,14},{5,9},{9,5},... | collective-permute-start | bytes 73736 | tf_op jit(solution)/shard_map/ppermute | solution.py:855
  19.6 4.7 %collective-permute-start.8 = (f32[48,128]{1,0:T(8,128)S(1)}, f32[48,128]{1,0:T(8,128)S(1)}, u32[]{:S(2)}, u32[]{:S(2)}) collective-permute-start(f32[48,128]{1,0:T(8,128)S(1)} %get-tuple-element.98), channel_id=1, source_target_pairs={{0,4},{4,0},{2,6},{6,2},{8,12},{12,8},{10,14},{14,10},{1,5},{5,1},... | collective-permute-start | bytes 73736 | tf_op jit(solution)/shard_map/ppermute | solution.py:854
  25.3 3.6 %collective-permute-start.12 = (f32[144,128]{1,0:T(8,128)S(1)}, f32[144,128]{1,0:T(8,128)S(1)}, u32[]{:S(2)}, u32[]{:S(2)}) collective-permute-start(f32[144,128]{1,0:T(8,128)S(1)} %get-tuple-element.113), channel_id=1, source_target_pairs={{0,1},{1,0},{2,3},{3,2},{4,5},{5,4},{6,7},{7,6},{8,9},{9,8},{10,11... | collective-permute-start | bytes 221192 | tf_op jit(solution)/shard_map/ppermute | solution.py:859
  25.4 6.2 %collective-permute-start.10 = (f32[160,128]{1,0:T(8,128)S(1)}, f32[160,128]{1,0:T(8,128)S(1)}, u32[]{:S(2)}, u32[]{:S(2)}) collective-permute-start(f32[160,128]{1,0:T(8,128)S(1)} %get-tuple-element.110), channel_id=1, source_target_pairs={{0,2},{2,0},{4,6},{6,4},{8,10},{10,8},{12,14},{14,12},{1,3},{3,1},... | collective-permute-start | bytes 245768 | tf_op jit(solution)/shard_map/ppermute | solution.py:848
  25.7 7.6 %collective-permute-start.11 = (f32[160,128]{1,0:T(8,128)S(1)}, f32[160,128]{1,0:T(8,128)S(1)}, u32[]{:S(2)}, u32[]{:S(2)}) collective-permute-start(f32[160,128]{1,0:T(8,128)S(1)} %get-tuple-element.111), channel_id=1, source_target_pairs={{2,4},{4,2},{6,8},{8,6},{10,12},{12,10},{14,0},{0,14},{3,5},{5,3},... | collective-permute-start | bytes 245768 | tf_op jit(solution)/shard_map/ppermute | solution.py:849
  29.0 5.5 %collective-permute-start.14 = (f32[32,128]{1,0:T(8,128)S(1)}, f32[32,128]{1,0:T(8,128)S(1)}, u32[]{:S(2)}, u32[]{:S(2)}) collective-permute-start(f32[32,128]{1,0:T(8,128)S(1)} %get-tuple-element.114), channel_id=1, source_target_pairs={{4,8},{8,4},{6,10},{10,6},{12,0},{0,12},{14,2},{2,14},{5,9},{9,5},... | collective-permute-start | bytes 49160 | tf_op jit(solution)/shard_map/ppermute | solution.py:855
  29.4 5.1 %collective-permute-start.13 = (f32[32,128]{1,0:T(8,128)S(1)}, f32[32,128]{1,0:T(8,128)S(1)}, u32[]{:S(2)}, u32[]{:S(2)}) collective-permute-start(f32[32,128]{1,0:T(8,128)S(1)} %get-tuple-element.114), channel_id=1, source_target_pairs={{0,4},{4,0},{2,6},{6,2},{8,12},{12,8},{10,14},{14,10},{1,5},{5,1},... | collective-permute-start | bytes 49160 | tf_op jit(solution)/shard_map/ppermute | solution.py:854
  35.3 3.6 %collective-permute-start.17 = (f32[80,128]{1,0:T(8,128)S(1)}, f32[80,128]{1,0:T(8,128)S(1)}, u32[]{:S(2)}, u32[]{:S(2)}) collective-permute-start(f32[80,128]{1,0:T(8,128)S(1)} %get-tuple-element.127), channel_id=1, source_target_pairs={{0,1},{1,0},{2,3},{3,2},{4,5},{5,4},{6,7},{7,6},{8,9},{9,8},{10,11... | collective-permute-start | bytes 122888 | tf_op jit(solution)/shard_map/ppermute | solution.py:859
  35.4 5.3 %collective-permute-start.15 = (f32[80,128]{1,0:T(8,128)S(1)}, f32[80,128]{1,0:T(8,128)S(1)}, u32[]{:S(2)}, u32[]{:S(2)}) collective-permute-start(f32[80,128]{1,0:T(8,128)S(1)} %get-tuple-element.124), channel_id=1, source_target_pairs={{0,2},{2,0},{4,6},{6,4},{8,10},{10,8},{12,14},{14,12},{1,3},{3,1},... | collective-permute-start | bytes 122888 | tf_op jit(solution)/shard_map/ppermute | solution.py:848
  35.7 6.7 %collective-permute-start.16 = (f32[80,128]{1,0:T(8,128)S(1)}, f32[80,128]{1,0:T(8,128)S(1)}, u32[]{:S(2)}, u32[]{:S(2)}) collective-permute-start(f32[80,128]{1,0:T(8,128)S(1)} %get-tuple-element.125), channel_id=1, source_target_pairs={{2,4},{4,2},{6,8},{8,6},{10,12},{12,10},{14,0},{0,14},{3,5},{5,3},... | collective-permute-start | bytes 122888 | tf_op jit(solution)/shard_map/ppermute | solution.py:849
  38.9 5.4 %collective-permute-start.19 = (f32[16,128]{1,0:T(8,128)S(1)}, f32[16,128]{1,0:T(8,128)S(1)}, u32[]{:S(2)}, u32[]{:S(2)}) collective-permute-start(f32[16,128]{1,0:T(8,128)S(1)} %get-tuple-element.128), channel_id=1, source_target_pairs={{4,8},{8,4},{6,10},{10,6},{12,0},{0,12},{14,2},{2,14},{5,9},{9,5},... | collective-permute-start | bytes 24584 | tf_op jit(solution)/shard_map/ppermute | solution.py:855
  39.5 4.9 %collective-permute-start.18 = (f32[16,128]{1,0:T(8,128)S(1)}, f32[16,128]{1,0:T(8,128)S(1)}, u32[]{:S(2)}, u32[]{:S(2)}) collective-permute-start(f32[16,128]{1,0:T(8,128)S(1)} %get-tuple-element.128), channel_id=1, source_target_pairs={{0,4},{4,0},{2,6},{6,2},{8,12},{12,8},{10,14},{14,10},{1,5},{5,1},... | collective-permute-start | bytes 24584 | tf_op jit(solution)/shard_map/ppermute | solution.py:854

commit v5 on v4

--- a/solution.py
+++ b/solution.py
@@ -223,6 +223,7 @@
     perm_ref,
     border_ref,
     oslot_ref,
+    cond_ref,
     source_f_ref,
     storage_ref,
     live_ref,
@@ -232,7 +233,9 @@
     ox_ref,
     weight_ref,
     first_ref,
-    second_ref,
+    cond_first_ref,
+    cond_second_ref,
+    wsum_ref,
     table_ref,
     ghost_table_ref,
     ofrac_ref,
@@ -325,11 +328,15 @@
     other = line(other_in_ref)
     first, second = one_hot(line(local_ref), frac_cells), one_hot(other, frac_cells)
     first_ref[...] = first
-    second_ref[...] = second
+    cond = cond_ref[...]
+    cond_first_ref[...] = pick(cond, first)
+    cond_second_ref[...] = pick(cond, second)
     table_ref[:, :rows] = first - second
     table_ref[:, rows:] = oslot_ref[...]
     ghost_table_ref[...] = one_hot(other - frac_cells, ghost_table_ref.shape[0])
-    ofrac_ref[...] = one_hot(line(frac_ref), frac_cells)
+    ofrac = one_hot(line(frac_ref), frac_cells)
+    ofrac_ref[...] = ofrac
+    wsum_ref[...] = pick(jnp.broadcast_to(weight, (8, weight.shape[1])), ofrac, True)
 
     inverse = 1.0 / part
     inner_x = jnp.where((row_x == 0) | (row_x == x_cells - 1), 0.0, ox)
@@ -358,7 +365,6 @@
     live_ref,
     coef_ref,
     perm_ref,
-    cond_ref,
     edge_ref,
     source_f_ref,
     weight_ref,
@@ -367,7 +373,9 @@
     far_c_ref,
     far_d_ref,
     first_ref,
-    second_ref,
+    cond_first_ref,
+    cond_second_ref,
+    wsum_ref,
     table_ref,
     ghost_table_ref,
     ofrac_ref,
@@ -399,9 +407,8 @@
 
     ghosts = by_group(minus1(0, half), plus1(0, half), minus2(0, half), plus2(0, half))
     table, ghost_table = table_ref[...], ghost_table_ref[...]
-    cond = cond_ref[...]
-    cond_first = pick(cond, first_ref[...])
-    cond_second = pick(cond, second_ref[...]) + pick(ghosts, ghost_table)
+    cond_first = cond_first_ref[...]
+    cond_second = cond_second_ref[...] + pick(ghosts, ghost_table)
     sr = jnp.where(live_ref[...] > 0.0, harmonic(cond_first, cond_second), 0.0)
     sr_ref[...] = sr
     diag_f = FRACTURE_STORAGE + pick(sr, first_ref[...], True)
@@ -443,9 +450,8 @@
     )
     weight = weight_ref[...]
     send_core(core_ref, vf, margin, weight, ofrac_ref[...], column, j, work_ref, wown_ref)
-    wsum = pick(jnp.broadcast_to(weight, (8, weight.shape[1])), ofrac_ref[...], True)
     tail = core_ref.shape[0] - 8 * (frac_cells // LANES)
-    core_ref[tail:, :] = to_blocks(wsum)
+    core_ref[tail:, :] = to_blocks(wsum_ref[...])
 
 
 def interior_kernel(
@@ -549,8 +555,7 @@
     ghost_table_ref,
     *refs,
 ):
-    if power == 2:
-        own_f_in_ref, *refs = refs
+    own_f_in_ref, *refs = refs
     weight_ref, ofrac_ref, oy_ref, ox_ref, inner_margin_ref, inner_column_ref, image_in_ref, *refs = refs
     if power == 1:
         own_f_ref, out_f_ref, diff_ref, wown_ref, to_a_ref, to_b_ref, sent_ref, core_ref, image_ref, work_ref = refs
@@ -580,10 +585,8 @@
         back = by_group(
             plus1(base + at, half), minus1(base + at, half), plus2(at, half), minus2(at, half)
         )
-        weight = weight_ref[...]
-        wsum = pick(jnp.broadcast_to(weight, (8, weight.shape[1])), ofrac_ref[...], True)
         tail = core_in_ref.shape[0] - 8 * frac_blocks
-        wsum = wsum + from_blocks(core_in_ref[tail:, :], 8)
+        wsum = own_f_in_ref[...] + from_blocks(core_in_ref[tail:, :], 8)
         own_f = FRACTURE_STORAGE + wsum[:1] + pick(back, table[:, rows:], True)
         own_f_ref[...] = own_f
     else:
@@ -894,7 +897,7 @@
         return near_a, near_b, far_c, far_d, core_in
 
     near_a, near_b, far_c, far_d, border = exchange(to_a, to_b, sent, border)
-    source_f, storage_in, live, edges, coef, oy, ox, weight, first, second, table, ghost_table, ofrac, v0, margin_in, column = call(
+    source_f, storage_in, live, edges, coef, oy, ox, weight, *network, v0, margin_in, column = call(
         inside_kernel,
         "inside",
         (
@@ -911,6 +914,7 @@
             perm,
             border,
             oslot,
+            cond,
         ),
         [
             (own, F32),
@@ -922,7 +926,9 @@
             ((x_cells, margin), F32),
             ((1, margin), F32),
             ((frac_cells, rows), BF16),
-            ((frac_cells, rows), BF16),
+            ((half, rows), F32),
+            ((half, rows), F32),
+            ((8, frac_cells), F32),
             ((frac_cells, rows + slots), BF16),
             ((slots, rows), BF16),
             ((frac_cells, margin), BF16),
@@ -944,6 +950,7 @@
         far_in=10,
         cost=hidden,
     )
+    first, cond_first, cond_second, wsum, table, ghost_table, ofrac = network
     core_rows = 2 * frac_blocks * half + x_cells
     edge_rows = blocks * members
     unit, f0, sr, scale_f, diff, wown, to_a, to_b, sent, core_msg, v0 = call(
@@ -953,7 +960,6 @@
             live,
             coef,
             perm,
-            cond,
             edges,
             source_f,
             weight,
@@ -961,11 +967,7 @@
             near_b,
             far_c,
             far_d,
-            first,
-            second,
-            table,
-            ghost_table,
-            ofrac,
+            *network,
             oy,
             ox,
             margin_in,
@@ -986,7 +988,7 @@
             (field, F32),
         ],
         scratch=[pltpu.VMEM((members, frac_cells), F32)],
-        aliases={20: 10},
+        aliases={21: 10},
     )
     near_rows = edge_rows + 2 * half
 
@@ -1020,10 +1022,10 @@
         functools.partial(finish_kernel, 1),
         "finish_1",
         (f0, near_a, near_b, far_c, far_d, core_in, diff, wown, sr, scale_f, unit, table, ghost_table)
-        + (weight, ofrac, oy, ox, margin_in, column, image),
+        + (wsum, weight, ofrac, oy, ox, margin_in, column, image),
         [(own, F32)] + finish_outs,
         scratch=finish_scratch,
-        aliases={19: 8},
+        aliases={20: 8},
     )
     near_a, near_b, far_c, far_d, core_in = exchange(to_a, to_b, sent, core_msg)
     image, margin_in, column, dots2 = interior(2, v1, v0, f1, f0, core_in)

time: 56 us -> 55.7 us (level)
  transfers between devices with their start and end apart: 20 -> 20, of which waited for: 7 -> 7; matrix products, arithmetic and copies ran while one was open for 0% -> 0% of each run, Pallas kernels for 14% -> 15%
where the time goes in v5:
time: 55.7 us; the launch traced here: 55.5 us
  starting transfers between devices  19.9 us (36%)
  Pallas kernels  13.6 us (24%)
  waiting for transfers between devices  11.5 us (21%)
  blocking collectives  9.7 us (17%)
  between operations  0.76 us (1%)
    pallas_call x10, Pallas kernels, call(): pl.pallas_call(kernel, name=name, out_shape=[jax.ShapeDtypeStruct(shape,...  13.6 us
    ppermute x4, starting transfers between devices, near(): lax.ppermute(to_b, 'gx', pairs_of(count, 1, 1))  13.5 us
    all_to_all x1, blocking collectives, per_device(): totals = lax.all_to_all(moments, ('gx', 'gy'), 0, 0)  9.7 us
    ppermute x4, waiting for transfers between devices, far(): lax.ppermute(value, 'gx', pairs_of(count, 2, 1))  6.49 us
    ppermute x4, waiting for transfers between devices, near(): lax.ppermute(to_b, 'gx', pairs_of(count, 1, 1))  4.97 us
    ppermute x4, starting transfers between devices, near(): lax.ppermute(to_a, 'gx', pairs_of(count, 1, 0))  3.27 us
    ppermute x4, starting transfers between devices, far(): lax.ppermute(value, 'gx', pairs_of(count, 2, 1))  2.44 us
  transfers between devices with their start and end apart: 20, of which 7 were waited for; matrix products, arithmetic and copies ran while one was open for 0% of the time, Pallas kernels for 15%

profile of v5, /device:TPU:0, one launch (start us, length us, event | category | flops | bytes accessed | tf_op | source)
XLA Modules:
  0.0 55.5 jit_solution(17137128770481684566)
XLA Ops:
  0.6 1.0 %opening.1 = (f32[16,512]{1,0:T(8,128)S(1)}, f32[16,512]{1,0:T(8,128)S(1)}, bf16[512,128]{1,0:T(8,128)(2,1)S(1)}, f32[24,128]{1,0:T(8,128)S(1)}, f32[24,128]{1,0...) custom-call(f32[8]{0:T(128)} %perm_table_hbm.1, s32[16,512]{1,0:T(8,128)} %class_hbm.1, ...), custom_call_target="tpu_custom_call" | custom-call | tf_op jit(solution)/shard_map/opening/pallas_call | solution.py:813
  1.7 0.5 collective-permute-start
  2.2 2.6 %collective-permute-start.1 = (f32[24,128]{1,0:T(8,128)S(1)}, f32[24,128]{1,0:T(8,128)S(1)}, u32[]{:S(2)}, u32[]{:S(2)}) collective-permute-start(f32[24,128]{1,0:T(8,128)S(1)} %get-tuple-element.82), channel_id=1, source_target_pairs={{0,2},{2,0},{4,6},{6,4},{8,10},{10,8},{12,14},{14,12},{1,3},{3,1},... | collective-permute-start | bytes 36872 | tf_op jit(solution)/shard_map/ppermute | solution.py:851
  4.7 3.6 %collective-permute-start.2 = (f32[24,128]{1,0:T(8,128)S(1)}, f32[24,128]{1,0:T(8,128)S(1)}, u32[]{:S(2)}, u32[]{:S(2)}) collective-permute-start(f32[24,128]{1,0:T(8,128)S(1)} %get-tuple-element.83), channel_id=1, source_target_pairs={{2,4},{4,2},{6,8},{8,6},{10,12},{12,10},{14,0},{0,14},{3,5},{5,3},... | collective-permute-start | bytes 36872 | tf_op jit(solution)/shard_map/ppermute | solution.py:852
  8.3 0.0 collective-permute-done.border_ref
  8.3 0.5 collective-permute-start.4
  8.8 0.0 collective-permute-start.3
  8.8 2.5 %inside.1 = (f32[16,512]{1,0:T(8,128)S(1)}, f32[16,512]{1,0:T(8,128)S(1)}, f32[1,512]{1,0:T(1,128)S(1)}, f32[2,32,512]{2,1,0:T(8,128)S(1)}, f32[5,16,512]{2,1,0:...) custom-call(s32[2]{0:T(128)} %bitcast.7, ...), custom_call_target="tpu_custom_call" | custom-call | flops 4000000000 | bytes 12000000 | tf_op jit(solution)/shard_map/inside/pallas_call | solution.py:813
  11.3 0.0 collective-permute-done.1.near_a_ref
  11.3 0.0 collective-permute-done.2.near_b_ref
  11.3 2.4 %collective-permute-done.4.far_d_ref = f32[16,128]{1,0:T(8,128)S(1)} collective-permute-done((f32[16,128]{1,0:T(8,128)S(1)}, f32[16,128]{1,0:T(8,128)S(1)}, u32[]{:S(2)}, u32[]{:S(2)}) %collective-permute-start.4) | collective-permute-done | bytes 8224 | tf_op jit(solution)/shard_map/ppermute | solution.py:858
  13.8 0.0 collective-permute-done.3.far_c_ref
  13.8 1.1 %first_vector.1 = (f32[6,16,512]{2,1,0:T(8,128)S(1)}, f32[16,512]{1,0:T(8,128)S(1)}, f32[16,512]{1,0:T(8,128)S(1)}, f32[2,16,512]{2,1,0:T(8,128)S(1)}, f32[16,51...) custom-call(f32[1,512]{1,0:T(1,128)S(1)} %get-tuple-element.77.live_, ...), custom_call_target="tpu_custom_call", output_to_operand_aliasing={{10}: (21, {})} | custom-call | tf_op jit(solution)/shard_map/first_vector/pallas_call | solution.py:813
  14.8 0.0 collective-permute-start.7
  14.9 0.1 collective-permute-start.5
  15.0 3.5 %collective-permute-start.6 = (f32[176,128]{1,0:T(8,128)S(1)}, f32[176,128]{1,0:T(8,128)S(1)}, u32[]{:S(2)}, u32[]{:S(2)}) collective-permute-start(f32[176,128]{1,0:T(8,128)S(1)} %get-tuple-element.99), channel_id=1, source_target_pairs={{2,4},{4,2},{6,8},{8,6},{10,12},{12,10},{14,0},{0,14},{3,5},{5,3},... | collective-permute-start | bytes 270344 | tf_op jit(solution)/shard_map/ppermute | solution.py:852
  18.4 0.0 collective-permute-done.7.core_ref.core_in_ref
  18.4 1.0 %collective-permute-start.9 = (f32[48,128]{1,0:T(8,128)S(1)}, f32[48,128]{1,0:T(8,128)S(1)}, u32[]{:S(2)}, u32[]{:S(2)}) collective-permute-start(f32[48,128]{1,0:T(8,128)S(1)} %get-tuple-element.102), channel_id=1, source_target_pairs={{4,8},{8,4},{6,10},{10,6},{12,0},{0,12},{14,2},{2,14},{5,9},{9,5},... | collective-permute-start | bytes 73736 | tf_op jit(solution)/shard_map/ppermute | solution.py:858
  19.4 0.0 collective-permute-start.8
  19.4 2.2 %interior_1.1 = (f32[32,16,512]{2,1,0:T(8,128)S(1)}, f32[32,256]{1,0:T(8,128)S(1)}, f32[16,128]{1,0:T(8,128)S(1)}, f32[8,32]{1,0:T(8,128)S(1)}) custom-call(f32[32,16,512]{2,1,0:T(8,128)S(1)} %get-tuple-element.109.v_ref.before_ref.v0_ref, f32[32,16,512]{2,1,0:T(8,128)S(1)} %get-tuple-element.109.v_ref.before_ref.v0_ref, ...), custom_call_target="tpu_custom_call" | custom-call | flops 4000000000 | bytes 12000000 | tf_op jit(solution)/shard_map/interior_1/pallas_call | solution.py:813
  21.6 0.0 collective-permute-done.5.near_a_ref
  21.6 1.5 %collective-permute-done.6.near_b_ref = f32[176,128]{1,0:T(8,128)S(1)} collective-permute-done((f32[176,128]{1,0:T(8,128)S(1)}, f32[176,128]{1,0:T(8,128)S(1)}, u32[]{:S(2)}, u32[]{:S(2)}) %collective-permute-start.6) | collective-permute-done | bytes 90144 | tf_op jit(solution)/shard_map/ppermute | solution.py:852
  23.1 0.9 %collective-permute-done.9.far_d_ref = f32[48,128]{1,0:T(8,128)S(1)} collective-permute-done((f32[48,128]{1,0:T(8,128)S(1)}, f32[48,128]{1,0:T(8,128)S(1)}, u32[]{:S(2)}, u32[]{:S(2)}) %collective-permute-start.9) | collective-permute-done | bytes 24608 | tf_op jit(solution)/shard_map/ppermute | solution.py:858
  24.1 0.0 collective-permute-done.8.far_c_ref
  24.1 1.0 %finish_1.1 = (f32[16,512]{1,0:T(8,128)S(1)}, f32[16,512]{1,0:T(8,128)S(1)}, f32[16,512]{1,0:T(8,128)S(1)}, f32[16,512]{1,0:T(8,128)S(1)}, f32[160,128]{1,0:T(8,...) custom-call(f32[16,512]{1,0:T(8,128)S(1)} %get-tuple-element.97.vf_r, ...), custom_call_target="tpu_custom_call", output_to_operand_aliasing={{8}: (20, {})} | custom-call | tf_op jit(solution)/shard_map/finish_1/pallas_call | solution.py:813
  25.0 0.1 collective-permute-start.12
  25.1 0.3 collective-permute-start.10
  25.4 3.2 %collective-permute-start.11 = (f32[160,128]{1,0:T(8,128)S(1)}, f32[160,128]{1,0:T(8,128)S(1)}, u32[]{:S(2)}, u32[]{:S(2)}) collective-permute-start(f32[160,128]{1,0:T(8,128)S(1)} %get-tuple-element.115), channel_id=1, source_target_pairs={{2,4},{4,2},{6,8},{8,6},{10,12},{12,10},{14,0},{0,14},{3,5},{5,3},... | collective-permute-start | bytes 245768 | tf_op jit(solution)/shard_map/ppermute | solution.py:852
  28.7 0.0 collective-permute-done.12.core_ref.core_in_ref
  28.7 0.4 collective-permute-start.14
  29.1 0.0 collective-permute-start.13
  29.1 2.2 %interior_2.1 = (f32[32,16,512]{2,1,0:T(8,128)S(1)}, f32[32,256]{1,0:T(8,128)S(1)}, f32[16,128]{1,0:T(8,128)S(1)}, f32[8,32]{1,0:T(8,128)S(1)}) custom-call(f32[32,16,512]{2,1,0:T(8,128)S(1)} %get-tuple-element.123.v_ref.before_ref.v1_ref, f32[32,16,512]{2,1,0:T(8,128)S(1)} %get-tuple-element.109.v_ref.before_ref.v0_ref, ...), custom_call_target="tpu_custom_call" | custom-call | flops 4000000000 | bytes 12000000 | tf_op jit(solution)/shard_map/interior_2/pallas_call | solution.py:813
  31.4 0.0 collective-permute-done.10.near_a_ref
  31.4 1.7 %collective-permute-done.11.near_b_ref = f32[160,128]{1,0:T(8,128)S(1)} collective-permute-done((f32[160,128]{1,0:T(8,128)S(1)}, f32[160,128]{1,0:T(8,128)S(1)}, u32[]{:S(2)}, u32[]{:S(2)}) %collective-permute-start.11) | collective-permute-done | bytes 81952 | tf_op jit(solution)/shard_map/ppermute | solution.py:852
  33.1 1.1 %collective-permute-done.14.far_d_ref = f32[32,128]{1,0:T(8,128)S(1)} collective-permute-done((f32[32,128]{1,0:T(8,128)S(1)}, f32[32,128]{1,0:T(8,128)S(1)}, u32[]{:S(2)}, u32[]{:S(2)}) %collective-permute-start.14) | collective-permute-done | bytes 16416 | tf_op jit(solution)/shard_map/ppermute | solution.py:858
  34.2 0.0 collective-permute-done.13.far_c_ref
  34.2 0.8 %finish_2.1 = (f32[16,512]{1,0:T(8,128)S(1)}, f32[16,512]{1,0:T(8,128)S(1)}, f32[32,256]{1,0:T(8,128)S(1)}, f32[80,128]{1,0:T(8,128)S(1)}, f32[80,128]{1,0:T(8,1...) custom-call(f32[16,512]{1,0:T(8,128)S(1)} %get-tuple-element.113.vf_, ...), custom_call_target="tpu_custom_call", output_to_operand_aliasing={{7}: (20, {})} | custom-call | tf_op jit(solution)/shard_map/finish_2/pallas_call | solution.py:813
  35.0 0.1 collective-permute-start.17
  35.1 0.3 collective-permute-start.15
  35.4 3.2 %collective-permute-start.16 = (f32[80,128]{1,0:T(8,128)S(1)}, f32[80,128]{1,0:T(8,128)S(1)}, u32[]{:S(2)}, u32[]{:S(2)}) collective-permute-start(f32[80,128]{1,0:T(8,128)S(1)} %get-tuple-element.129), channel_id=1, source_target_pairs={{2,4},{4,2},{6,8},{8,6},{10,12},{12,10},{14,0},{0,14},{3,5},{5,3},... | collective-permute-start | bytes 122888 | tf_op jit(solution)/shard_map/ppermute | solution.py:852
  38.6 0.0 collective-permute-done.17.core_ref
  38.6 0.6 %collective-permute-start.19 = (f32[16,128]{1,0:T(8,128)S(1)}, f32[16,128]{1,0:T(8,128)S(1)}, u32[]{:S(2)}, u32[]{:S(2)}) collective-permute-start(f32[16,128]{1,0:T(8,128)S(1)} %get-tuple-element.132), channel_id=1, source_target_pairs={{4,8},{8,4},{6,10},{10,6},{12,0},{0,12},{14,2},{2,14},{5,9},{9,5},... | collective-permute-start | bytes 24584 | tf_op jit(solution)/shard_map/ppermute | solution.py:858
  39.2 0.0 collective-permute-start.18
  39.2 1.1 %energy.1.dots3_ref = f32[8,32]{1,0:T(8,128)S(1)} custom-call(f32[32,16,512]{2,1,0:T(8,128)S(1)} %get-tuple-element.134.v_ref.v2_ref, f32[32,16,512]{2,1,0:T(8,128)S(1)} %get-tuple-element.123.v_ref.before_ref.v1_ref, f32[16,512]{1,0:T(8,128)S(1)} %get-tuple-element.127.vf_ref.f2_ref, f32[16,512]{1,0:T(8,128)S(1)} %get-tuple-element.113.vf_ref.before_f_ref.f1_ref, ...), custom_call_target="tpu_custom_call" | custom-call | flops 4000000000 | bytes 12000000 | tf_op jit(solution)/shard_map/energy/pallas_call | solution.py:813
  40.3 0.0 collective-permute-done.15.near_a_ref
  40.3 1.7 %collective-permute-done.16.near_b_ref = f32[80,128]{1,0:T(8,128)S(1)} collective-permute-done((f32[80,128]{1,0:T(8,128)S(1)}, f32[80,128]{1,0:T(8,128)S(1)}, u32[]{:S(2)}, u32[]{:S(2)}) %collective-permute-start.16) | collective-permute-done | bytes 40992 | tf_op jit(solution)/shard_map/ppermute | solution.py:852
  42.1 2.0 %collective-permute-done.19.far_d_ref = f32[16,128]{1,0:T(8,128)S(1)} collective-permute-done((f32[16,128]{1,0:T(8,128)S(1)}, f32[16,128]{1,0:T(8,128)S(1)}, u32[]{:S(2)}, u32[]{:S(2)}) %collective-permute-start.19) | collective-permute-done | bytes 8224 | tf_op jit(solution)/shard_map/ppermute | solution.py:858
  44.1 0.0 collective-permute-done.18.far_c_ref
  44.1 0.3 moments.1
  44.4 9.7 %all_to_all.5.totals_ref = f32[16,2,128]{2,1,0:T(2,128)S(1)} all-to-all(f32[16,2,128]{2,1,0:T(2,128)S(1)} %moments.1), channel_id=1, replica_groups=mesh['grp'=2,'gx'=8,'gy'=2] {'gx','gy'}, dimensions={0} | all-to-all | bytes 32768 | tf_op jit(solution)/shard_map/all_to_all | solution.py:1066
  54.1 1.4 %iterate.1 = (f32[32,16,512]{2,1,0:T(8,128)}, f32[16,512]{1,0:T(8,128)}) custom-call(f32[16,2,128]{2,1,0:T(2,128)S(1)} %all_to_all.5.totals_ref, f32[32,16,512]{2,1,0:T(8,128)S(1)} %get-tuple-element.109.v_ref.before_ref.v0_ref, f32[32,16,512]{2,1,0:T(8,128)S(1)} %get-tuple-element.123.v_ref.before_ref.v1_ref, ...), custom_call_target="tpu_custom_call" | custom-call | tf_op jit(solution)/shard_map/iterate/pallas_call | solution.py:813
Async XLA Ops:
  1.7 6.7 %collective-permute-start = (f32[16,128]{1,0:T(8,128)S(1)}, f32[16,128]{1,0:T(8,128)S(1)}, u32[]{:S(2)}, u32[]{:S(2)}) collective-permute-start(f32[16,128]{1,0:T(8,128)S(1)} %get-tuple-element.73), channel_id=1, source_target_pairs={{0,1},{1,0},{2,3},{3,2},{4,5},{5,4},{6,7},{7,6},{8,9},{9,8},{10,11... | collective-permute-start | bytes 24584 | tf_op jit(solution)/shard_map/ppermute | solution.py:862
  2.2 9.1 %collective-permute-start.1 = (f32[24,128]{1,0:T(8,128)S(1)}, f32[24,128]{1,0:T(8,128)S(1)}, u32[]{:S(2)}, u32[]{:S(2)}) collective-permute-start(f32[24,128]{1,0:T(8,128)S(1)} %get-tuple-element.82), channel_id=1, source_target_pairs={{0,2},{2,0},{4,6},{6,4},{8,10},{10,8},{12,14},{14,12},{1,3},{3,1},... | collective-permute-start | bytes 36872 | tf_op jit(solution)/shard_map/ppermute | solution.py:851
  4.7 6.6 %collective-permute-start.2 = (f32[24,128]{1,0:T(8,128)S(1)}, f32[24,128]{1,0:T(8,128)S(1)}, u32[]{:S(2)}, u32[]{:S(2)}) collective-permute-start(f32[24,128]{1,0:T(8,128)S(1)} %get-tuple-element.83), channel_id=1, source_target_pairs={{2,4},{4,2},{6,8},{8,6},{10,12},{12,10},{14,0},{0,14},{3,5},{5,3},... | collective-permute-start | bytes 36872 | tf_op jit(solution)/shard_map/ppermute | solution.py:852
  8.3 5.4 %collective-permute-start.4 = (f32[16,128]{1,0:T(8,128)S(1)}, f32[16,128]{1,0:T(8,128)S(1)}, u32[]{:S(2)}, u32[]{:S(2)}) collective-permute-start(f32[16,128]{1,0:T(8,128)S(1)} %get-tuple-element.84), channel_id=1, source_target_pairs={{4,8},{8,4},{6,10},{10,6},{12,0},{0,12},{14,2},{2,14},{5,9},{9,5},... | collective-permute-start | bytes 24584 | tf_op jit(solution)/shard_map/ppermute | solution.py:858
  8.8 5.0 %collective-permute-start.3 = (f32[16,128]{1,0:T(8,128)S(1)}, f32[16,128]{1,0:T(8,128)S(1)}, u32[]{:S(2)}, u32[]{:S(2)}) collective-permute-start(f32[16,128]{1,0:T(8,128)S(1)} %get-tuple-element.84), channel_id=1, source_target_pairs={{0,4},{4,0},{2,6},{6,2},{8,12},{12,8},{10,14},{14,10},{1,5},{5,1},... | collective-permute-start | bytes 24584 | tf_op jit(solution)/shard_map/ppermute | solution.py:857
  14.8 3.6 %collective-permute-start.7 = (f32[176,128]{1,0:T(8,128)S(1)}, f32[176,128]{1,0:T(8,128)S(1)}, u32[]{:S(2)}, u32[]{:S(2)}) collective-permute-start(f32[176,128]{1,0:T(8,128)S(1)} %get-tuple-element.101), channel_id=1, source_target_pairs={{0,1},{1,0},{2,3},{3,2},{4,5},{5,4},{6,7},{7,6},{8,9},{9,8},{10,11... | collective-permute-start | bytes 270344 | tf_op jit(solution)/shard_map/ppermute | solution.py:862
  14.9 6.7 %collective-permute-start.5 = (f32[176,128]{1,0:T(8,128)S(1)}, f32[176,128]{1,0:T(8,128)S(1)}, u32[]{:S(2)}, u32[]{:S(2)}) collective-permute-start(f32[176,128]{1,0:T(8,128)S(1)} %get-tuple-element.98), channel_id=1, source_target_pairs={{0,2},{2,0},{4,6},{6,4},{8,10},{10,8},{12,14},{14,12},{1,3},{3,1},... | collective-permute-start | bytes 270344 | tf_op jit(solution)/shard_map/ppermute | solution.py:851
  15.0 8.2 %collective-permute-start.6 = (f32[176,128]{1,0:T(8,128)S(1)}, f32[176,128]{1,0:T(8,128)S(1)}, u32[]{:S(2)}, u32[]{:S(2)}) collective-permute-start(f32[176,128]{1,0:T(8,128)S(1)} %get-tuple-element.99), channel_id=1, source_target_pairs={{2,4},{4,2},{6,8},{8,6},{10,12},{12,10},{14,0},{0,14},{3,5},{5,3},... | collective-permute-start | bytes 270344 | tf_op jit(solution)/shard_map/ppermute | solution.py:852
  18.4 5.6 %collective-permute-start.9 = (f32[48,128]{1,0:T(8,128)S(1)}, f32[48,128]{1,0:T(8,128)S(1)}, u32[]{:S(2)}, u32[]{:S(2)}) collective-permute-start(f32[48,128]{1,0:T(8,128)S(1)} %get-tuple-element.102), channel_id=1, source_target_pairs={{4,8},{8,4},{6,10},{10,6},{12,0},{0,12},{14,2},{2,14},{5,9},{9,5},... | collective-permute-start | bytes 73736 | tf_op jit(solution)/shard_map/ppermute | solution.py:858
  19.4 4.7 %collective-permute-start.8 = (f32[48,128]{1,0:T(8,128)S(1)}, f32[48,128]{1,0:T(8,128)S(1)}, u32[]{:S(2)}, u32[]{:S(2)}) collective-permute-start(f32[48,128]{1,0:T(8,128)S(1)} %get-tuple-element.102), channel_id=1, source_target_pairs={{0,4},{4,0},{2,6},{6,2},{8,12},{12,8},{10,14},{14,10},{1,5},{5,1},... | collective-permute-start | bytes 73736 | tf_op jit(solution)/shard_map/ppermute | solution.py:857
  25.0 3.6 %collective-permute-start.12 = (f32[144,128]{1,0:T(8,128)S(1)}, f32[144,128]{1,0:T(8,128)S(1)}, u32[]{:S(2)}, u32[]{:S(2)}) collective-permute-start(f32[144,128]{1,0:T(8,128)S(1)} %get-tuple-element.117), channel_id=1, source_target_pairs={{0,1},{1,0},{2,3},{3,2},{4,5},{5,4},{6,7},{7,6},{8,9},{9,8},{10,11... | collective-permute-start | bytes 221192 | tf_op jit(solution)/shard_map/ppermute | solution.py:862
  25.1 6.2 %collective-permute-start.10 = (f32[160,128]{1,0:T(8,128)S(1)}, f32[160,128]{1,0:T(8,128)S(1)}, u32[]{:S(2)}, u32[]{:S(2)}) collective-permute-start(f32[160,128]{1,0:T(8,128)S(1)} %get-tuple-element.114), channel_id=1, source_target_pairs={{0,2},{2,0},{4,6},{6,4},{8,10},{10,8},{12,14},{14,12},{1,3},{3,1},... | collective-permute-start | bytes 245768 | tf_op jit(solution)/shard_map/ppermute | solution.py:851
  25.4 7.6 %collective-permute-start.11 = (f32[160,128]{1,0:T(8,128)S(1)}, f32[160,128]{1,0:T(8,128)S(1)}, u32[]{:S(2)}, u32[]{:S(2)}) collective-permute-start(f32[160,128]{1,0:T(8,128)S(1)} %get-tuple-element.115), channel_id=1, source_target_pairs={{2,4},{4,2},{6,8},{8,6},{10,12},{12,10},{14,0},{0,14},{3,5},{5,3},... | collective-permute-start | bytes 245768 | tf_op jit(solution)/shard_map/ppermute | solution.py:852
  28.7 5.5 %collective-permute-start.14 = (f32[32,128]{1,0:T(8,128)S(1)}, f32[32,128]{1,0:T(8,128)S(1)}, u32[]{:S(2)}, u32[]{:S(2)}) collective-permute-start(f32[32,128]{1,0:T(8,128)S(1)} %get-tuple-element.118), channel_id=1, source_target_pairs={{4,8},{8,4},{6,10},{10,6},{12,0},{0,12},{14,2},{2,14},{5,9},{9,5},... | collective-permute-start | bytes 49160 | tf_op jit(solution)/shard_map/ppermute | solution.py:858
  29.1 5.1 %collective-permute-start.13 = (f32[32,128]{1,0:T(8,128)S(1)}, f32[32,128]{1,0:T(8,128)S(1)}, u32[]{:S(2)}, u32[]{:S(2)}) collective-permute-start(f32[32,128]{1,0:T(8,128)S(1)} %get-tuple-element.118), channel_id=1, source_target_pairs={{0,4},{4,0},{2,6},{6,2},{8,12},{12,8},{10,14},{14,10},{1,5},{5,1},... | collective-permute-start | bytes 49160 | tf_op jit(solution)/shard_map/ppermute | solution.py:857
  35.0 3.6 %collective-permute-start.17 = (f32[80,128]{1,0:T(8,128)S(1)}, f32[80,128]{1,0:T(8,128)S(1)}, u32[]{:S(2)}, u32[]{:S(2)}) collective-permute-start(f32[80,128]{1,0:T(8,128)S(1)} %get-tuple-element.131), channel_id=1, source_target_pairs={{0,1},{1,0},{2,3},{3,2},{4,5},{5,4},{6,7},{7,6},{8,9},{9,8},{10,11... | collective-permute-start | bytes 122888 | tf_op jit(solution)/shard_map/ppermute | solution.py:862
  35.1 5.3 %collective-permute-start.15 = (f32[80,128]{1,0:T(8,128)S(1)}, f32[80,128]{1,0:T(8,128)S(1)}, u32[]{:S(2)}, u32[]{:S(2)}) collective-permute-start(f32[80,128]{1,0:T(8,128)S(1)} %get-tuple-element.128), channel_id=1, source_target_pairs={{0,2},{2,0},{4,6},{6,4},{8,10},{10,8},{12,14},{14,12},{1,3},{3,1},... | collective-permute-start | bytes 122888 | tf_op jit(solution)/shard_map/ppermute | solution.py:851
  35.4 6.7 %collective-permute-start.16 = (f32[80,128]{1,0:T(8,128)S(1)}, f32[80,128]{1,0:T(8,128)S(1)}, u32[]{:S(2)}, u32[]{:S(2)}) collective-permute-start(f32[80,128]{1,0:T(8,128)S(1)} %get-tuple-element.129), channel_id=1, source_target_pairs={{2,4},{4,2},{6,8},{8,6},{10,12},{12,10},{14,0},{0,14},{3,5},{5,3},... | collective-permute-start | bytes 122888 | tf_op jit(solution)/shard_map/ppermute | solution.py:852
  38.6 5.4 %collective-permute-start.19 = (f32[16,128]{1,0:T(8,128)S(1)}, f32[16,128]{1,0:T(8,128)S(1)}, u32[]{:S(2)}, u32[]{:S(2)}) collective-permute-start(f32[16,128]{1,0:T(8,128)S(1)} %get-tuple-element.132), channel_id=1, source_target_pairs={{4,8},{8,4},{6,10},{10,6},{12,0},{0,12},{14,2},{2,14},{5,9},{9,5},... | collective-permute-start | bytes 24584 | tf_op jit(solution)/shard_map/ppermute | solution.py:858
  39.2 4.9 %collective-permute-start.18 = (f32[16,128]{1,0:T(8,128)S(1)}, f32[16,128]{1,0:T(8,128)S(1)}, u32[]{:S(2)}, u32[]{:S(2)}) collective-permute-start(f32[16,128]{1,0:T(8,128)S(1)} %get-tuple-element.132), channel_id=1, source_target_pairs={{0,4},{4,0},{2,6},{6,2},{8,12},{12,8},{10,14},{14,10},{1,5},{5,1},... | collective-permute-start | bytes 24584 | tf_op jit(solution)/shard_map/ppermute | solution.py:857

commit v6 on v5

--- a/solution.py
+++ b/solution.py
@@ -11,7 +11,7 @@
 F32 = jnp.float32
 BF16 = jnp.bfloat16
 LANES = 128
-GROUP = 16
+GROUP = 32
 
 
 def split3(x):
@@ -1073,7 +1073,7 @@
             pltpu.VMEM((3, LANES, LANES), F32),
             pltpu.VMEM(field, F32),
             pltpu.VMEM(own, F32),
-            pltpu.SemaphoreType.DMA((5,)),
+            pltpu.SemaphoreType.DMA((9,)),
         ],
         far_out=True,
     )

time: 55.7 us -> 55.7 us (level)
  waiting for transfers between devices: 11.5 us -> 13 us
  Pallas kernels: 13.6 us -> 12.7 us
  starting transfers between devices: 19.9 us -> 19.3 us
    ppermute x4, waiting for transfers between devices: 4.97 us -> 6.3 us  [near(): lax.ppermute(to_b, 'gx', pairs_of(count, 1, 1))]
    pallas_call x10, Pallas kernels: 13.6 us -> 12.7 us  [call(): pl.pallas_call(kernel, name=name, out_shape=[jax.ShapeDtypeStruct(shape,...]
    ppermute x4, starting transfers between devices: 2.44 us -> 1.84 us  [far(): lax.ppermute(value, 'gx', pairs_of(count, 2, 1))]
  transfers between devices with their start and end apart: 20 -> 20, of which waited for: 7 -> 7; matrix products, arithmetic and copies ran while one was open for 0% -> 0% of each run, Pallas kernels for 15% -> 13%
where the time goes in v6:
time: 55.7 us; the launch traced here: 55.5 us
  starting transfers between devices  19.3 us (35%)
  waiting for transfers between devices  13 us (23%)
  Pallas kernels  12.7 us (23%)
  blocking collectives  9.7 us (17%)
  between operations  0.77 us (1%)
    ppermute x4, starting transfers between devices, near(): lax.ppermute(to_b, 'gx', pairs_of(count, 1, 1))  13.5 us
    pallas_call x10, Pallas kernels, call(): pl.pallas_call(kernel, name=name, out_shape=[jax.ShapeDtypeStruct(shape,...  12.7 us
    all_to_all x1, blocking collectives, per_device(): totals = lax.all_to_all(moments, ('gx', 'gy'), 0, 0)  9.7 us
    ppermute x4, waiting for transfers between devices, far(): lax.ppermute(value, 'gx', pairs_of(count, 2, 1))  6.63 us
    ppermute x4, waiting for transfers between devices, near(): lax.ppermute(to_b, 'gx', pairs_of(count, 1, 1))  6.3 us
    ppermute x4, starting transfers between devices, near(): lax.ppermute(to_a, 'gx', pairs_of(count, 1, 0))  3.27 us
    ppermute x4, starting transfers between devices, far(): lax.ppermute(value, 'gx', pairs_of(count, 2, 1))  1.84 us
  transfers between devices with their start and end apart: 20, of which 7 were waited for; matrix products, arithmetic and copies ran while one was open for 0% of the time, Pallas kernels for 13%

profile of v6, /device:TPU:0, one launch (start us, length us, event | category | flops | bytes accessed | tf_op | source)
XLA Modules:
  0.0 55.5 jit_solution(434000571168144480)
XLA Ops:
  0.6 1.0 %opening.1 = (f32[16,512]{1,0:T(8,128)S(1)}, f32[16,512]{1,0:T(8,128)S(1)}, bf16[512,128]{1,0:T(8,128)(2,1)S(1)}, f32[24,128]{1,0:T(8,128)S(1)}, f32[24,128]{1,0...) custom-call(f32[8]{0:T(128)} %perm_table_hbm.1, s32[16,512]{1,0:T(8,128)} %class_hbm.1, ...), custom_call_target="tpu_custom_call" | custom-call | tf_op jit(solution)/shard_map/opening/pallas_call | solution.py:813
  1.7 0.5 collective-permute-start
  2.2 2.6 %collective-permute-start.1 = (f32[24,128]{1,0:T(8,128)S(1)}, f32[24,128]{1,0:T(8,128)S(1)}, u32[]{:S(2)}, u32[]{:S(2)}) collective-permute-start(f32[24,128]{1,0:T(8,128)S(1)} %get-tuple-element.82), channel_id=1, source_target_pairs={{0,2},{2,0},{4,6},{6,4},{8,10},{10,8},{12,14},{14,12},{1,3},{3,1},... | collective-permute-start | bytes 36872 | tf_op jit(solution)/shard_map/ppermute | solution.py:851
  4.7 3.6 %collective-permute-start.2 = (f32[24,128]{1,0:T(8,128)S(1)}, f32[24,128]{1,0:T(8,128)S(1)}, u32[]{:S(2)}, u32[]{:S(2)}) collective-permute-start(f32[24,128]{1,0:T(8,128)S(1)} %get-tuple-element.83), channel_id=1, source_target_pairs={{2,4},{4,2},{6,8},{8,6},{10,12},{12,10},{14,0},{0,14},{3,5},{5,3},... | collective-permute-start | bytes 36872 | tf_op jit(solution)/shard_map/ppermute | solution.py:852
  8.3 0.0 collective-permute-done.border_ref
  8.3 0.5 collective-permute-start.4
  8.8 0.0 collective-permute-start.3
  8.8 2.4 %inside.1 = (f32[16,512]{1,0:T(8,128)S(1)}, f32[16,512]{1,0:T(8,128)S(1)}, f32[1,512]{1,0:T(1,128)S(1)}, f32[2,32,512]{2,1,0:T(8,128)S(1)}, f32[5,16,512]{2,1,0:...) custom-call(s32[2]{0:T(128)} %bitcast.7, ...), custom_call_target="tpu_custom_call" | custom-call | flops 4000000000 | bytes 12000000 | tf_op jit(solution)/shard_map/inside/pallas_call | solution.py:813
  11.2 0.0 collective-permute-done.1.near_a_ref
  11.2 0.0 collective-permute-done.2.near_b_ref
  11.2 2.6 %collective-permute-done.4.far_d_ref = f32[16,128]{1,0:T(8,128)S(1)} collective-permute-done((f32[16,128]{1,0:T(8,128)S(1)}, f32[16,128]{1,0:T(8,128)S(1)}, u32[]{:S(2)}, u32[]{:S(2)}) %collective-permute-start.4) | collective-permute-done | bytes 8224 | tf_op jit(solution)/shard_map/ppermute | solution.py:858
  13.8 0.0 collective-permute-done.3.far_c_ref
  13.8 1.1 %first_vector.1 = (f32[6,16,512]{2,1,0:T(8,128)S(1)}, f32[16,512]{1,0:T(8,128)S(1)}, f32[16,512]{1,0:T(8,128)S(1)}, f32[2,16,512]{2,1,0:T(8,128)S(1)}, f32[16,51...) custom-call(f32[1,512]{1,0:T(1,128)S(1)} %get-tuple-element.77.live_, ...), custom_call_target="tpu_custom_call", output_to_operand_aliasing={{10}: (21, {})} | custom-call | tf_op jit(solution)/shard_map/first_vector/pallas_call | solution.py:813
  14.8 0.0 collective-permute-start.7
  14.9 0.1 collective-permute-start.5
  15.0 3.5 %collective-permute-start.6 = (f32[176,128]{1,0:T(8,128)S(1)}, f32[176,128]{1,0:T(8,128)S(1)}, u32[]{:S(2)}, u32[]{:S(2)}) collective-permute-start(f32[176,128]{1,0:T(8,128)S(1)} %get-tuple-element.99), channel_id=1, source_target_pairs={{2,4},{4,2},{6,8},{8,6},{10,12},{12,10},{14,0},{0,14},{3,5},{5,3},... | collective-permute-start | bytes 270344 | tf_op jit(solution)/shard_map/ppermute | solution.py:852
  18.4 0.0 collective-permute-done.7.core_ref.core_in_ref
  18.4 0.8 %collective-permute-start.9 = (f32[48,128]{1,0:T(8,128)S(1)}, f32[48,128]{1,0:T(8,128)S(1)}, u32[]{:S(2)}, u32[]{:S(2)}) collective-permute-start(f32[48,128]{1,0:T(8,128)S(1)} %get-tuple-element.102), channel_id=1, source_target_pairs={{4,8},{8,4},{6,10},{10,6},{12,0},{0,12},{14,2},{2,14},{5,9},{9,5},... | collective-permute-start | bytes 73736 | tf_op jit(solution)/shard_map/ppermute | solution.py:858
  19.3 0.0 collective-permute-start.8
  19.3 1.9 %interior_1.1 = (f32[32,16,512]{2,1,0:T(8,128)S(1)}, f32[32,256]{1,0:T(8,128)S(1)}, f32[16,128]{1,0:T(8,128)S(1)}, f32[8,32]{1,0:T(8,128)S(1)}) custom-call(f32[32,16,512]{2,1,0:T(8,128)S(1)} %get-tuple-element.109.v_ref.before_ref.v0_ref, f32[32,16,512]{2,1,0:T(8,128)S(1)} %get-tuple-element.109.v_ref.before_ref.v0_ref, ...), custom_call_target="tpu_custom_call" | custom-call | flops 4000000000 | bytes 12000000 | tf_op jit(solution)/shard_map/interior_1/pallas_call | solution.py:813
  21.2 0.0 collective-permute-done.5.near_a_ref
  21.2 2.0 %collective-permute-done.6.near_b_ref = f32[176,128]{1,0:T(8,128)S(1)} collective-permute-done((f32[176,128]{1,0:T(8,128)S(1)}, f32[176,128]{1,0:T(8,128)S(1)}, u32[]{:S(2)}, u32[]{:S(2)}) %collective-permute-start.6) | collective-permute-done | bytes 90144 | tf_op jit(solution)/shard_map/ppermute | solution.py:852
  23.2 0.9 %collective-permute-done.9.far_d_ref = f32[48,128]{1,0:T(8,128)S(1)} collective-permute-done((f32[48,128]{1,0:T(8,128)S(1)}, f32[48,128]{1,0:T(8,128)S(1)}, u32[]{:S(2)}, u32[]{:S(2)}) %collective-permute-start.9) | collective-permute-done | bytes 24608 | tf_op jit(solution)/shard_map/ppermute | solution.py:858
  24.1 0.0 collective-permute-done.8.far_c_ref
  24.1 1.0 %finish_1.1 = (f32[16,512]{1,0:T(8,128)S(1)}, f32[16,512]{1,0:T(8,128)S(1)}, f32[16,512]{1,0:T(8,128)S(1)}, f32[16,512]{1,0:T(8,128)S(1)}, f32[160,128]{1,0:T(8,...) custom-call(f32[16,512]{1,0:T(8,128)S(1)} %get-tuple-element.97.vf_r, ...), custom_call_target="tpu_custom_call", output_to_operand_aliasing={{8}: (20, {})} | custom-call | tf_op jit(solution)/shard_map/finish_1/pallas_call | solution.py:813
  25.0 0.1 collective-permute-start.12
  25.1 0.3 collective-permute-start.10
  25.4 3.2 %collective-permute-start.11 = (f32[160,128]{1,0:T(8,128)S(1)}, f32[160,128]{1,0:T(8,128)S(1)}, u32[]{:S(2)}, u32[]{:S(2)}) collective-permute-start(f32[160,128]{1,0:T(8,128)S(1)} %get-tuple-element.115), channel_id=1, source_target_pairs={{2,4},{4,2},{6,8},{8,6},{10,12},{12,10},{14,0},{0,14},{3,5},{5,3},... | collective-permute-start | bytes 245768 | tf_op jit(solution)/shard_map/ppermute | solution.py:852
  28.7 0.0 collective-permute-done.12.core_ref.core_in_ref
  28.7 0.3 collective-permute-start.14
  28.9 0.0 collective-permute-start.13
  28.9 1.9 %interior_2.1 = (f32[32,16,512]{2,1,0:T(8,128)S(1)}, f32[32,256]{1,0:T(8,128)S(1)}, f32[16,128]{1,0:T(8,128)S(1)}, f32[8,32]{1,0:T(8,128)S(1)}) custom-call(f32[32,16,512]{2,1,0:T(8,128)S(1)} %get-tuple-element.123.v_ref.before_ref.v1_ref, f32[32,16,512]{2,1,0:T(8,128)S(1)} %get-tuple-element.109.v_ref.before_ref.v0_ref, ...), custom_call_target="tpu_custom_call" | custom-call | flops 4000000000 | bytes 12000000 | tf_op jit(solution)/shard_map/interior_2/pallas_call | solution.py:813
  30.9 0.0 collective-permute-done.10.near_a_ref
  30.9 2.2 %collective-permute-done.11.near_b_ref = f32[160,128]{1,0:T(8,128)S(1)} collective-permute-done((f32[160,128]{1,0:T(8,128)S(1)}, f32[160,128]{1,0:T(8,128)S(1)}, u32[]{:S(2)}, u32[]{:S(2)}) %collective-permute-start.11) | collective-permute-done | bytes 81952 | tf_op jit(solution)/shard_map/ppermute | solution.py:852
  33.1 1.1 %collective-permute-done.14.far_d_ref = f32[32,128]{1,0:T(8,128)S(1)} collective-permute-done((f32[32,128]{1,0:T(8,128)S(1)}, f32[32,128]{1,0:T(8,128)S(1)}, u32[]{:S(2)}, u32[]{:S(2)}) %collective-permute-start.14) | collective-permute-done | bytes 16416 | tf_op jit(solution)/shard_map/ppermute | solution.py:858
  34.2 0.0 collective-permute-done.13.far_c_ref
  34.2 0.8 %finish_2.1 = (f32[16,512]{1,0:T(8,128)S(1)}, f32[16,512]{1,0:T(8,128)S(1)}, f32[32,256]{1,0:T(8,128)S(1)}, f32[80,128]{1,0:T(8,128)S(1)}, f32[80,128]{1,0:T(8,1...) custom-call(f32[16,512]{1,0:T(8,128)S(1)} %get-tuple-element.113.vf_, ...), custom_call_target="tpu_custom_call", output_to_operand_aliasing={{7}: (20, {})} | custom-call | tf_op jit(solution)/shard_map/finish_2/pallas_call | solution.py:813
  35.0 0.1 collective-permute-start.17
  35.1 0.3 collective-permute-start.15
  35.4 3.2 %collective-permute-start.16 = (f32[80,128]{1,0:T(8,128)S(1)}, f32[80,128]{1,0:T(8,128)S(1)}, u32[]{:S(2)}, u32[]{:S(2)}) collective-permute-start(f32[80,128]{1,0:T(8,128)S(1)} %get-tuple-element.129), channel_id=1, source_target_pairs={{2,4},{4,2},{6,8},{8,6},{10,12},{12,10},{14,0},{0,14},{3,5},{5,3},... | collective-permute-start | bytes 122888 | tf_op jit(solution)/shard_map/ppermute | solution.py:852
  38.6 0.0 collective-permute-done.17.core_ref
  38.6 0.3 collective-permute-start.19
  38.9 0.0 collective-permute-start.18
  38.9 1.0 %energy.1.dots3_ref = f32[8,32]{1,0:T(8,128)S(1)} custom-call(f32[32,16,512]{2,1,0:T(8,128)S(1)} %get-tuple-element.134.v_ref.v2_ref, f32[32,16,512]{2,1,0:T(8,128)S(1)} %get-tuple-element.123.v_ref.before_ref.v1_ref, f32[16,512]{1,0:T(8,128)S(1)} %get-tuple-element.127.vf_ref.f2_ref, f32[16,512]{1,0:T(8,128)S(1)} %get-tuple-element.113.vf_ref.before_f_ref.f1_ref, ...), custom_call_target="tpu_custom_call" | custom-call | flops 4000000000 | bytes 12000000 | tf_op jit(solution)/shard_map/energy/pallas_call | solution.py:813
  39.9 0.0 collective-permute-done.15.near_a_ref
  39.9 2.2 %collective-permute-done.16.near_b_ref = f32[80,128]{1,0:T(8,128)S(1)} collective-permute-done((f32[80,128]{1,0:T(8,128)S(1)}, f32[80,128]{1,0:T(8,128)S(1)}, u32[]{:S(2)}, u32[]{:S(2)}) %collective-permute-start.16) | collective-permute-done | bytes 40992 | tf_op jit(solution)/shard_map/ppermute | solution.py:852
  42.1 2.0 %collective-permute-done.19.far_d_ref = f32[16,128]{1,0:T(8,128)S(1)} collective-permute-done((f32[16,128]{1,0:T(8,128)S(1)}, f32[16,128]{1,0:T(8,128)S(1)}, u32[]{:S(2)}, u32[]{:S(2)}) %collective-permute-start.19) | collective-permute-done | bytes 8224 | tf_op jit(solution)/shard_map/ppermute | solution.py:858
  44.1 0.0 collective-permute-done.18.far_c_ref
  44.1 0.3 moments.1
  44.4 9.7 %all_to_all.5.totals_ref = f32[16,2,128]{2,1,0:T(2,128)S(1)} all-to-all(f32[16,2,128]{2,1,0:T(2,128)S(1)} %moments.1), channel_id=1, replica_groups=mesh['grp'=2,'gx'=8,'gy'=2] {'gx','gy'}, dimensions={0} | all-to-all | bytes 32768 | tf_op jit(solution)/shard_map/all_to_all | solution.py:1066
  54.1 1.4 %iterate.1 = (f32[32,16,512]{2,1,0:T(8,128)}, f32[16,512]{1,0:T(8,128)}) custom-call(f32[16,2,128]{2,1,0:T(2,128)S(1)} %all_to_all.5.totals_ref, f32[32,16,512]{2,1,0:T(8,128)S(1)} %get-tuple-element.109.v_ref.before_ref.v0_ref, f32[32,16,512]{2,1,0:T(8,128)S(1)} %get-tuple-element.123.v_ref.before_ref.v1_ref, ...), custom_call_target="tpu_custom_call" | custom-call | tf_op jit(solution)/shard_map/iterate/pallas_call | solution.py:813
Async XLA Ops:
  1.7 6.7 %collective-permute-start = (f32[16,128]{1,0:T(8,128)S(1)}, f32[16,128]{1,0:T(8,128)S(1)}, u32[]{:S(2)}, u32[]{:S(2)}) collective-permute-start(f32[16,128]{1,0:T(8,128)S(1)} %get-tuple-element.73), channel_id=1, source_target_pairs={{0,1},{1,0},{2,3},{3,2},{4,5},{5,4},{6,7},{7,6},{8,9},{9,8},{10,11... | collective-permute-start | bytes 24584 | tf_op jit(solution)/shard_map/ppermute | solution.py:862
  2.2 9.0 %collective-permute-start.1 = (f32[24,128]{1,0:T(8,128)S(1)}, f32[24,128]{1,0:T(8,128)S(1)}, u32[]{:S(2)}, u32[]{:S(2)}) collective-permute-start(f32[24,128]{1,0:T(8,128)S(1)} %get-tuple-element.82), channel_id=1, source_target_pairs={{0,2},{2,0},{4,6},{6,4},{8,10},{10,8},{12,14},{14,12},{1,3},{3,1},... | collective-permute-start | bytes 36872 | tf_op jit(solution)/shard_map/ppermute | solution.py:851
  4.7 6.4 %collective-permute-start.2 = (f32[24,128]{1,0:T(8,128)S(1)}, f32[24,128]{1,0:T(8,128)S(1)}, u32[]{:S(2)}, u32[]{:S(2)}) collective-permute-start(f32[24,128]{1,0:T(8,128)S(1)} %get-tuple-element.83), channel_id=1, source_target_pairs={{2,4},{4,2},{6,8},{8,6},{10,12},{12,10},{14,0},{0,14},{3,5},{5,3},... | collective-permute-start | bytes 36872 | tf_op jit(solution)/shard_map/ppermute | solution.py:852
  8.3 5.4 %collective-permute-start.4 = (f32[16,128]{1,0:T(8,128)S(1)}, f32[16,128]{1,0:T(8,128)S(1)}, u32[]{:S(2)}, u32[]{:S(2)}) collective-permute-start(f32[16,128]{1,0:T(8,128)S(1)} %get-tuple-element.84), channel_id=1, source_target_pairs={{4,8},{8,4},{6,10},{10,6},{12,0},{0,12},{14,2},{2,14},{5,9},{9,5},... | collective-permute-start | bytes 24584 | tf_op jit(solution)/shard_map/ppermute | solution.py:858
  8.8 5.0 %collective-permute-start.3 = (f32[16,128]{1,0:T(8,128)S(1)}, f32[16,128]{1,0:T(8,128)S(1)}, u32[]{:S(2)}, u32[]{:S(2)}) collective-permute-start(f32[16,128]{1,0:T(8,128)S(1)} %get-tuple-element.84), channel_id=1, source_target_pairs={{0,4},{4,0},{2,6},{6,2},{8,12},{12,8},{10,14},{14,10},{1,5},{5,1},... | collective-permute-start | bytes 24584 | tf_op jit(solution)/shard_map/ppermute | solution.py:857
  14.8 3.6 %collective-permute-start.7 = (f32[176,128]{1,0:T(8,128)S(1)}, f32[176,128]{1,0:T(8,128)S(1)}, u32[]{:S(2)}, u32[]{:S(2)}) collective-permute-start(f32[176,128]{1,0:T(8,128)S(1)} %get-tuple-element.101), channel_id=1, source_target_pairs={{0,1},{1,0},{2,3},{3,2},{4,5},{5,4},{6,7},{7,6},{8,9},{9,8},{10,11... | collective-permute-start | bytes 270344 | tf_op jit(solution)/shard_map/ppermute | solution.py:862
  14.9 6.3 %collective-permute-start.5 = (f32[176,128]{1,0:T(8,128)S(1)}, f32[176,128]{1,0:T(8,128)S(1)}, u32[]{:S(2)}, u32[]{:S(2)}) collective-permute-start(f32[176,128]{1,0:T(8,128)S(1)} %get-tuple-element.98), channel_id=1, source_target_pairs={{0,2},{2,0},{4,6},{6,4},{8,10},{10,8},{12,14},{14,12},{1,3},{3,1},... | collective-permute-start | bytes 270344 | tf_op jit(solution)/shard_map/ppermute | solution.py:851
  15.0 8.2 %collective-permute-start.6 = (f32[176,128]{1,0:T(8,128)S(1)}, f32[176,128]{1,0:T(8,128)S(1)}, u32[]{:S(2)}, u32[]{:S(2)}) collective-permute-start(f32[176,128]{1,0:T(8,128)S(1)} %get-tuple-element.99), channel_id=1, source_target_pairs={{2,4},{4,2},{6,8},{8,6},{10,12},{12,10},{14,0},{0,14},{3,5},{5,3},... | collective-permute-start | bytes 270344 | tf_op jit(solution)/shard_map/ppermute | solution.py:852
  18.4 5.6 %collective-permute-start.9 = (f32[48,128]{1,0:T(8,128)S(1)}, f32[48,128]{1,0:T(8,128)S(1)}, u32[]{:S(2)}, u32[]{:S(2)}) collective-permute-start(f32[48,128]{1,0:T(8,128)S(1)} %get-tuple-element.102), channel_id=1, source_target_pairs={{4,8},{8,4},{6,10},{10,6},{12,0},{0,12},{14,2},{2,14},{5,9},{9,5},... | collective-permute-start | bytes 73736 | tf_op jit(solution)/shard_map/ppermute | solution.py:858
  19.3 4.8 %collective-permute-start.8 = (f32[48,128]{1,0:T(8,128)S(1)}, f32[48,128]{1,0:T(8,128)S(1)}, u32[]{:S(2)}, u32[]{:S(2)}) collective-permute-start(f32[48,128]{1,0:T(8,128)S(1)} %get-tuple-element.102), channel_id=1, source_target_pairs={{0,4},{4,0},{2,6},{6,2},{8,12},{12,8},{10,14},{14,10},{1,5},{5,1},... | collective-permute-start | bytes 73736 | tf_op jit(solution)/shard_map/ppermute | solution.py:857
  25.0 3.6 %collective-permute-start.12 = (f32[144,128]{1,0:T(8,128)S(1)}, f32[144,128]{1,0:T(8,128)S(1)}, u32[]{:S(2)}, u32[]{:S(2)}) collective-permute-start(f32[144,128]{1,0:T(8,128)S(1)} %get-tuple-element.117), channel_id=1, source_target_pairs={{0,1},{1,0},{2,3},{3,2},{4,5},{5,4},{6,7},{7,6},{8,9},{9,8},{10,11... | collective-permute-start | bytes 221192 | tf_op jit(solution)/shard_map/ppermute | solution.py:862
  25.1 5.8 %collective-permute-start.10 = (f32[160,128]{1,0:T(8,128)S(1)}, f32[160,128]{1,0:T(8,128)S(1)}, u32[]{:S(2)}, u32[]{:S(2)}) collective-permute-start(f32[160,128]{1,0:T(8,128)S(1)} %get-tuple-element.114), channel_id=1, source_target_pairs={{0,2},{2,0},{4,6},{6,4},{8,10},{10,8},{12,14},{14,12},{1,3},{3,1},... | collective-permute-start | bytes 245768 | tf_op jit(solution)/shard_map/ppermute | solution.py:851
  25.4 7.6 %collective-permute-start.11 = (f32[160,128]{1,0:T(8,128)S(1)}, f32[160,128]{1,0:T(8,128)S(1)}, u32[]{:S(2)}, u32[]{:S(2)}) collective-permute-start(f32[160,128]{1,0:T(8,128)S(1)} %get-tuple-element.115), channel_id=1, source_target_pairs={{2,4},{4,2},{6,8},{8,6},{10,12},{12,10},{14,0},{0,14},{3,5},{5,3},... | collective-permute-start | bytes 245768 | tf_op jit(solution)/shard_map/ppermute | solution.py:852
  28.7 5.5 %collective-permute-start.14 = (f32[32,128]{1,0:T(8,128)S(1)}, f32[32,128]{1,0:T(8,128)S(1)}, u32[]{:S(2)}, u32[]{:S(2)}) collective-permute-start(f32[32,128]{1,0:T(8,128)S(1)} %get-tuple-element.118), channel_id=1, source_target_pairs={{4,8},{8,4},{6,10},{10,6},{12,0},{0,12},{14,2},{2,14},{5,9},{9,5},... | collective-permute-start | bytes 49160 | tf_op jit(solution)/shard_map/ppermute | solution.py:858
  28.9 5.3 %collective-permute-start.13 = (f32[32,128]{1,0:T(8,128)S(1)}, f32[32,128]{1,0:T(8,128)S(1)}, u32[]{:S(2)}, u32[]{:S(2)}) collective-permute-start(f32[32,128]{1,0:T(8,128)S(1)} %get-tuple-element.118), channel_id=1, source_target_pairs={{0,4},{4,0},{2,6},{6,2},{8,12},{12,8},{10,14},{14,10},{1,5},{5,1},... | collective-permute-start | bytes 49160 | tf_op jit(solution)/shard_map/ppermute | solution.py:857
  35.0 3.6 %collective-permute-start.17 = (f32[80,128]{1,0:T(8,128)S(1)}, f32[80,128]{1,0:T(8,128)S(1)}, u32[]{:S(2)}, u32[]{:S(2)}) collective-permute-start(f32[80,128]{1,0:T(8,128)S(1)} %get-tuple-element.131), channel_id=1, source_target_pairs={{0,1},{1,0},{2,3},{3,2},{4,5},{5,4},{6,7},{7,6},{8,9},{9,8},{10,11... | collective-permute-start | bytes 122888 | tf_op jit(solution)/shard_map/ppermute | solution.py:862
  35.1 4.8 %collective-permute-start.15 = (f32[80,128]{1,0:T(8,128)S(1)}, f32[80,128]{1,0:T(8,128)S(1)}, u32[]{:S(2)}, u32[]{:S(2)}) collective-permute-start(f32[80,128]{1,0:T(8,128)S(1)} %get-tuple-element.128), channel_id=1, source_target_pairs={{0,2},{2,0},{4,6},{6,4},{8,10},{10,8},{12,14},{14,12},{1,3},{3,1},... | collective-permute-start | bytes 122888 | tf_op jit(solution)/shard_map/ppermute | solution.py:851
  35.4 6.7 %collective-permute-start.16 = (f32[80,128]{1,0:T(8,128)S(1)}, f32[80,128]{1,0:T(8,128)S(1)}, u32[]{:S(2)}, u32[]{:S(2)}) collective-permute-start(f32[80,128]{1,0:T(8,128)S(1)} %get-tuple-element.129), channel_id=1, source_target_pairs={{2,4},{4,2},{6,8},{8,6},{10,12},{12,10},{14,0},{0,14},{3,5},{5,3},... | collective-permute-start | bytes 122888 | tf_op jit(solution)/shard_map/ppermute | solution.py:852
  38.6 5.4 %collective-permute-start.19 = (f32[16,128]{1,0:T(8,128)S(1)}, f32[16,128]{1,0:T(8,128)S(1)}, u32[]{:S(2)}, u32[]{:S(2)}) collective-permute-start(f32[16,128]{1,0:T(8,128)S(1)} %get-tuple-element.132), channel_id=1, source_target_pairs={{4,8},{8,4},{6,10},{10,6},{12,0},{0,12},{14,2},{2,14},{5,9},{9,5},... | collective-permute-start | bytes 24584 | tf_op jit(solution)/shard_map/ppermute | solution.py:858
  38.9 5.2 %collective-permute-start.18 = (f32[16,128]{1,0:T(8,128)S(1)}, f32[16,128]{1,0:T(8,128)S(1)}, u32[]{:S(2)}, u32[]{:S(2)}) collective-permute-start(f32[16,128]{1,0:T(8,128)S(1)} %get-tuple-element.132), channel_id=1, source_target_pairs={{0,4},{4,0},{2,6},{6,2},{8,12},{12,8},{10,14},{14,10},{1,5},{5,1},... | collective-permute-start | bytes 24584 | tf_op jit(solution)/shard_map/ppermute | solution.py:857

commit v7 on v5

--- a/solution.py
+++ b/solution.py
@@ -896,7 +896,12 @@
         far_c, far_d = far(sent)
         return near_a, near_b, far_c, far_d, core_in
 
-    near_a, near_b, far_c, far_d, border = exchange(to_a, to_b, sent, border)
+    near_a = lax.ppermute(to_a, "gx", pairs_of(count, 1, 0))
+    far_d = lax.ppermute(sent, "gx", pairs_of(count, 2, 1))
+    border = core(border)
+    sent, to_b, border = lax.optimization_barrier((sent, to_b, border))
+    near_b = lax.ppermute(to_b, "gx", pairs_of(count, 1, 1))
+    far_c = lax.ppermute(sent, "gx", pairs_of(count, 2, 0))
     source_f, storage_in, live, edges, coef, oy, ox, weight, *network, v0, margin_in, column = call(
         inside_kernel,
         "inside",

time: 55.7 us -> 56.1 us (level)
  blocking collectives: 9.7 us -> 11.1 us
  starting transfers between devices: 19.9 us -> 18.6 us
    ppermute x4 -> x3, starting transfers between devices: 13.5 us -> 3.59 us  [near(): lax.ppermute(to_b, 'gx', pairs_of(count, 1, 1))]
    ppermute x0 -> x4, starting transfers between devices: none -> 7.14 us  [the longest x1 4.67 us: per_device(): far_d = lax.ppermute(sent, 'gx', pairs_of(count, 2, 1))]
    ppermute x4 -> x3, waiting for transfers between devices: 6.49 us -> 0.08 us  [far(): lax.ppermute(value, 'gx', pairs_of(count, 2, 1))]
    ppermute x4 -> x3, waiting for transfers between devices: 4.97 us -> 8.66 us  [near(): lax.ppermute(to_b, 'gx', pairs_of(count, 1, 1))]
    ppermute x0 -> x4, waiting for transfers between devices: none -> 2.87 us  [the longest x1 2.74 us: per_device(): near_b = lax.ppermute(to_b, 'gx', pairs_of(count, 1, 1))]
    ppermute x4 -> x3, starting transfers between devices: 0.01 us -> 1.44 us  [far(): lax.ppermute(value, 'gx', pairs_of(count, 2, 0))]
    all_to_all x1, blocking collectives: 9.7 us -> 11.1 us  [per_device(): totals = lax.all_to_all(moments, ('gx', 'gy'), 0, 0)]
    ppermute x4 -> x3, starting transfers between devices: 2.44 us -> 3.07 us  [far(): lax.ppermute(value, 'gx', pairs_of(count, 2, 1))]
  transfers between devices with their start and end apart: 20 -> 20, of which waited for: 7 -> 7; matrix products, arithmetic and copies ran while one was open for 0% -> 0% of each run, Pallas kernels for 15% -> 14%
where the time goes in v7:
time: 56.1 us; the launch traced here: 55.8 us
  starting transfers between devices  18.6 us (33%)
  Pallas kernels  13.6 us (24%)
  waiting for transfers between devices  11.8 us (21%)
  blocking collectives  11.1 us (20%)
  between operations  0.76 us (1%)
    pallas_call x10, Pallas kernels, call(): pl.pallas_call(kernel, name=name, out_shape=[jax.ShapeDtypeStruct(shape,...  13.6 us
    all_to_all x1, blocking collectives, per_device(): totals = lax.all_to_all(moments, ('gx', 'gy'), 0, 0)  11.1 us
    ppermute x3, waiting for transfers between devices, near(): lax.ppermute(to_b, 'gx', pairs_of(count, 1, 1))  8.66 us
    ppermute x1, starting transfers between devices, per_device(): far_d = lax.ppermute(sent, 'gx', pairs_of(count, 2, 1))  4.67 us
    ppermute x3, starting transfers between devices, near(): lax.ppermute(to_b, 'gx', pairs_of(count, 1, 1))  3.59 us
    ppermute x3, starting transfers between devices, far(): lax.ppermute(value, 'gx', pairs_of(count, 2, 1))  3.07 us
    ppermute x1, waiting for transfers between devices, per_device(): near_b = lax.ppermute(to_b, 'gx', pairs_of(count, 1, 1))  2.74 us
    ppermute x3, starting transfers between devices, near(): lax.ppermute(to_a, 'gx', pairs_of(count, 1, 0))  2.67 us
  transfers between devices with their start and end apart: 20, of which 7 were waited for; matrix products, arithmetic and copies ran while one was open for 0% of the time, Pallas kernels for 14%

profile of v7, /device:TPU:0, one launch (start us, length us, event | category | flops | bytes accessed | tf_op | source)
XLA Modules:
  0.0 55.8 jit_solution(1920491775387412652)
XLA Ops:
  0.6 1.0 %opening.1 = (f32[16,512]{1,0:T(8,128)S(1)}, f32[16,512]{1,0:T(8,128)S(1)}, bf16[512,128]{1,0:T(8,128)(2,1)S(1)}, f32[24,128]{1,0:T(8,128)S(1)}, f32[24,128]{1,0...) custom-call(f32[8]{0:T(128)} %perm_table_hbm.1, s32[16,512]{1,0:T(8,128)} %class_hbm.1, ...), custom_call_target="tpu_custom_call" | custom-call | tf_op jit(solution)/shard_map/opening/pallas_call | solution.py:813
  1.7 0.5 collective-permute-start
  2.2 4.7 %collective-permute-start.4 = (f32[16,128]{1,0:T(8,128)S(1)}, f32[16,128]{1,0:T(8,128)S(1)}, u32[]{:S(2)}, u32[]{:S(2)}) collective-permute-start(f32[16,128]{1,0:T(8,128)S(1)} %get-tuple-element.86), channel_id=1, source_target_pairs={{4,8},{8,4},{6,10},{10,6},{12,0},{0,12},{14,2},{2,14},{5,9},{9,5},... | collective-permute-start | bytes 24584 | tf_op jit(solution)/shard_map/ppermute | solution.py:900
  6.9 1.5 %collective-permute-start.1 = (f32[24,128]{1,0:T(8,128)S(1)}, f32[24,128]{1,0:T(8,128)S(1)}, u32[]{:S(2)}, u32[]{:S(2)}) collective-permute-start(f32[24,128]{1,0:T(8,128)S(1)} %get-tuple-element.84), channel_id=1, source_target_pairs={{0,2},{2,0},{4,6},{6,4},{8,10},{10,8},{12,14},{14,12},{1,3},{3,1},... | collective-permute-start | bytes 36872 | tf_op jit(solution)/shard_map/ppermute | solution.py:899
  8.3 0.0 collective-permute-done.border_ref
  8.3 0.0 collective-permute-start.3
  8.3 1.0 %collective-permute-start.2 = (f32[24,128]{1,0:T(8,128)S(1)}, f32[24,128]{1,0:T(8,128)S(1)}, u32[]{:S(2)}, u32[]{:S(2)}) collective-permute-start(f32[24,128]{1,0:T(8,128)S(1)} %get-tuple-element.85), channel_id=1, source_target_pairs={{2,4},{4,2},{6,8},{8,6},{10,12},{12,10},{14,0},{0,14},{3,5},{5,3},... | collective-permute-start | bytes 36872 | tf_op jit(solution)/shard_map/ppermute | solution.py:903
  9.3 2.5 %inside.1 = (f32[16,512]{1,0:T(8,128)S(1)}, f32[16,512]{1,0:T(8,128)S(1)}, f32[1,512]{1,0:T(1,128)S(1)}, f32[2,32,512]{2,1,0:T(8,128)S(1)}, f32[5,16,512]{2,1,0:...) custom-call(s32[2]{0:T(128)} %bitcast.7, ...), custom_call_target="tpu_custom_call" | custom-call | flops 4000000000 | bytes 12000000 | tf_op jit(solution)/shard_map/inside/pallas_call | solution.py:813
  11.9 0.0 collective-permute-done.4.far_d_ref
  11.9 0.0 collective-permute-done.1.near_a_ref
  11.9 0.1 collective-permute-done.3.far_c_ref
  12.0 2.7 %collective-permute-done.2.near_b_ref = f32[24,128]{1,0:T(8,128)S(1)} collective-permute-done((f32[24,128]{1,0:T(8,128)S(1)}, f32[24,128]{1,0:T(8,128)S(1)}, u32[]{:S(2)}, u32[]{:S(2)}) %collective-permute-start.2) | collective-permute-done | bytes 12320 | tf_op jit(solution)/shard_map/ppermute | solution.py:903
  14.7 1.1 %first_vector.1 = (f32[6,16,512]{2,1,0:T(8,128)S(1)}, f32[16,512]{1,0:T(8,128)S(1)}, f32[16,512]{1,0:T(8,128)S(1)}, f32[2,16,512]{2,1,0:T(8,128)S(1)}, f32[16,51...) custom-call(f32[1,512]{1,0:T(1,128)S(1)} %get-tuple-element.79.live_, ...), custom_call_target="tpu_custom_call", output_to_operand_aliasing={{10}: (21, {})} | custom-call | tf_op jit(solution)/shard_map/first_vector/pallas_call | solution.py:813
  15.8 0.0 collective-permute-start.7
  15.9 0.1 collective-permute-start.5
  15.9 1.0 %collective-permute-start.6 = (f32[176,128]{1,0:T(8,128)S(1)}, f32[176,128]{1,0:T(8,128)S(1)}, u32[]{:S(2)}, u32[]{:S(2)}) collective-permute-start(f32[176,128]{1,0:T(8,128)S(1)} %get-tuple-element.101), channel_id=1, source_target_pairs={{2,4},{4,2},{6,8},{8,6},{10,12},{12,10},{14,0},{0,14},{3,5},{5,3},... | collective-permute-start | bytes 270344 | tf_op jit(solution)/shard_map/ppermute | solution.py:852
  17.0 0.2 collective-permute-done.7.core_ref.core_in_ref
  17.1 1.4 %collective-permute-start.9 = (f32[48,128]{1,0:T(8,128)S(1)}, f32[48,128]{1,0:T(8,128)S(1)}, u32[]{:S(2)}, u32[]{:S(2)}) collective-permute-start(f32[48,128]{1,0:T(8,128)S(1)} %get-tuple-element.104), channel_id=1, source_target_pairs={{4,8},{8,4},{6,10},{10,6},{12,0},{0,12},{14,2},{2,14},{5,9},{9,5},... | collective-permute-start | bytes 73736 | tf_op jit(solution)/shard_map/ppermute | solution.py:858
  18.5 1.1 %collective-permute-start.8 = (f32[48,128]{1,0:T(8,128)S(1)}, f32[48,128]{1,0:T(8,128)S(1)}, u32[]{:S(2)}, u32[]{:S(2)}) collective-permute-start(f32[48,128]{1,0:T(8,128)S(1)} %get-tuple-element.104), channel_id=1, source_target_pairs={{0,4},{4,0},{2,6},{6,2},{8,12},{12,8},{10,14},{14,10},{1,5},{5,1},... | collective-permute-start | bytes 73736 | tf_op jit(solution)/shard_map/ppermute | solution.py:857
  19.6 2.2 %interior_1.1 = (f32[32,16,512]{2,1,0:T(8,128)S(1)}, f32[32,256]{1,0:T(8,128)S(1)}, f32[16,128]{1,0:T(8,128)S(1)}, f32[8,32]{1,0:T(8,128)S(1)}) custom-call(f32[32,16,512]{2,1,0:T(8,128)S(1)} %get-tuple-element.111.v_ref.before_ref.v0_ref, f32[32,16,512]{2,1,0:T(8,128)S(1)} %get-tuple-element.111.v_ref.before_ref.v0_ref, ...), custom_call_target="tpu_custom_call" | custom-call | flops 4000000000 | bytes 12000000 | tf_op jit(solution)/shard_map/interior_1/pallas_call | solution.py:813
  21.8 0.0 collective-permute-done.5.near_a_ref
  21.8 2.3 %collective-permute-done.6.near_b_ref = f32[176,128]{1,0:T(8,128)S(1)} collective-permute-done((f32[176,128]{1,0:T(8,128)S(1)}, f32[176,128]{1,0:T(8,128)S(1)}, u32[]{:S(2)}, u32[]{:S(2)}) %collective-permute-start.6) | collective-permute-done | bytes 90144 | tf_op jit(solution)/shard_map/ppermute | solution.py:852
  24.1 0.0 collective-permute-done.9.far_d_ref
  24.1 0.0 collective-permute-done.8.far_c_ref
  24.1 1.0 %finish_1.1 = (f32[16,512]{1,0:T(8,128)S(1)}, f32[16,512]{1,0:T(8,128)S(1)}, f32[16,512]{1,0:T(8,128)S(1)}, f32[16,512]{1,0:T(8,128)S(1)}, f32[160,128]{1,0:T(8,...) custom-call(f32[16,512]{1,0:T(8,128)S(1)} %get-tuple-element.99.vf_r, ...), custom_call_target="tpu_custom_call", output_to_operand_aliasing={{8}: (20, {})} | custom-call | tf_op jit(solution)/shard_map/finish_1/pallas_call | solution.py:813
  25.1 0.1 collective-permute-start.12
  25.2 1.1 %collective-permute-start.10 = (f32[160,128]{1,0:T(8,128)S(1)}, f32[160,128]{1,0:T(8,128)S(1)}, u32[]{:S(2)}, u32[]{:S(2)}) collective-permute-start(f32[160,128]{1,0:T(8,128)S(1)} %get-tuple-element.116), channel_id=1, source_target_pairs={{0,2},{2,0},{4,6},{6,4},{8,10},{10,8},{12,14},{14,12},{1,3},{3,1},... | collective-permute-start | bytes 245768 | tf_op jit(solution)/shard_map/ppermute | solution.py:851
  26.3 1.2 %collective-permute-start.11 = (f32[160,128]{1,0:T(8,128)S(1)}, f32[160,128]{1,0:T(8,128)S(1)}, u32[]{:S(2)}, u32[]{:S(2)}) collective-permute-start(f32[160,128]{1,0:T(8,128)S(1)} %get-tuple-element.117), channel_id=1, source_target_pairs={{2,4},{4,2},{6,8},{8,6},{10,12},{12,10},{14,0},{0,14},{3,5},{5,3},... | collective-permute-start | bytes 245768 | tf_op jit(solution)/shard_map/ppermute | solution.py:852
  27.5 0.0 collective-permute-done.12.core_ref.core_in_ref
  27.6 1.2 %collective-permute-start.14 = (f32[32,128]{1,0:T(8,128)S(1)}, f32[32,128]{1,0:T(8,128)S(1)}, u32[]{:S(2)}, u32[]{:S(2)}) collective-permute-start(f32[32,128]{1,0:T(8,128)S(1)} %get-tuple-element.120), channel_id=1, source_target_pairs={{4,8},{8,4},{6,10},{10,6},{12,0},{0,12},{14,2},{2,14},{5,9},{9,5},... | collective-permute-start | bytes 49160 | tf_op jit(solution)/shard_map/ppermute | solution.py:858
  28.7 0.0 collective-permute-start.13
  28.7 2.2 %interior_2.1 = (f32[32,16,512]{2,1,0:T(8,128)S(1)}, f32[32,256]{1,0:T(8,128)S(1)}, f32[16,128]{1,0:T(8,128)S(1)}, f32[8,32]{1,0:T(8,128)S(1)}) custom-call(f32[32,16,512]{2,1,0:T(8,128)S(1)} %get-tuple-element.125.v_ref.before_ref.v1_ref, f32[32,16,512]{2,1,0:T(8,128)S(1)} %get-tuple-element.111.v_ref.before_ref.v0_ref, ...), custom_call_target="tpu_custom_call" | custom-call | flops 4000000000 | bytes 12000000 | tf_op jit(solution)/shard_map/interior_2/pallas_call | solution.py:813
  31.0 0.0 collective-permute-done.10.near_a_ref
  31.0 2.9 %collective-permute-done.11.near_b_ref = f32[160,128]{1,0:T(8,128)S(1)} collective-permute-done((f32[160,128]{1,0:T(8,128)S(1)}, f32[160,128]{1,0:T(8,128)S(1)}, u32[]{:S(2)}, u32[]{:S(2)}) %collective-permute-start.11) | collective-permute-done | bytes 81952 | tf_op jit(solution)/shard_map/ppermute | solution.py:852
  33.9 0.0 collective-permute-done.14.far_d_ref
  33.9 0.0 collective-permute-done.13.far_c_ref
  34.0 0.8 %finish_2.1 = (f32[16,512]{1,0:T(8,128)S(1)}, f32[16,512]{1,0:T(8,128)S(1)}, f32[32,256]{1,0:T(8,128)S(1)}, f32[80,128]{1,0:T(8,128)S(1)}, f32[80,128]{1,0:T(8,1...) custom-call(f32[16,512]{1,0:T(8,128)S(1)} %get-tuple-element.115.vf_, ...), custom_call_target="tpu_custom_call", output_to_operand_aliasing={{7}: (20, {})} | custom-call | tf_op jit(solution)/shard_map/finish_2/pallas_call | solution.py:813
  34.7 0.1 collective-permute-start.17
  34.8 1.5 %collective-permute-start.15 = (f32[80,128]{1,0:T(8,128)S(1)}, f32[80,128]{1,0:T(8,128)S(1)}, u32[]{:S(2)}, u32[]{:S(2)}) collective-permute-start(f32[80,128]{1,0:T(8,128)S(1)} %get-tuple-element.130), channel_id=1, source_target_pairs={{0,2},{2,0},{4,6},{6,4},{8,10},{10,8},{12,14},{14,12},{1,3},{3,1},... | collective-permute-start | bytes 122888 | tf_op jit(solution)/shard_map/ppermute | solution.py:851
  36.3 1.3 %collective-permute-start.16 = (f32[80,128]{1,0:T(8,128)S(1)}, f32[80,128]{1,0:T(8,128)S(1)}, u32[]{:S(2)}, u32[]{:S(2)}) collective-permute-start(f32[80,128]{1,0:T(8,128)S(1)} %get-tuple-element.131), channel_id=1, source_target_pairs={{2,4},{4,2},{6,8},{8,6},{10,12},{12,10},{14,0},{0,14},{3,5},{5,3},... | collective-permute-start | bytes 122888 | tf_op jit(solution)/shard_map/ppermute | solution.py:852
  37.6 0.0 collective-permute-done.17.core_ref
  37.6 0.5 collective-permute-start.19
  38.1 0.3 collective-permute-start.18
  38.4 1.1 %energy.1.dots3_ref = f32[8,32]{1,0:T(8,128)S(1)} custom-call(f32[32,16,512]{2,1,0:T(8,128)S(1)} %get-tuple-element.136.v_ref.v2_ref, f32[32,16,512]{2,1,0:T(8,128)S(1)} %get-tuple-element.125.v_ref.before_ref.v1_ref, f32[16,512]{1,0:T(8,128)S(1)} %get-tuple-element.129.vf_ref.f2_ref, f32[16,512]{1,0:T(8,128)S(1)} %get-tuple-element.115.vf_ref.before_f_ref.f1_ref, ...), custom_call_target="tpu_custom_call" | custom-call | flops 4000000000 | bytes 12000000 | tf_op jit(solution)/shard_map/energy/pallas_call | solution.py:813
  39.5 0.0 collective-permute-done.15.near_a_ref
  39.5 3.4 %collective-permute-done.16.near_b_ref = f32[80,128]{1,0:T(8,128)S(1)} collective-permute-done((f32[80,128]{1,0:T(8,128)S(1)}, f32[80,128]{1,0:T(8,128)S(1)}, u32[]{:S(2)}, u32[]{:S(2)}) %collective-permute-start.16) | collective-permute-done | bytes 40992 | tf_op jit(solution)/shard_map/ppermute | solution.py:852
  43.0 0.1 collective-permute-done.19.far_d_ref
  43.0 0.0 collective-permute-done.18.far_c_ref
  43.0 0.3 moments.1
  43.4 11.1 %all_to_all.5.totals_ref = f32[16,2,128]{2,1,0:T(2,128)S(1)} all-to-all(f32[16,2,128]{2,1,0:T(2,128)S(1)} %moments.1), channel_id=1, replica_groups=mesh['grp'=2,'gx'=8,'gy'=2] {'gx','gy'}, dimensions={0} | all-to-all | bytes 32768 | tf_op jit(solution)/shard_map/all_to_all | solution.py:1071
  54.5 1.4 %iterate.1 = (f32[32,16,512]{2,1,0:T(8,128)}, f32[16,512]{1,0:T(8,128)}) custom-call(f32[16,2,128]{2,1,0:T(2,128)S(1)} %all_to_all.5.totals_ref, f32[32,16,512]{2,1,0:T(8,128)S(1)} %get-tuple-element.111.v_ref.before_ref.v0_ref, f32[32,16,512]{2,1,0:T(8,128)S(1)} %get-tuple-element.125.v_ref.before_ref.v1_ref, ...), custom_call_target="tpu_custom_call" | custom-call | tf_op jit(solution)/shard_map/iterate/pallas_call | solution.py:813
Async XLA Ops:
  1.7 6.7 %collective-permute-start = (f32[16,128]{1,0:T(8,128)S(1)}, f32[16,128]{1,0:T(8,128)S(1)}, u32[]{:S(2)}, u32[]{:S(2)}) collective-permute-start(f32[16,128]{1,0:T(8,128)S(1)} %get-tuple-element.75), channel_id=1, source_target_pairs={{0,1},{1,0},{2,3},{3,2},{4,5},{5,4},{6,7},{7,6},{8,9},{9,8},{10,11... | collective-permute-start | bytes 24584 | tf_op jit(solution)/shard_map/ppermute | solution.py:862
  2.2 9.7 %collective-permute-start.4 = (f32[16,128]{1,0:T(8,128)S(1)}, f32[16,128]{1,0:T(8,128)S(1)}, u32[]{:S(2)}, u32[]{:S(2)}) collective-permute-start(f32[16,128]{1,0:T(8,128)S(1)} %get-tuple-element.86), channel_id=1, source_target_pairs={{4,8},{8,4},{6,10},{10,6},{12,0},{0,12},{14,2},{2,14},{5,9},{9,5},... | collective-permute-start | bytes 24584 | tf_op jit(solution)/shard_map/ppermute | solution.py:900
  6.9 5.0 %collective-permute-start.1 = (f32[24,128]{1,0:T(8,128)S(1)}, f32[24,128]{1,0:T(8,128)S(1)}, u32[]{:S(2)}, u32[]{:S(2)}) collective-permute-start(f32[24,128]{1,0:T(8,128)S(1)} %get-tuple-element.84), channel_id=1, source_target_pairs={{0,2},{2,0},{4,6},{6,4},{8,10},{10,8},{12,14},{14,12},{1,3},{3,1},... | collective-permute-start | bytes 36872 | tf_op jit(solution)/shard_map/ppermute | solution.py:899
  8.3 3.7 %collective-permute-start.3 = (f32[16,128]{1,0:T(8,128)S(1)}, f32[16,128]{1,0:T(8,128)S(1)}, u32[]{:S(2)}, u32[]{:S(2)}) collective-permute-start(f32[16,128]{1,0:T(8,128)S(1)} %get-tuple-element.86), channel_id=1, source_target_pairs={{0,4},{4,0},{2,6},{6,2},{8,12},{12,8},{10,14},{14,10},{1,5},{5,1},... | collective-permute-start | bytes 24584 | tf_op jit(solution)/shard_map/ppermute | solution.py:904
  8.3 6.4 %collective-permute-start.2 = (f32[24,128]{1,0:T(8,128)S(1)}, f32[24,128]{1,0:T(8,128)S(1)}, u32[]{:S(2)}, u32[]{:S(2)}) collective-permute-start(f32[24,128]{1,0:T(8,128)S(1)} %get-tuple-element.85), channel_id=1, source_target_pairs={{2,4},{4,2},{6,8},{8,6},{10,12},{12,10},{14,0},{0,14},{3,5},{5,3},... | collective-permute-start | bytes 36872 | tf_op jit(solution)/shard_map/ppermute | solution.py:903
  15.8 1.3 %collective-permute-start.7 = (f32[176,128]{1,0:T(8,128)S(1)}, f32[176,128]{1,0:T(8,128)S(1)}, u32[]{:S(2)}, u32[]{:S(2)}) collective-permute-start(f32[176,128]{1,0:T(8,128)S(1)} %get-tuple-element.103), channel_id=1, source_target_pairs={{0,1},{1,0},{2,3},{3,2},{4,5},{5,4},{6,7},{7,6},{8,9},{9,8},{10,11... | collective-permute-start | bytes 270344 | tf_op jit(solution)/shard_map/ppermute | solution.py:862
  15.9 6.0 %collective-permute-start.5 = (f32[176,128]{1,0:T(8,128)S(1)}, f32[176,128]{1,0:T(8,128)S(1)}, u32[]{:S(2)}, u32[]{:S(2)}) collective-permute-start(f32[176,128]{1,0:T(8,128)S(1)} %get-tuple-element.100), channel_id=1, source_target_pairs={{0,2},{2,0},{4,6},{6,4},{8,10},{10,8},{12,14},{14,12},{1,3},{3,1},... | collective-permute-start | bytes 270344 | tf_op jit(solution)/shard_map/ppermute | solution.py:851
  15.9 8.2 %collective-permute-start.6 = (f32[176,128]{1,0:T(8,128)S(1)}, f32[176,128]{1,0:T(8,128)S(1)}, u32[]{:S(2)}, u32[]{:S(2)}) collective-permute-start(f32[176,128]{1,0:T(8,128)S(1)} %get-tuple-element.101), channel_id=1, source_target_pairs={{2,4},{4,2},{6,8},{8,6},{10,12},{12,10},{14,0},{0,14},{3,5},{5,3},... | collective-permute-start | bytes 270344 | tf_op jit(solution)/shard_map/ppermute | solution.py:852
  17.1 7.0 %collective-permute-start.9 = (f32[48,128]{1,0:T(8,128)S(1)}, f32[48,128]{1,0:T(8,128)S(1)}, u32[]{:S(2)}, u32[]{:S(2)}) collective-permute-start(f32[48,128]{1,0:T(8,128)S(1)} %get-tuple-element.104), channel_id=1, source_target_pairs={{4,8},{8,4},{6,10},{10,6},{12,0},{0,12},{14,2},{2,14},{5,9},{9,5},... | collective-permute-start | bytes 73736 | tf_op jit(solution)/shard_map/ppermute | solution.py:858
  18.5 5.6 %collective-permute-start.8 = (f32[48,128]{1,0:T(8,128)S(1)}, f32[48,128]{1,0:T(8,128)S(1)}, u32[]{:S(2)}, u32[]{:S(2)}) collective-permute-start(f32[48,128]{1,0:T(8,128)S(1)} %get-tuple-element.104), channel_id=1, source_target_pairs={{0,4},{4,0},{2,6},{6,2},{8,12},{12,8},{10,14},{14,10},{1,5},{5,1},... | collective-permute-start | bytes 73736 | tf_op jit(solution)/shard_map/ppermute | solution.py:857
  25.1 2.5 %collective-permute-start.12 = (f32[144,128]{1,0:T(8,128)S(1)}, f32[144,128]{1,0:T(8,128)S(1)}, u32[]{:S(2)}, u32[]{:S(2)}) collective-permute-start(f32[144,128]{1,0:T(8,128)S(1)} %get-tuple-element.119), channel_id=1, source_target_pairs={{0,1},{1,0},{2,3},{3,2},{4,5},{5,4},{6,7},{7,6},{8,9},{9,8},{10,11... | collective-permute-start | bytes 221192 | tf_op jit(solution)/shard_map/ppermute | solution.py:862
  25.2 5.8 %collective-permute-start.10 = (f32[160,128]{1,0:T(8,128)S(1)}, f32[160,128]{1,0:T(8,128)S(1)}, u32[]{:S(2)}, u32[]{:S(2)}) collective-permute-start(f32[160,128]{1,0:T(8,128)S(1)} %get-tuple-element.116), channel_id=1, source_target_pairs={{0,2},{2,0},{4,6},{6,4},{8,10},{10,8},{12,14},{14,12},{1,3},{3,1},... | collective-permute-start | bytes 245768 | tf_op jit(solution)/shard_map/ppermute | solution.py:851
  26.3 7.6 %collective-permute-start.11 = (f32[160,128]{1,0:T(8,128)S(1)}, f32[160,128]{1,0:T(8,128)S(1)}, u32[]{:S(2)}, u32[]{:S(2)}) collective-permute-start(f32[160,128]{1,0:T(8,128)S(1)} %get-tuple-element.117), channel_id=1, source_target_pairs={{2,4},{4,2},{6,8},{8,6},{10,12},{12,10},{14,0},{0,14},{3,5},{5,3},... | collective-permute-start | bytes 245768 | tf_op jit(solution)/shard_map/ppermute | solution.py:852
  27.6 6.4 %collective-permute-start.14 = (f32[32,128]{1,0:T(8,128)S(1)}, f32[32,128]{1,0:T(8,128)S(1)}, u32[]{:S(2)}, u32[]{:S(2)}) collective-permute-start(f32[32,128]{1,0:T(8,128)S(1)} %get-tuple-element.120), channel_id=1, source_target_pairs={{4,8},{8,4},{6,10},{10,6},{12,0},{0,12},{14,2},{2,14},{5,9},{9,5},... | collective-permute-start | bytes 49160 | tf_op jit(solution)/shard_map/ppermute | solution.py:858
  28.7 5.2 %collective-permute-start.13 = (f32[32,128]{1,0:T(8,128)S(1)}, f32[32,128]{1,0:T(8,128)S(1)}, u32[]{:S(2)}, u32[]{:S(2)}) collective-permute-start(f32[32,128]{1,0:T(8,128)S(1)} %get-tuple-element.120), channel_id=1, source_target_pairs={{0,4},{4,0},{2,6},{6,2},{8,12},{12,8},{10,14},{14,10},{1,5},{5,1},... | collective-permute-start | bytes 49160 | tf_op jit(solution)/shard_map/ppermute | solution.py:857
  34.7 2.9 %collective-permute-start.17 = (f32[80,128]{1,0:T(8,128)S(1)}, f32[80,128]{1,0:T(8,128)S(1)}, u32[]{:S(2)}, u32[]{:S(2)}) collective-permute-start(f32[80,128]{1,0:T(8,128)S(1)} %get-tuple-element.133), channel_id=1, source_target_pairs={{0,1},{1,0},{2,3},{3,2},{4,5},{5,4},{6,7},{7,6},{8,9},{9,8},{10,11... | collective-permute-start | bytes 122888 | tf_op jit(solution)/shard_map/ppermute | solution.py:862
  34.8 4.7 %collective-permute-start.15 = (f32[80,128]{1,0:T(8,128)S(1)}, f32[80,128]{1,0:T(8,128)S(1)}, u32[]{:S(2)}, u32[]{:S(2)}) collective-permute-start(f32[80,128]{1,0:T(8,128)S(1)} %get-tuple-element.130), channel_id=1, source_target_pairs={{0,2},{2,0},{4,6},{6,4},{8,10},{10,8},{12,14},{14,12},{1,3},{3,1},... | collective-permute-start | bytes 122888 | tf_op jit(solution)/shard_map/ppermute | solution.py:851
  36.3 6.7 %collective-permute-start.16 = (f32[80,128]{1,0:T(8,128)S(1)}, f32[80,128]{1,0:T(8,128)S(1)}, u32[]{:S(2)}, u32[]{:S(2)}) collective-permute-start(f32[80,128]{1,0:T(8,128)S(1)} %get-tuple-element.131), channel_id=1, source_target_pairs={{2,4},{4,2},{6,8},{8,6},{10,12},{12,10},{14,0},{0,14},{3,5},{5,3},... | collective-permute-start | bytes 122888 | tf_op jit(solution)/shard_map/ppermute | solution.py:852
  37.6 5.4 %collective-permute-start.19 = (f32[16,128]{1,0:T(8,128)S(1)}, f32[16,128]{1,0:T(8,128)S(1)}, u32[]{:S(2)}, u32[]{:S(2)}) collective-permute-start(f32[16,128]{1,0:T(8,128)S(1)} %get-tuple-element.134), channel_id=1, source_target_pairs={{4,8},{8,4},{6,10},{10,6},{12,0},{0,12},{14,2},{2,14},{5,9},{9,5},... | collective-permute-start | bytes 24584 | tf_op jit(solution)/shard_map/ppermute | solution.py:858
  38.1 5.0 %collective-permute-start.18 = (f32[16,128]{1,0:T(8,128)S(1)}, f32[16,128]{1,0:T(8,128)S(1)}, u32[]{:S(2)}, u32[]{:S(2)}) collective-permute-start(f32[16,128]{1,0:T(8,128)S(1)} %get-tuple-element.134), channel_id=1, source_target_pairs={{0,4},{4,0},{2,6},{6,2},{8,12},{12,8},{10,14},{14,10},{1,5},{5,1},... | collective-permute-start | bytes 24584 | tf_op jit(solution)/shard_map/ppermute | solution.py:857
